TPU v7x, 256 devices: a whole 4x4x8 slice. The times are simulated.
256 devices in a mesh: row: 16 (over y, x_lo, core), col: 16 (over x_hi, z).
Axes of the slice: x: 4 (x_hi: 2, x_lo: 2; x = x_hi * 2 + x_lo), y: 4, z: 8, core: 2. Of those that a mesh axis runs over, the one named last changes fastest.
Arguments:
- tokens: bfloat16 [4096, 6144], P('row', 'col'), may hold values from -6 to 6
- gate_weight_blocks: bfloat16 [2816, 128, 128], P(('row', 'col')), may hold values from -0.125 to 0.125
- up_weight_blocks: bfloat16 [2816, 128, 128], P(('row', 'col')), may hold values from -0.125 to 0.125
- block_row: int32 [2816], P(('row', 'col')), may hold values from -1 to 47, as said below
- block_col: int32 [2816], P(('row', 'col')), may hold values from -1 to 191, as said below
- grad_hidden: bfloat16 [4096, 24576], P('row', 'col'), may hold values from -6 to 6
Outputs:
- hidden: bfloat16 [4096, 24576], P('row', 'col')
- grad_tokens: bfloat16 [4096, 6144], P('row', 'col')
Inputs may be any that keep to these rules, and one draw needn't show every extreme that they name: Slot s of the device at index r of row and c of col lies at position (r * 16 + c) * 11 + s. Such a slot is empty (block_row and block_col both -1) or names a block with block_row in [r * 3, (r + 1) * 3) and block_col in [c * 12, (c + 1) * 12); the live slots of a device come first, at least one, and name distinct blocks; in every draw some device has all 11 slots live. `block_col`: empty exactly where block_row is empty, as described there.
All inputs are finite; a program needn't handle non-finite values.
Results may differ from a plain program's by a relative error of at most 0.0049.
Values may be sent and summed in bfloat16 or wider, within the bound.
No kernel may reach another device: no remote copies, remote signals or barrier semaphores. Data moves between devices by JAX's collectives and lax.ppermute only.
A program may use at most 64 MiB of HBM per device.

v0:
```python
import jax
import jax.numpy as jnp
from jax import lax
from jax.sharding import PartitionSpec as P


def split_groups(pieces, slot_group):
    gate_set, up_set, row_ids, col_ids = pieces
    group_total = gate_set.shape[0] // slot_group
    return (
        gate_set.reshape((group_total, slot_group) + gate_set.shape[1:]),
        up_set.reshape((group_total, slot_group) + up_set.shape[1:]),
        row_ids.reshape(group_total, slot_group),
        col_ids.reshape(group_total, slot_group),
    )


def place_terms(terms, selector):
    return jnp.sum(terms[:, :, None, :] * selector[None, :, :, None], axis=1)


def panel_forward(running, pieces, token_blocks, col_base, slot_group):
    col_count = running[0].shape[1]

    def slot_step(totals, group_item):
        gate_group, up_group, row_group, col_group = group_item
        taken_rows = jnp.take(token_blocks, jnp.maximum(row_group, 0), axis=1)
        selector = (col_group[:, None] - col_base == jnp.arange(col_count)[None, :]).astype(
            jnp.float32
        )
        gate_partial_terms = jnp.einsum(
            "tmk,mkc->tmc", taken_rows, gate_group, preferred_element_type=jnp.float32
        )
        up_terms = jnp.einsum(
            "tmk,mkc->tmc", taken_rows, up_group, preferred_element_type=jnp.float32
        )
        gate_sum = totals[0] + place_terms(gate_partial_terms, selector)
        up_sum = totals[1] + place_terms(up_terms, selector)
        return ((gate_sum, up_sum), None)

    result, _ = lax.scan(slot_step, running, split_groups(pieces, slot_group))
    return result


def panel_backward(running, pieces, grad_blocks, col_base, slot_group, tile_rows):
    col_count = grad_blocks[0].shape[1]

    def slot_step(totals, group_item):
        gate_group, up_group, row_group, col_group = group_item
        local_cols = jnp.clip(col_group - col_base, 0, col_count - 1)
        gate_taken = jnp.take(grad_blocks[0], local_cols, axis=1)
        up_selected = jnp.take(grad_blocks[1], local_cols, axis=1)
        terms = jnp.einsum(
            "tmc,mkc->tmk", gate_taken, gate_group, preferred_element_type=jnp.float32
        )
        terms = terms + jnp.einsum(
            "tmc,mkc->tmk", up_selected, up_group, preferred_element_type=jnp.float32
        )
        window_start = jnp.max(row_group) // tile_rows * tile_rows
        selector = (row_group[:, None] - window_start == jnp.arange(tile_rows)[None, :]).astype(
            jnp.float32
        )
        window = lax.dynamic_slice_in_dim(totals, window_start, tile_rows, 1)
        window = window + place_terms(terms, selector)
        return (lax.dynamic_update_slice_in_dim(totals, window, window_start, 1), None)

    result, _ = lax.scan(slot_step, running, split_groups(pieces, slot_group))
    return result


def on_device(tokens, gate_weight_blocks, up_weight_blocks, block_row, block_col, grad_hidden):
    token_full = lax.all_gather(tokens, "col", axis=1, tiled=True)
    token_count = token_full.shape[0]
    full_width = token_full.shape[1]
    block_size = gate_weight_blocks.shape[1]
    slot_group = gate_weight_blocks.shape[0]
    panel_width = grad_hidden.shape[1]
    col_count = panel_width // block_size
    row_count = full_width // block_size
    tile_rows = row_count // lax.axis_size("row")
    col_base = lax.axis_index("col") * col_count
    token_blocks = token_full.reshape(token_count, row_count, block_size)
    zero_cols = jnp.zeros((token_count, col_count, block_size), jnp.float32)
    gate_act, up_act = panel_forward(
        (zero_cols, zero_cols),
        (
            lax.all_gather(gate_weight_blocks, "row", axis=0, tiled=True),
            lax.all_gather(up_weight_blocks, "row", axis=0, tiled=True),
            lax.all_gather(block_row, "row", axis=0, tiled=True),
            lax.all_gather(block_col, "row", axis=0, tiled=True),
        ),
        token_blocks,
        col_base,
        slot_group,
    )
    gate_act = gate_act.reshape(token_count, panel_width)
    up_act = up_act.reshape(token_count, panel_width)
    sigmoid_gate = jax.nn.sigmoid(gate_act)
    silu_gate = gate_act * sigmoid_gate
    hidden = (silu_gate * up_act).astype(jnp.bfloat16)
    upstream = grad_hidden.astype(jnp.float32)
    grad_gate = (upstream * up_act * sigmoid_gate * (1.0 + gate_act * (1.0 - sigmoid_gate))).astype(
        jnp.bfloat16
    )
    grad_up = (upstream * silu_gate).astype(jnp.bfloat16)
    grad_blocks = (
        grad_gate.reshape(token_count, col_count, block_size),
        grad_up.reshape(token_count, col_count, block_size),
    )
    zero_rows = jnp.zeros((token_count, row_count, block_size), jnp.float32)
    summed_terms = panel_backward(
        zero_rows,
        (
            lax.all_gather(gate_weight_blocks, "row", axis=0, tiled=True),
            lax.all_gather(up_weight_blocks, "row", axis=0, tiled=True),
            lax.all_gather(block_row, "row", axis=0, tiled=True),
            lax.all_gather(block_col, "row", axis=0, tiled=True),
        ),
        grad_blocks,
        col_base,
        slot_group,
        tile_rows,
    )
    grad_tokens = lax.psum_scatter(
        summed_terms.reshape(token_count, full_width), "col", scatter_dimension=1, tiled=True
    ).astype(jnp.bfloat16)
    return (hidden, grad_tokens)


def solution(mesh):
    return jax.shard_map(
        on_device,
        mesh=mesh,
        in_specs=(
            P("row", "col"),
            P(("row", "col"), None, None),
            P(("row", "col"), None, None),
            P(("row", "col")),
            P(("row", "col")),
            P("row", "col"),
        ),
        out_specs=(P("row", "col"), P("row", "col")),
        check_vma=False,
    )
```

profile of v0, /device:TPU:32, one launch (start us, length us, event | category | flops | bytes accessed | tf_op | source)
XLA Modules:
  0.0 891.2 jit_solution(17711240488314291715)
XLA Ops:
  14.2 12.6 %all-reduce.2 = (s32[176]{0:T(256)S(1)}, s32[176]{0:T(256)S(1)}) all-reduce(s32[176]{0:T(256)S(1)} %dynamic-update-slice, s32[176]{0:T(256)S(1)} %dynamic-update-slice.1), channel_id=1, replica_groups=mesh['row'=16,'col'=16] {'row'}, use_global_device_ids=true, to_apply=%add | all-reduce | flops 352 | bytes 2816
  28.2 78.6 %all-gather.6.cloned.1.call-done = bf16[256,6144]{0,1:T(8,128)(2,1)} async-done(((bf16[256,384]{0,1:T(8,128)(2,1)}), bf16[256,6144]{0,1:T(8,128)(2,1)}) %all-gather.6.cloned.1.call-update) | async-done | bytes 3145744 | tf_op jit(solution)/shard_map/all_gather | solution.py:72
  106.7 4.7 copy.65
  111.4 37.4 %all-gather.4.cloned.1.call-done = bf16[176,128,128]{2,1,0:T(8,128)(2,1)} async-done(((bf16[11,128,128]{2,1,0:T(8,128)(2,1)}), bf16[176,128,128]{2,1,0:T(8,128)(2,1)}) %all-gather.4.cloned.1.call-update) | async-done | bytes 5767184 | tf_op jit(solution)/shard_map/all_gather | solution.py:87
  148.8 45.3 %all-gather.8.cloned.1.call-done = bf16[176,128,128]{2,1,0:T(8,128)(2,1)} async-done(((bf16[11,128,128]{2,1,0:T(8,128)(2,1)}), bf16[176,128,128]{2,1,0:T(8,128)(2,1)}) %all-gather.8.cloned.1.call-update) | async-done | bytes 5767184 | tf_op jit(solution)/shard_map/all_gather | solution.py:88
  194.1 280.4 %while.26 = (s32[]{:T(128)}, f32[256,12,128]{2,0,1:T(8,128)}, f32[256,12,128]{2,0,1:T(8,128)}, bf16[16,11,128,128]{3,2,1,0:T(8,128)(2,1)}, s32[16,11]{1,0:T(8,12...) while((s32[]{:T(128)}, f32[256,12,128]{2,0,1:T(8,128)}, ...), condition=%wide.region_3.4_spmd.clone, body=%wide.region_0.3_spmd.clone.sunk | while | flops 203359536 | bytes 27727412 | solution.py:41
  194.2 2.6 gather_fusion.2
  202.8 4.8 multiply_reduce_fusion.6
  207.6 2.3 select_add_fusion.3
  210.0 2.6 gather_fusion.2
  218.6 4.8 multiply_reduce_fusion.6
  223.4 4.1 select_add_fusion.3
  227.7 2.6 gather_fusion.2
  236.2 4.8 multiply_reduce_fusion.6
  241.0 4.1 select_add_fusion.3
  245.3 2.6 gather_fusion.2
  253.9 4.8 multiply_reduce_fusion.6
  258.7 4.1 select_add_fusion.3
  262.9 2.6 gather_fusion.2
  271.5 4.8 multiply_reduce_fusion.6
  276.3 4.1 select_add_fusion.3
  280.6 2.6 gather_fusion.2
  289.2 4.8 multiply_reduce_fusion.6
  294.0 4.1 select_add_fusion.3
  298.2 2.6 gather_fusion.2
  306.8 4.8 multiply_reduce_fusion.6
  311.6 4.1 select_add_fusion.3
  315.9 2.6 gather_fusion.2
  324.4 4.8 multiply_reduce_fusion.6
  329.2 4.1 select_add_fusion.3
  333.5 2.6 gather_fusion.2
  342.1 4.8 multiply_reduce_fusion.6
  346.9 4.1 select_add_fusion.3
  351.2 2.6 gather_fusion.2
  359.7 4.8 multiply_reduce_fusion.6
  364.5 4.1 select_add_fusion.3
  368.8 2.6 gather_fusion.2
  377.4 4.8 multiply_reduce_fusion.6
  382.2 4.1 select_add_fusion.3
  386.5 2.6 gather_fusion.2
  395.0 4.8 multiply_reduce_fusion.6
  399.8 4.1 select_add_fusion.3
  404.1 2.6 gather_fusion.2
  412.7 4.8 multiply_reduce_fusion.6
  417.5 4.1 select_add_fusion.3
  421.8 2.6 gather_fusion.2
  430.3 4.8 multiply_reduce_fusion.6
  435.1 4.1 select_add_fusion.3
  439.4 2.6 gather_fusion.2
  448.0 4.8 multiply_reduce_fusion.6
  452.8 4.1 select_add_fusion.3
  457.0 2.6 gather_fusion.2
  465.6 4.8 multiply_reduce_fusion.6
  470.4 4.1 select_add_fusion.3
  474.5 1.9 copy.68
  476.4 1.9 copy.67
  478.3 3.4 fusion.39
  481.7 2.4 copy.70
  484.5 3.4 broadcast_in_dim.36
  487.9 173.3 %while.25 = (s32[]{:T(128)}, f32[256,48,128]{2,0,1:T(8,128)}, s32[16,11]{1,0:T(8,128)S(1)}, bf16[16,11,128,128]{3,2,1,0:T(8,128)(2,1)}, s32[16,11]{1,0:T(8,128)S...) while((s32[]{:T(128)}, f32[256,48,128]{2,0,1:T(8,128)}, ...), condition=%wide.region_7.9_spmd, body=%wide.region_4.8_spmd.sunk | while | flops 187794624 | bytes 21566488 | solution.py:67
  551.1 1.8 add_dynamic-update-slice_fusion.2
  626.9 1.8 add_dynamic-update-slice_fusion.2
  661.3 6.2 copy_bitcast_fusion
  669.7 213.2 %reduce-scatter.2.cloned.1.call-done = f32[256,384]{1,0:T(8,128)} async-done(((f32[256,6144]{1,0:T(8,128)}), f32[256,384]{1,0:T(8,128)}) %reduce-scatter.2.cloned.1.call-update) | async-done | bytes 393232 | tf_op jit(solution)/shard_map/reduce_scatter | solution.py:124
  (426 shorter events, 246.3 us)
Async XLA Ops:
  7.2 19.8 %copy-start.4 = (bf16[256,1536]{1,0:T(8,128)(2,1)S(1)}, bf16[256,1536]{1,0:T(8,128)(2,1)}, u32[]{:S(2)}) copy-start(bf16[256,1536]{1,0:T(8,128)(2,1)} %param.17) | copy-start | bytes 2359300
  7.2 99.5 %all-gather.6.cloned.1.call-start = ((), (), s32[]{:S(2)}) async-start(), calls=%async_computation.2 | async-start | bytes 3342336 | tf_op jit(solution)/shard_map/all_gather | solution.py:72
  9.0 139.7 %all-gather.4.cloned.1.call-start = ((), (), s32[]{:S(2)}) async-start(), calls=%async_computation.1 | async-start | bytes 6127616 | tf_op jit(solution)/shard_map/all_gather | solution.py:87
  9.8 184.3 %all-gather.8.cloned.1.call-start = ((), (), s32[]{:S(2)}) async-start(), calls=%async_computation.3 | async-start | bytes 6127616 | tf_op jit(solution)/shard_map/all_gather | solution.py:88
  10.5 872.4 %reduce-scatter.2.cloned.1.call-start = ((), (), s32[]{:S(2)}) async-start(), calls=%async_computation.4 | async-start | bytes 6684672 | tf_op jit(solution)/shard_map/reduce_scatter | solution.py:124
  481.7 2.4 copy-start.3
  487.9 2.9 copy-start
  496.6 2.2 copy-start.1
  498.8 2.9 copy-start
  507.4 2.2 copy-start.1
  509.6 2.9 copy-start
  518.2 2.2 copy-start.1
  520.4 2.9 copy-start
  529.1 2.2 copy-start.1
  531.2 2.9 copy-start
  539.9 2.2 copy-start.1
  542.1 2.9 copy-start
  550.7 2.2 copy-start.1
  552.9 2.9 copy-start
  561.6 2.2 copy-start.1
  563.8 2.9 copy-start
  572.4 2.2 copy-start.1
  574.6 2.9 copy-start
  583.3 2.2 copy-start.1
  585.4 2.9 copy-start
  594.1 2.2 copy-start.1
  596.3 2.9 copy-start
  604.9 2.2 copy-start.1
  607.1 2.9 copy-start
  615.7 2.2 copy-start.1
  617.9 2.9 copy-start
  626.6 2.2 copy-start.1
  628.8 2.9 copy-start
  637.4 2.2 copy-start.1
  639.6 2.9 copy-start
  648.2 2.2 copy-start.1
  650.4 2.9 copy-start
  659.1 2.2 copy-start.1
  667.5 1.1 copy-start.2
Sparse Core Ops, SparseCore 0:
  11.2 95.5 all-gather.5
  108.6 40.1 all-gather.3
  150.6 43.4 all-gather.7
  667.6 215.3 reduce-scatter.1
where the time goes:
time: 898 us; the launch traced here: 891 us
  waiting for transfers between devices  376 us (42%)
  other arithmetic  196 us (22%)
  local copies, waits for them, and re-layouts  167 us (19%)
  matrix products  90.8 us (10%)
  loops' own time  33.5 us (4%)
  between operations  14.5 us (2%)
  blocking collectives  12.6 us (1%)
    reduce_scatter x1, waiting for transfers between devices, on_device(): lax.psum_scatter(summed_terms.reshape(token_count, full_width), 'col', sc...  213 us
    reduce_sum x32, other arithmetic, place_terms(): return jnp.sum(terms[:, :, None, :] * selector[None, :, :, None], axis=1)  82.4 us
    all_gather x1, waiting for transfers between devices, on_device(): token_full = lax.all_gather(tokens, 'col', axis=1, tiled=True)  78.6 us
    add x16, other arithmetic, slot_step(): up_sum = totals[1] + place_terms(up_terms, selector)  64.4 us
    all_gather x1, waiting for transfers between devices, on_device(): lax.all_gather(up_weight_blocks, 'row', axis=0, tiled=True)  45.3 us
    gather x16, local copies, waits for them, and re-layouts, slot_step(): taken_rows = jnp.take(token_blocks, jnp.maximum(row_group, 0), axis=1)  41.2 us
    all_gather x1, waiting for transfers between devices, on_device(): lax.all_gather(gate_weight_blocks, 'row', axis=0, tiled=True)  37.4 us
    another operation x1, loops' own time, panel_backward(): result, _ = lax.scan(slot_step, running, split_groups(pieces, slot_group))  32.7 us
  transfers between devices with their start and end apart: 4, of which 4 were waited for; matrix products, arithmetic and copies ran while one was open for 1% of the time, Pallas kernels for 0%

commit v1 on v0

v1 whole, which is shorter than its diff:
```python
import jax
import jax.numpy as jnp
from jax import lax
from jax.experimental import pallas as pl
from jax.experimental.pallas import tpu as pltpu
from jax.sharding import Mesh, PartitionSpec as P

AXES = ("y", "x_lo", "core", "x_hi", "z")
ROW = ("y", "x_lo", "core")
COL = ("x_hi", "z")
SIZES = {"y": 4, "x_lo": 2, "core": 2, "x_hi": 2, "z": 8}
VMEM_LIMIT = 56 * 1024 * 1024


def shift(value, axis, step):
    size = SIZES[axis]
    return lax.ppermute(value, axis, [(i, (i + step) % size) for i in range(size)])


def forward_kernel(order, rows, cols, x_ref, w_ref, up_ref, hidden_ref, grads_ref, acc):
    step = pl.program_id(0)
    slots = w_ref.shape[1]
    side = w_ref.shape[2]
    col_count = grads_ref.shape[0]
    base = order[step] * slots

    @pl.when(step == 0)
    def _():
        acc[...] = jnp.zeros_like(acc)

    for slot in range(slots):
        row = rows[base + slot]
        col = cols[base + slot]
        taken = x_ref[0, :, pl.ds(pl.multiple_of(jnp.minimum(row, 2) * side, side), side)]
        acc[col] += jnp.dot(taken, w_ref[0, slot], preferred_element_type=jnp.float32)

    @pl.when(step == pl.num_programs(0) - 1)
    def _():
        for j in range(col_count):
            gate = acc[j, :, :side]
            up = acc[j, :, side:]
            sig = 1.0 / (1.0 + jnp.exp(-gate))
            silu = gate * sig
            hidden_ref[:, j * side:(j + 1) * side] = (silu * up).astype(jnp.bfloat16)
            upstream = up_ref[:, j * side:(j + 1) * side].astype(jnp.float32)
            grads_ref[j, :, :side] = (
                upstream * up * sig * (1.0 + gate * (1.0 - sig))
            ).astype(jnp.bfloat16)
            grads_ref[j, :, side:] = (upstream * silu).astype(jnp.bfloat16)


def forward(order, rows, cols, x, w, upstream):
    tiles, tokens, span = x.shape
    slots, side, pair = w.shape[1:]
    width = upstream.shape[1]
    col_count = width // side
    grid_spec = pltpu.PrefetchScalarGridSpec(
        num_scalar_prefetch=3,
        grid=(tiles,),
        in_specs=[
            pl.BlockSpec((1, tokens, span), lambda i, order, rows, cols: (i, 0, 0)),
            pl.BlockSpec((1, slots, side, pair), lambda i, order, rows, cols: (order[i], 0, 0, 0)),
            pl.BlockSpec((tokens, width), lambda i, order, rows, cols: (0, 0)),
        ],
        out_specs=[
            pl.BlockSpec((tokens, width), lambda i, order, rows, cols: (0, 0)),
            pl.BlockSpec((col_count, tokens, pair), lambda i, order, rows, cols: (0, 0, 0)),
        ],
        scratch_shapes=[pltpu.VMEM((col_count + 1, tokens, pair), jnp.float32)],
    )
    return pl.pallas_call(
        forward_kernel,
        grid_spec=grid_spec,
        out_shape=[
            jax.ShapeDtypeStruct((tokens, width), jnp.bfloat16),
            jax.ShapeDtypeStruct((col_count, tokens, pair), jnp.bfloat16),
        ],
        compiler_params=pltpu.CompilerParams(vmem_limit_bytes=VMEM_LIMIT),
        cost_estimate=pl.CostEstimate(
            flops=2 * tiles * slots * tokens * side * pair,
            bytes_accessed=2 * (x.size + w.size + 5 * upstream.size),
            transcendentals=2 * upstream.size,
        ),
        name="forward",
    )(order, rows, cols, x, w, upstream)


def backward_kernel(order, rows, cols, grads_ref, w_ref, out_ref, acc):
    step = pl.program_id(0)
    slots = w_ref.shape[1]
    side = w_ref.shape[2]
    col_count = grads_ref.shape[0]
    base = order[step] * slots
    acc[...] = jnp.zeros_like(acc)
    for slot in range(slots):
        row = rows[base + slot]
        col = jnp.minimum(cols[base + slot], col_count - 1)
        acc[row] += lax.dot_general(
            grads_ref[col],
            w_ref[0, slot],
            (((1,), (1,)), ((), ())),
            preferred_element_type=jnp.float32,
        )
    for j in range(out_ref.shape[2] // side):
        out_ref[0, :, j * side:(j + 1) * side] = acc[j].astype(out_ref.dtype)


def backward(order, rows, cols, grads, w, dtype):
    steps = order.shape[0]
    col_count, tokens, pair = grads.shape
    slots, side = w.shape[1:3]
    tile_rows = 3
    span = tile_rows * side
    grid_spec = pltpu.PrefetchScalarGridSpec(
        num_scalar_prefetch=3,
        grid=(steps,),
        in_specs=[
            pl.BlockSpec((col_count, tokens, pair), lambda i, order, rows, cols: (0, 0, 0)),
            pl.BlockSpec((1, slots, side, pair), lambda i, order, rows, cols: (order[i], 0, 0, 0)),
        ],
        out_specs=pl.BlockSpec((1, tokens, span), lambda i, order, rows, cols: (i, 0, 0)),
        scratch_shapes=[pltpu.VMEM((tile_rows + 1, tokens, side), jnp.float32)],
    )
    return pl.pallas_call(
        backward_kernel,
        grid_spec=grid_spec,
        out_shape=jax.ShapeDtypeStruct((steps, tokens, span), dtype),
        compiler_params=pltpu.CompilerParams(vmem_limit_bytes=VMEM_LIMIT),
        cost_estimate=pl.CostEstimate(
            flops=2 * steps * slots * tokens * side * pair,
            bytes_accessed=2 * (grads.size + steps * slots * side * pair + 2 * steps * tokens * span),
            transcendentals=0,
        ),
        name="backward",
    )(order, rows, cols, grads, w)


def gather_tokens(tokens, home):
    x_hi, z = home
    across = shift(tokens, "x_hi", 1)
    chunks = []
    for value, hi, far in ((tokens, x_hi, 1), (across, 1 - x_hi, -1)):
        chunks.append((value, hi * 8 + z))
        for step in (1, -1):
            moving = value
            for hop in range(1, 4 + (step == far)):
                moving = shift(moving, "z", step)
                chunks.append((moving, hi * 8 + (z - step * hop) % 8))
    return chunks


def on_device(tokens, gate_blocks, up_blocks, block_row, block_col, upstream):
    x_hi, z = lax.axis_index("x_hi"), lax.axis_index("z")
    bf16, f32 = jnp.bfloat16, jnp.float32
    slots, side = gate_blocks.shape[:2]
    pairs = jnp.concatenate([gate_blocks, up_blocks], axis=2)
    w = lax.all_gather(pairs, ROW, axis=0, tiled=True).reshape(-1, slots, side, 2 * side)
    chunks = gather_tokens(tokens, (x_hi, z))
    x = jnp.stack([value for value, _ in chunks])
    order = jnp.stack([index for _, index in chunks]).astype(jnp.int32)

    ids = jnp.concatenate([
        jnp.where(block_row < 0, 3, block_row % 3),
        jnp.where(block_row < 0, 12, block_col % 12),
    ])
    ids = lax.all_gather(ids, ROW, axis=0, tiled=True).reshape(-1, 2, slots)
    rows, cols = ids[:, 0].reshape(-1), ids[:, 1].reshape(-1)

    hidden, grads = forward(order, rows, cols, x, w, upstream)

    def terms(offsets):
        group = [hi * 8 + (z + dz) % 8 for dz in offsets for hi in (0, 1)]
        return backward(jnp.stack(group).astype(jnp.int32), rows, cols, grads, w, f32)

    part = terms((4,)).astype(bf16)
    plus, minus = shift(part[0], "z", 1), shift(part[1], "z", -1)
    part = terms((3, -3))
    plus = jnp.stack([part[0] + plus, part[1]]).astype(bf16)
    minus = jnp.stack([part[2], part[3] + minus]).astype(bf16)
    for distance in (2, 1):
        plus, minus = shift(plus, "z", 1), shift(minus, "z", -1)
        part = terms((distance, -distance))
        plus = (part[:2] + plus).astype(bf16)
        minus = (part[2:] + minus).astype(bf16)
    plus, minus = shift(plus, "z", 1), shift(minus, "z", -1)
    total = terms((0,)) + plus + minus
    mine = jnp.where(x_hi == 0, total[0], total[1])
    other = jnp.where(x_hi == 0, total[1], total[0]).astype(bf16)
    grad_tokens = (mine + shift(other, "x_hi", 1)).astype(bf16)
    return hidden, grad_tokens


def solution(mesh):
    fine = Mesh(mesh.devices.reshape([SIZES[a] for a in AXES]), AXES)
    both = P(ROW, COL)
    return jax.shard_map(
        on_device,
        mesh=fine,
        in_specs=(both, P(ROW + COL, None, None), P(ROW + COL, None, None), P(ROW + COL), P(ROW + COL), both),
        out_specs=(both, both),
        check_vma=False,
    )
```

time: 898 us -> 174 us (0.19)
  waiting for transfers between devices: 376 us -> 42.4 us
  other arithmetic: 196 us -> 14 us
  local copies, waits for them, and re-layouts: 167 us -> 6.08 us
  matrix products: 90.8 us -> 0 us
  Pallas kernels: 0 us -> 46.3 us
  starting transfers between devices: 0.16 us -> 37.8 us
  loops' own time: 33.5 us -> 0 us
    reduce_scatter x1 -> x0, waiting for transfers between devices: 213 us -> none  [on_device(): lax.psum_scatter(summed_terms.reshape(token_count, full_width), 'col', sc...]
    all_gather x3 -> x1, waiting for transfers between devices: 161 us -> 9.6 us  [on_device(): lax.all_gather(pairs, ROW, axis=0, tiled=True)]
    dot_general x64 -> x0, matrix products: 90.8 us -> none  [the longest x16 22.8 us: slot_step(): jnp.einsum('tmk,mkc->tmc', taken_rows, gate_group, preferred_element_type...]
    reduce_sum x32 -> x0, other arithmetic: 82.4 us -> none  [place_terms(): return jnp.sum(terms[:, :, None, :] * selector[None, :, :, None], axis=1)]
    gather x48 -> x0, local copies, waits for them, and re-layouts: 81.2 us -> none  [the longest x16 41.2 us: slot_step(): taken_rows = jnp.take(token_blocks, jnp.maximum(row_group, 0), axis=1)]
    add x16 -> x1, other arithmetic: 64.4 us -> 1.24 us  [on_device(): total = terms((0,)) + plus + minus]
    transpose x32 -> x0, local copies, waits for them, and re-layouts: 50 us -> none  [the longest x16 25.4 us: slot_step(): jnp.einsum('tmk,mkc->tmc', taken_rows, gate_group, preferred_element_type...]
    pallas_call x0 -> x6, Pallas kernels: none -> 46.3 us  [the longest x5 27.5 us: backward(): pl.pallas_call(backward_kernel, grid_spec=grid_spec, out_shape=jax.ShapeD...]
  transfers between devices with their start and end apart: 4 -> 25, of which waited for: 4 -> 14; matrix products, arithmetic and copies ran while one was open for 1% -> 7% of each run, Pallas kernels for 0% -> 13%
where the time goes in v1:
time: 174 us; the launch traced here: 173 us
  Pallas kernels  46.3 us (27%)
  waiting for transfers between devices  42.4 us (24%)
  starting transfers between devices  37.8 us (22%)
  between operations  14.9 us (9%)
  other arithmetic  14 us (8%)
  blocking collectives  11.9 us (7%)
  local copies, waits for them, and re-layouts  6.08 us (3%)
    ppermute x24, starting transfers between devices, shift(): lax.ppermute(value, axis, [(i, (i + step) % size) for i in range(size)])  37.7 us
    ppermute x24, waiting for transfers between devices, shift(): lax.ppermute(value, axis, [(i, (i + step) % size) for i in range(size)])  32.7 us
    pallas_call x5, Pallas kernels, backward(): pl.pallas_call(backward_kernel, grid_spec=grid_spec, out_shape=jax.ShapeD...  27.5 us
    pallas_call x1, Pallas kernels, forward(): pl.pallas_call(forward_kernel, grid_spec=grid_spec, out_shape=[jax.ShapeD...  18.9 us
    unnamed x1, blocking collectives  11.9 us
    all_gather x1, waiting for transfers between devices, on_device(): lax.all_gather(pairs, ROW, axis=0, tiled=True)  9.6 us
    unnamed x21, local copies, waits for them, and re-layouts  3.83 us
  transfers between devices with their start and end apart: 25, of which 14 were waited for; matrix products, arithmetic and copies ran while one was open for 7% of the time, Pallas kernels for 13%

profile of v1, /device:TPU:32, one launch (start us, length us, event | category | flops | bytes accessed | tf_op | source)
XLA Modules:
  0.0 173.4 jit_solution(131752430765656571)
XLA Ops:
  7.2 2.0 %pad_maximum_fusion = bf16[11,128,256]{2,1,0:T(8,128)(2,1)} fusion(bf16[11,128,128]{2,1,0:T(8,128)(2,1)} %param.8, bf16[11,128,128]{2,1,0:T(8,128)(2,1)} %param.7), kind=kLoop, calls=%fused_computation.9 | loop fusion | flops 1441792 | bytes 1441792 | tf_op jit(solution)/shard_map/concatenate | solution.py:156
  9.3 2.0 %collective-permute-start = (bf16[256,384]{1,0:T(8,128)(2,1)}, bf16[256,384]{1,0:T(8,128)(2,1)}, u32[]{:S(2)}, u32[]{:S(2)}) collective-permute-start(bf16[256,384]{1,0:T(8,128)(2,1)} %param.6), channel_id=1, source_target_pairs={{0,1},{1,2},{2,3},{3,4},{4,5},{5,6},{6,7},{7,0},{8,9},{9,10},{10,1... | collective-permute-start | bytes 589832 | tf_op jit(solution)/shard_map/ppermute | solution.py:17
  11.3 0.1 collective-permute-start.4
  11.4 3.0 %collective-permute-start.7 = (bf16[256,384]{1,0:T(8,128)(2,1)}, bf16[256,384]{1,0:T(8,128)(2,1)S(1)}, u32[]{:S(2)}, u32[]{:S(2)}) collective-permute-start(bf16[256,384]{1,0:T(8,128)(2,1)} %param.6), channel_id=1, source_target_pairs={{0,8},{8,0},{1,9},{9,1},{2,10},{10,2},{3,11},{11,3},{4,12},{12,4},... | collective-permute-start | bytes 589832 | tf_op jit(solution)/shard_map/ppermute | solution.py:17
  14.4 1.3 dynamic-slice
  16.3 0.7 compare_select_fusion.1
  17.0 0.2 add_dynamic-update-slice_fusion
  17.2 11.9 %all-reduce = s32[352]{0:T(512)S(1)} all-reduce(s32[352]{0:T(512)S(1)} %add_dynamic-update-slice_fusion), channel_id=1, replica_groups=mesh['y'=4,'x_lo'=2,'core'=2,'x_hi'=2,'z'=8] {'y','x_lo','core'}, use_global_device_ids=true, to_apply=%add | all-reduce | flops 352 | bytes 2816
  29.1 0.1 reshape.15
  29.3 0.7 reshape_squeeze.6.rows
  29.9 0.7 reshape_squeeze.7.cols
  30.6 0.6 stack.197.order
  31.3 0.6 pad_add_fusion.4.order
  31.9 0.6 pad_add_fusion.3.order
  32.5 0.9 bitcast_dynamic-update-slice_fusion.15
  33.4 2.0 %collective-permute-start.8 = (bf16[256,384]{1,0:T(8,128)(2,1)S(1)}, bf16[256,384]{1,0:T(8,128)(2,1)S(1)}, u32[]{:S(2)}, u32[]{:S(2)}) collective-permute-start(bf16[256,384]{1,0:T(8,128)(2,1)S(1)} %collective-permute-done.7), channel_id=1, source_target_pairs={{0,1},{1,2},{2,3},{3,4},{4,5},{5,6},{6,7},{7,0},{8,9},{9,10},{10,1... | collective-permute-start | bytes 589832 | tf_op jit(solution)/shard_map/ppermute | solution.py:17
  35.4 2.3 %collective-permute-start.11 = (bf16[256,384]{1,0:T(8,128)(2,1)S(1)}, bf16[256,384]{1,0:T(8,128)(2,1)S(1)}, u32[]{:S(2)}, u32[]{:S(2)}) collective-permute-start(bf16[256,384]{1,0:T(8,128)(2,1)S(1)} %collective-permute-done.7), channel_id=1, source_target_pairs={{0,7},{1,0},{2,1},{3,2},{4,3},{5,4},{6,5},{7,6},{8,15},{9,8},{10,9... | collective-permute-start | bytes 589832 | tf_op jit(solution)/shard_map/ppermute | solution.py:17
  37.7 0.8 collective-permute-start.1
  38.5 2.4 %collective-permute-start.5 = (bf16[256,384]{1,0:T(8,128)(2,1)S(1)}, bf16[256,384]{1,0:T(8,128)(2,1)S(1)}, u32[]{:S(2)}, u32[]{:S(2)}) collective-permute-start(bf16[256,384]{1,0:T(8,128)(2,1)S(1)} %collective-permute-done.4), channel_id=1, source_target_pairs={{0,7},{1,0},{2,1},{3,2},{4,3},{5,4},{6,5},{7,6},{8,15},{9,8},{10,9... | collective-permute-start | bytes 589832 | tf_op jit(solution)/shard_map/ppermute | solution.py:17
  40.9 1.0 bitcast_dynamic-update-slice_fusion.14
  41.9 3.3 %collective-permute-done.1 = bf16[256,384]{1,0:T(8,128)(2,1)S(1)} collective-permute-done((bf16[256,384]{1,0:T(8,128)(2,1)}, bf16[256,384]{1,0:T(8,128)(2,1)S(1)}, u32[]{:S(2)}, u32[]{:S(2)}) %collective-permute-start.1) | collective-permute-done | bytes 196640 | tf_op jit(solution)/shard_map/ppermute | solution.py:17
  45.2 0.1 collective-permute-start.2
  45.3 0.1 collective-permute-done.5
  45.5 2.7 %collective-permute-start.6 = (bf16[256,384]{1,0:T(8,128)(2,1)S(1)}, bf16[256,384]{1,0:T(8,128)(2,1)S(1)}, u32[]{:S(2)}, u32[]{:S(2)}) collective-permute-start(bf16[256,384]{1,0:T(8,128)(2,1)S(1)} %collective-permute-done.5), channel_id=1, source_target_pairs={{0,7},{1,0},{2,1},{3,2},{4,3},{5,4},{6,5},{7,6},{8,15},{9,8},{10,9... | collective-permute-start | bytes 589832 | tf_op jit(solution)/shard_map/ppermute | solution.py:17
  48.2 0.5 collective-permute-start.9
  48.7 2.8 %collective-permute-start.12 = (bf16[256,384]{1,0:T(8,128)(2,1)S(1)}, bf16[256,384]{1,0:T(8,128)(2,1)S(1)}, u32[]{:S(2)}, u32[]{:S(2)}) collective-permute-start(bf16[256,384]{1,0:T(8,128)(2,1)S(1)} %collective-permute-done.11), channel_id=1, source_target_pairs={{0,7},{1,0},{2,1},{3,2},{4,3},{5,4},{6,5},{7,6},{8,15},{9,8},{10,9... | collective-permute-start | bytes 589832 | tf_op jit(solution)/shard_map/ppermute | solution.py:17
  51.6 2.3 %collective-permute-done.2 = bf16[256,384]{1,0:T(8,128)(2,1)S(1)} collective-permute-done((bf16[256,384]{1,0:T(8,128)(2,1)S(1)}, bf16[256,384]{1,0:T(8,128)(2,1)S(1)}, u32[]{:S(2)}, u32[]{:S(2)}) %collective-permute-start.2) | collective-permute-done | bytes 196640 | tf_op jit(solution)/shard_map/ppermute | solution.py:17
  53.9 4.2 %collective-permute-done.9 = bf16[256,384]{1,0:T(8,128)(2,1)S(1)} collective-permute-done((bf16[256,384]{1,0:T(8,128)(2,1)S(1)}, bf16[256,384]{1,0:T(8,128)(2,1)S(1)}, u32[]{:S(2)}, u32[]{:S(2)}) %collective-permute-start.9) | collective-permute-done | bytes 196640 | tf_op jit(solution)/shard_map/ppermute | solution.py:17
  58.1 3.3 %collective-permute-start.13 = (bf16[256,384]{1,0:T(8,128)(2,1)S(1)}, bf16[256,384]{1,0:T(8,128)(2,1)S(1)}, u32[]{:S(2)}, u32[]{:S(2)}) collective-permute-start(bf16[256,384]{1,0:T(8,128)(2,1)S(1)} %collective-permute-done.12), channel_id=1, source_target_pairs={{0,7},{1,0},{2,1},{3,2},{4,3},{5,4},{6,5},{7,6},{8,15},{9,8},{10,9... | collective-permute-start | bytes 589832 | tf_op jit(solution)/shard_map/ppermute | solution.py:17
  61.4 5.0 %collective-permute-done.13 = bf16[256,384]{1,0:T(8,128)(2,1)S(1)} collective-permute-done((bf16[256,384]{1,0:T(8,128)(2,1)S(1)}, bf16[256,384]{1,0:T(8,128)(2,1)S(1)}, u32[]{:S(2)}, u32[]{:S(2)}) %collective-permute-start.13) | collective-permute-done | bytes 196640 | tf_op jit(solution)/shard_map/ppermute | solution.py:17
  66.4 2.5 %collective-permute-start.14 = (bf16[256,384]{1,0:T(8,128)(2,1)S(1)}, bf16[256,384]{1,0:T(8,128)(2,1)S(1)}, u32[]{:S(2)}, u32[]{:S(2)}) collective-permute-start(bf16[256,384]{1,0:T(8,128)(2,1)S(1)} %collective-permute-done.13), channel_id=1, source_target_pairs={{0,7},{1,0},{2,1},{3,2},{4,3},{5,4},{6,5},{7,6},{8,15},{9,8},{10,9... | collective-permute-start | bytes 589832 | tf_op jit(solution)/shard_map/ppermute | solution.py:17
  69.4 3.5 %collective-permute-done.14 = bf16[256,384]{1,0:T(8,128)(2,1)S(1)} collective-permute-done((bf16[256,384]{1,0:T(8,128)(2,1)S(1)}, bf16[256,384]{1,0:T(8,128)(2,1)S(1)}, u32[]{:S(2)}, u32[]{:S(2)}) %collective-permute-start.14) | collective-permute-done | bytes 196640 | tf_op jit(solution)/shard_map/ppermute | solution.py:17
  72.9 9.6 %all-gather.2.cloned.1.call-done = bf16[176,128,256]{2,1,0:T(8,128)(2,1)} async-done(((bf16[11,128,256]{2,1,0:T(8,128)(2,1)}), bf16[176,128,256]{2,1,0:T(8,128)(2,1)}) %all-gather.2.cloned.1.call-update) | async-done | bytes 11534352 | tf_op jit(solution)/shard_map/all_gather | solution.py:157
  82.5 18.9 %forward.1 = (bf16[256,1536]{1,0:T(8,128)(2,1)}, bf16[12,256,256]{2,1,0:T(8,128)(2,1)}) custom-call(s32[16]{0:T(128)} %stack.197.order, s32[176]{0:T(256)} %reshape_squeeze.6.rows, s32[176]{0:T(256)} %reshape_squeeze.7.cols, bf16[16,256,384]{2,1,0:T(8,128)(2,1)} %copy-done.1, bf16[16,11,128,256]{3,2,1,0:T(8,128)(2,1)} %bitcast.96, bf16[256,1536]{1,0:T(8,128)(2,1)} %up_ref.1), custom_call_target="tpu_custom_call" | custom-call | flops 2952790016 | bytes 18612224 | tf_op jit(solution)/shard_map/forward/pallas_call | solution.py:71
  101.4 4.3 %backward.9 = f32[2,256,384]{2,1,0:T(8,128)} custom-call(s32[2]{0:T(128)} %pad_add_fusion.4.order, s32[176]{0:T(256)} %reshape_squeeze.6.rows, s32[176]{0:T(256)} %reshape_squeeze.7.cols, bf16[12,256,256]{2,1,0:T(8,128)(2,1)} %get-tuple-element.5.grads_ref, bf16[16,11,128,256]{3,2,1,0:T(8,128)(2,1)} %bitcast.97), custom_call_target="tpu_custom_call" | custom-call | flops 369098752 | bytes 3801088 | tf_op jit(solution)/shard_map/backward/pallas_call | solution.py:124
  105.7 1.2 convert_element_type.53
  107.0 1.7 collective-permute-start.15
  108.6 0.4 collective-permute-start.19
  109.1 6.3 %backward.8 = f32[4,256,384]{2,1,0:T(8,128)} custom-call(s32[4]{0:T(128)} %pad_add_fusion.3.order, s32[176]{0:T(256)} %reshape_squeeze.6.rows, s32[176]{0:T(256)} %reshape_squeeze.7.cols, bf16[12,256,256]{2,1,0:T(8,128)(2,1)} %get-tuple-element.5.grads_ref, bf16[16,11,128,256]{3,2,1,0:T(8,128)(2,1)} %bitcast.98), custom_call_target="tpu_custom_call" | custom-call | flops 738197504 | bytes 6029312 | tf_op jit(solution)/shard_map/backward/pallas_call | solution.py:124
  115.3 1.6 convert.15
  117.0 0.2 copy-done
  117.4 2.0 %collective-permute-start.20 = (bf16[2,256,384]{2,1,0:T(8,128)(2,1)S(1)}, bf16[2,256,384]{2,1,0:T(8,128)(2,1)S(1)}, u32[]{:S(2)}, u32[]{:S(2)}) collective-permute-start(bf16[2,256,384]{2,1,0:T(8,128)(2,1)S(1)} %pad_maximum_fusion.2), channel_id=1, source_target_pairs={{0,7},{1,0},{2,1},{3,2},{4,3},{5,4},{6,5},{7,6},{8,15},{9,8},{10,9... | collective-permute-start | bytes 1179656 | tf_op jit(solution)/shard_map/ppermute | solution.py:17
  119.4 0.2 collective-permute-start.16
  119.6 0.6 pad_add_fusion.2.order
  120.2 6.3 %backward.7 = f32[4,256,384]{2,1,0:T(8,128)} custom-call(s32[4]{0:T(128)} %pad_add_fusion.2.order, s32[176]{0:T(256)} %reshape_squeeze.6.rows, s32[176]{0:T(256)} %reshape_squeeze.7.cols, bf16[12,256,256]{2,1,0:T(8,128)(2,1)} %get-tuple-element.5.grads_ref, bf16[16,11,128,256]{3,2,1,0:T(8,128)(2,1)} %bitcast.99), custom_call_target="tpu_custom_call" | custom-call | flops 738197504 | bytes 6029312 | tf_op jit(solution)/shard_map/backward/pallas_call | solution.py:124
  126.5 1.7 collective-permute-done.20
  128.1 2.0 %collective-permute-done.16 = bf16[2,256,384]{2,1,0:T(8,128)(2,1)S(1)} collective-permute-done((bf16[2,256,384]{2,1,0:T(8,128)(2,1)S(1)}, bf16[2,256,384]{2,1,0:T(8,128)(2,1)S(1)}, u32[]{:S(2)}, u32[]{:S(2)}) %collective-permute-start.16) | collective-permute-done | bytes 393248 | tf_op jit(solution)/shard_map/ppermute | solution.py:17
  130.2 1.5 fusion.2
  131.7 0.5 collective-permute-start.17
  132.2 2.5 %collective-permute-start.21 = (bf16[2,256,384]{2,1,0:T(8,128)(2,1)S(1)}, bf16[2,256,384]{2,1,0:T(8,128)(2,1)S(1)}, u32[]{:S(2)}, u32[]{:S(2)}) collective-permute-start(bf16[2,256,384]{2,1,0:T(8,128)(2,1)S(1)} %get-tuple-element.11), channel_id=1, source_target_pairs={{0,7},{1,0},{2,1},{3,2},{4,3},{5,4},{6,5},{7,6},{8,15},{9,8},{10,9... | collective-permute-start | bytes 1179656 | tf_op jit(solution)/shard_map/ppermute | solution.py:17
  134.8 0.6 pad_add_fusion.1.order
  135.3 6.3 %backward.6 = f32[4,256,384]{2,1,0:T(8,128)} custom-call(s32[4]{0:T(128)} %pad_add_fusion.1.order, s32[176]{0:T(256)} %reshape_squeeze.6.rows, s32[176]{0:T(256)} %reshape_squeeze.7.cols, bf16[12,256,256]{2,1,0:T(8,128)(2,1)} %get-tuple-element.5.grads_ref, bf16[16,11,128,256]{3,2,1,0:T(8,128)(2,1)} %bitcast.100), custom_call_target="tpu_custom_call" | custom-call | flops 738197504 | bytes 6029312 | tf_op jit(solution)/shard_map/backward/pallas_call | solution.py:124
  141.6 0.8 collective-permute-done.17
  142.4 0.9 collective-permute-done.21
  143.3 1.5 fusion.3
  144.8 2.9 %collective-permute-start.18 = (bf16[2,256,384]{2,1,0:T(8,128)(2,1)S(1)}, bf16[2,256,384]{2,1,0:T(8,128)(2,1)S(1)}, u32[]{:S(2)}, u32[]{:S(2)}) collective-permute-start(bf16[2,256,384]{2,1,0:T(8,128)(2,1)S(1)} %get-tuple-element.8), channel_id=1, source_target_pairs={{0,1},{1,2},{2,3},{3,4},{4,5},{5,6},{6,7},{7,0},{8,9},{9,10},{10,1... | collective-permute-start | bytes 1179656 | tf_op jit(solution)/shard_map/ppermute | solution.py:17
  147.7 0.6 pad_add_fusion.order
  148.3 4.3 %backward.5 = f32[2,256,384]{2,1,0:T(8,128)} custom-call(s32[2]{0:T(128)} %pad_add_fusion.order, s32[176]{0:T(256)} %reshape_squeeze.6.rows, s32[176]{0:T(256)} %reshape_squeeze.7.cols, bf16[12,256,256]{2,1,0:T(8,128)(2,1)} %get-tuple-element.5.grads_ref, bf16[16,11,128,256]{3,2,1,0:T(8,128)(2,1)} %bitcast.101), custom_call_target="tpu_custom_call" | custom-call | flops 369098752 | bytes 3801088 | tf_op jit(solution)/shard_map/backward/pallas_call | solution.py:124
  152.6 1.5 collective-permute-done.18
  154.1 3.1 %collective-permute-done.22 = bf16[2,256,384]{2,1,0:T(8,128)(2,1)S(1)} collective-permute-done((bf16[2,256,384]{2,1,0:T(8,128)(2,1)S(1)}, bf16[2,256,384]{2,1,0:T(8,128)(2,1)S(1)}, u32[]{:S(2)}, u32[]{:S(2)}) %collective-permute-start.22) | collective-permute-done | bytes 393248 | tf_op jit(solution)/shard_map/ppermute | solution.py:17
  157.2 1.2 convert_add_fusion
  158.5 3.0 %collective-permute-start.23 = (bf16[256,384]{1,0:T(8,128)(2,1)S(1)}, bf16[256,384]{1,0:T(8,128)(2,1)S(1)}, u32[]{:S(2)}, u32[]{:S(2)}) collective-permute-start(bf16[256,384]{1,0:T(8,128)(2,1)S(1)} %fusion.9), channel_id=1, source_target_pairs={{0,8},{8,0},{1,9},{9,1},{2,10},{10,2},{3,11},{11,3},{4,12},{12,4},... | collective-permute-start | bytes 589832 | tf_op jit(solution)/shard_map/ppermute | solution.py:17
  161.5 4.2 %collective-permute-done.23 = bf16[256,384]{1,0:T(8,128)(2,1)S(1)} collective-permute-done((bf16[256,384]{1,0:T(8,128)(2,1)S(1)}, bf16[256,384]{1,0:T(8,128)(2,1)S(1)}, u32[]{:S(2)}, u32[]{:S(2)}) %collective-permute-start.23) | collective-permute-done | bytes 196640 | tf_op jit(solution)/shard_map/ppermute | solution.py:17
  165.8 0.7 fusion.8
  (41 shorter events, 0.9 us)
Async XLA Ops:
  7.2 75.4 %all-gather.2.cloned.1.call-start = ((), (), s32[]{:S(2)}) async-start(), calls=%async_computation | async-start | bytes 12255232 | tf_op jit(solution)/shard_map/all_gather | solution.py:157
  9.3 28.4 %collective-permute-start = (bf16[256,384]{1,0:T(8,128)(2,1)}, bf16[256,384]{1,0:T(8,128)(2,1)}, u32[]{:S(2)}, u32[]{:S(2)}) collective-permute-start(bf16[256,384]{1,0:T(8,128)(2,1)} %param.6), channel_id=1, source_target_pairs={{0,1},{1,2},{2,3},{3,4},{4,5},{5,6},{6,7},{7,0},{8,9},{9,10},{10,1... | collective-permute-start | bytes 589832 | tf_op jit(solution)/shard_map/ppermute | solution.py:17
  11.3 27.2 %collective-permute-start.4 = (bf16[256,384]{1,0:T(8,128)(2,1)}, bf16[256,384]{1,0:T(8,128)(2,1)S(1)}, u32[]{:S(2)}, u32[]{:S(2)}) collective-permute-start(bf16[256,384]{1,0:T(8,128)(2,1)} %param.6), channel_id=1, source_target_pairs={{0,7},{1,0},{2,1},{3,2},{4,3},{5,4},{6,5},{7,6},{8,15},{9,8},{10,9... | collective-permute-start | bytes 589832 | tf_op jit(solution)/shard_map/ppermute | solution.py:17
  11.4 22.1 %collective-permute-start.7 = (bf16[256,384]{1,0:T(8,128)(2,1)}, bf16[256,384]{1,0:T(8,128)(2,1)S(1)}, u32[]{:S(2)}, u32[]{:S(2)}) collective-permute-start(bf16[256,384]{1,0:T(8,128)(2,1)} %param.6), channel_id=1, source_target_pairs={{0,8},{8,0},{1,9},{9,1},{2,10},{10,2},{3,11},{11,3},{4,12},{12,4},... | collective-permute-start | bytes 589832 | tf_op jit(solution)/shard_map/ppermute | solution.py:17
  33.4 14.8 %collective-permute-start.8 = (bf16[256,384]{1,0:T(8,128)(2,1)S(1)}, bf16[256,384]{1,0:T(8,128)(2,1)S(1)}, u32[]{:S(2)}, u32[]{:S(2)}) collective-permute-start(bf16[256,384]{1,0:T(8,128)(2,1)S(1)} %collective-permute-done.7), channel_id=1, source_target_pairs={{0,1},{1,2},{2,3},{3,4},{4,5},{5,6},{6,7},{7,0},{8,9},{9,10},{10,1... | collective-permute-start | bytes 589832 | tf_op jit(solution)/shard_map/ppermute | solution.py:17
  35.4 13.3 %collective-permute-start.11 = (bf16[256,384]{1,0:T(8,128)(2,1)S(1)}, bf16[256,384]{1,0:T(8,128)(2,1)S(1)}, u32[]{:S(2)}, u32[]{:S(2)}) collective-permute-start(bf16[256,384]{1,0:T(8,128)(2,1)S(1)} %collective-permute-done.7), channel_id=1, source_target_pairs={{0,7},{1,0},{2,1},{3,2},{4,3},{5,4},{6,5},{7,6},{8,15},{9,8},{10,9... | collective-permute-start | bytes 589832 | tf_op jit(solution)/shard_map/ppermute | solution.py:17
  37.7 7.5 %collective-permute-start.1 = (bf16[256,384]{1,0:T(8,128)(2,1)}, bf16[256,384]{1,0:T(8,128)(2,1)S(1)}, u32[]{:S(2)}, u32[]{:S(2)}) collective-permute-start(bf16[256,384]{1,0:T(8,128)(2,1)} %collective-permute-done), channel_id=1, source_target_pairs={{0,1},{1,2},{2,3},{3,4},{4,5},{5,6},{6,7},{7,0},{8,9},{9,10},{10,1... | collective-permute-start | bytes 589832 | tf_op jit(solution)/shard_map/ppermute | solution.py:17
  38.5 7.0 %collective-permute-start.5 = (bf16[256,384]{1,0:T(8,128)(2,1)S(1)}, bf16[256,384]{1,0:T(8,128)(2,1)S(1)}, u32[]{:S(2)}, u32[]{:S(2)}) collective-permute-start(bf16[256,384]{1,0:T(8,128)(2,1)S(1)} %collective-permute-done.4), channel_id=1, source_target_pairs={{0,7},{1,0},{2,1},{3,2},{4,3},{5,4},{6,5},{7,6},{8,15},{9,8},{10,9... | collective-permute-start | bytes 589832 | tf_op jit(solution)/shard_map/ppermute | solution.py:17
  45.2 8.6 %collective-permute-start.2 = (bf16[256,384]{1,0:T(8,128)(2,1)S(1)}, bf16[256,384]{1,0:T(8,128)(2,1)S(1)}, u32[]{:S(2)}, u32[]{:S(2)}) collective-permute-start(bf16[256,384]{1,0:T(8,128)(2,1)S(1)} %collective-permute-done.1), channel_id=1, source_target_pairs={{0,1},{1,2},{2,3},{3,4},{4,5},{5,6},{6,7},{7,0},{8,9},{9,10},{10,1... | collective-permute-start | bytes 589832 | tf_op jit(solution)/shard_map/ppermute | solution.py:17
  45.5 23.5 %collective-permute-start.6 = (bf16[256,384]{1,0:T(8,128)(2,1)S(1)}, bf16[256,384]{1,0:T(8,128)(2,1)S(1)}, u32[]{:S(2)}, u32[]{:S(2)}) collective-permute-start(bf16[256,384]{1,0:T(8,128)(2,1)S(1)} %collective-permute-done.5), channel_id=1, source_target_pairs={{0,7},{1,0},{2,1},{3,2},{4,3},{5,4},{6,5},{7,6},{8,15},{9,8},{10,9... | collective-permute-start | bytes 589832 | tf_op jit(solution)/shard_map/ppermute | solution.py:17
  48.2 9.9 %collective-permute-start.9 = (bf16[256,384]{1,0:T(8,128)(2,1)S(1)}, bf16[256,384]{1,0:T(8,128)(2,1)S(1)}, u32[]{:S(2)}, u32[]{:S(2)}) collective-permute-start(bf16[256,384]{1,0:T(8,128)(2,1)S(1)} %collective-permute-done.8), channel_id=1, source_target_pairs={{0,1},{1,2},{2,3},{3,4},{4,5},{5,6},{6,7},{7,0},{8,9},{9,10},{10,1... | collective-permute-start | bytes 589832 | tf_op jit(solution)/shard_map/ppermute | solution.py:17
  48.7 9.4 %collective-permute-start.12 = (bf16[256,384]{1,0:T(8,128)(2,1)S(1)}, bf16[256,384]{1,0:T(8,128)(2,1)S(1)}, u32[]{:S(2)}, u32[]{:S(2)}) collective-permute-start(bf16[256,384]{1,0:T(8,128)(2,1)S(1)} %collective-permute-done.11), channel_id=1, source_target_pairs={{0,7},{1,0},{2,1},{3,2},{4,3},{5,4},{6,5},{7,6},{8,15},{9,8},{10,9... | collective-permute-start | bytes 589832 | tf_op jit(solution)/shard_map/ppermute | solution.py:17
  53.9 15.0 %collective-permute-start.3 = (bf16[256,384]{1,0:T(8,128)(2,1)S(1)}, bf16[256,384]{1,0:T(8,128)(2,1)S(1)}, u32[]{:S(2)}, u32[]{:S(2)}) collective-permute-start(bf16[256,384]{1,0:T(8,128)(2,1)S(1)} %collective-permute-done.2), channel_id=1, source_target_pairs={{0,1},{1,2},{2,3},{3,4},{4,5},{5,6},{6,7},{7,0},{8,9},{9,10},{10,1... | collective-permute-start | bytes 589832 | tf_op jit(solution)/shard_map/ppermute | solution.py:17
  58.1 11.1 %collective-permute-start.10 = (bf16[256,384]{1,0:T(8,128)(2,1)S(1)}, bf16[256,384]{1,0:T(8,128)(2,1)S(1)}, u32[]{:S(2)}, u32[]{:S(2)}) collective-permute-start(bf16[256,384]{1,0:T(8,128)(2,1)S(1)} %collective-permute-done.9), channel_id=1, source_target_pairs={{0,1},{1,2},{2,3},{3,4},{4,5},{5,6},{6,7},{7,0},{8,9},{9,10},{10,1... | collective-permute-start | bytes 589832 | tf_op jit(solution)/shard_map/ppermute | solution.py:17
  58.1 8.3 %collective-permute-start.13 = (bf16[256,384]{1,0:T(8,128)(2,1)S(1)}, bf16[256,384]{1,0:T(8,128)(2,1)S(1)}, u32[]{:S(2)}, u32[]{:S(2)}) collective-permute-start(bf16[256,384]{1,0:T(8,128)(2,1)S(1)} %collective-permute-done.12), channel_id=1, source_target_pairs={{0,7},{1,0},{2,1},{3,2},{4,3},{5,4},{6,5},{7,6},{8,15},{9,8},{10,9... | collective-permute-start | bytes 589832 | tf_op jit(solution)/shard_map/ppermute | solution.py:17
  66.4 6.5 %collective-permute-start.14 = (bf16[256,384]{1,0:T(8,128)(2,1)S(1)}, bf16[256,384]{1,0:T(8,128)(2,1)S(1)}, u32[]{:S(2)}, u32[]{:S(2)}) collective-permute-start(bf16[256,384]{1,0:T(8,128)(2,1)S(1)} %collective-permute-done.13), channel_id=1, source_target_pairs={{0,7},{1,0},{2,1},{3,2},{4,3},{5,4},{6,5},{7,6},{8,15},{9,8},{10,9... | collective-permute-start | bytes 589832 | tf_op jit(solution)/shard_map/ppermute | solution.py:17
  72.9 9.6 %copy-start.1 = (bf16[16,256,384]{2,1,0:T(8,128)(2,1)}, bf16[16,256,384]{2,1,0:T(8,128)(2,1)S(1)}, u32[]{:S(2)}) copy-start(bf16[16,256,384]{2,1,0:T(8,128)(2,1)S(1)} %bitcast_dynamic-update-slice_fusion.x_ref) | copy-start | bytes 9437188
  107.0 10.1 %collective-permute-start.15 = (bf16[256,384]{1,0:T(8,128)(2,1)S(1)}, bf16[256,384]{1,0:T(8,128)(2,1)S(1)}, u32[]{:S(2)}, u32[]{:S(2)}) collective-permute-start(bf16[256,384]{1,0:T(8,128)(2,1)S(1)} %get-tuple-element.16), channel_id=1, source_target_pairs={{0,1},{1,2},{2,3},{3,4},{4,5},{5,6},{6,7},{7,0},{8,9},{9,10},{10,1... | collective-permute-start | bytes 589832 | tf_op jit(solution)/shard_map/ppermute | solution.py:17
  108.6 8.4 %collective-permute-start.19 = (bf16[256,384]{1,0:T(8,128)(2,1)S(1)}, bf16[256,384]{1,0:T(8,128)(2,1)S(1)}, u32[]{:S(2)}, u32[]{:S(2)}) collective-permute-start(bf16[256,384]{1,0:T(8,128)(2,1)S(1)} %get-tuple-element.17), channel_id=1, source_target_pairs={{0,7},{1,0},{2,1},{3,2},{4,3},{5,4},{6,5},{7,6},{8,15},{9,8},{10,9... | collective-permute-start | bytes 589832 | tf_op jit(solution)/shard_map/ppermute | solution.py:17
  115.3 1.9 %copy-start = (f32[4,256,384]{2,1,0:T(8,128)S(1)}, f32[4,256,384]{2,1,0:T(8,128)}, u32[]{:S(2)}) copy-start(f32[4,256,384]{2,1,0:T(8,128)} %backward.8) | copy-start | bytes 4718596
  117.4 10.8 %collective-permute-start.20 = (bf16[2,256,384]{2,1,0:T(8,128)(2,1)S(1)}, bf16[2,256,384]{2,1,0:T(8,128)(2,1)S(1)}, u32[]{:S(2)}, u32[]{:S(2)}) collective-permute-start(bf16[2,256,384]{2,1,0:T(8,128)(2,1)S(1)} %pad_maximum_fusion.2), channel_id=1, source_target_pairs={{0,7},{1,0},{2,1},{3,2},{4,3},{5,4},{6,5},{7,6},{8,15},{9,8},{10,9... | collective-permute-start | bytes 1179656 | tf_op jit(solution)/shard_map/ppermute | solution.py:17
  119.4 10.8 %collective-permute-start.16 = (bf16[2,256,384]{2,1,0:T(8,128)(2,1)S(1)}, bf16[2,256,384]{2,1,0:T(8,128)(2,1)S(1)}, u32[]{:S(2)}, u32[]{:S(2)}) collective-permute-start(bf16[2,256,384]{2,1,0:T(8,128)(2,1)S(1)} %pad_maximum_fusion.1), channel_id=1, source_target_pairs={{0,1},{1,2},{2,3},{3,4},{4,5},{5,6},{6,7},{7,0},{8,9},{9,10},{10,1... | collective-permute-start | bytes 1179656 | tf_op jit(solution)/shard_map/ppermute | solution.py:17
  131.7 10.7 %collective-permute-start.17 = (bf16[2,256,384]{2,1,0:T(8,128)(2,1)S(1)}, bf16[2,256,384]{2,1,0:T(8,128)(2,1)S(1)}, u32[]{:S(2)}, u32[]{:S(2)}) collective-permute-start(bf16[2,256,384]{2,1,0:T(8,128)(2,1)S(1)} %get-tuple-element.10), channel_id=1, source_target_pairs={{0,1},{1,2},{2,3},{3,4},{4,5},{5,6},{6,7},{7,0},{8,9},{9,10},{10,1... | collective-permute-start | bytes 1179656 | tf_op jit(solution)/shard_map/ppermute | solution.py:17
  132.2 11.1 %collective-permute-start.21 = (bf16[2,256,384]{2,1,0:T(8,128)(2,1)S(1)}, bf16[2,256,384]{2,1,0:T(8,128)(2,1)S(1)}, u32[]{:S(2)}, u32[]{:S(2)}) collective-permute-start(bf16[2,256,384]{2,1,0:T(8,128)(2,1)S(1)} %get-tuple-element.11), channel_id=1, source_target_pairs={{0,7},{1,0},{2,1},{3,2},{4,3},{5,4},{6,5},{7,6},{8,15},{9,8},{10,9... | collective-permute-start | bytes 1179656 | tf_op jit(solution)/shard_map/ppermute | solution.py:17
  144.8 9.3 %collective-permute-start.18 = (bf16[2,256,384]{2,1,0:T(8,128)(2,1)S(1)}, bf16[2,256,384]{2,1,0:T(8,128)(2,1)S(1)}, u32[]{:S(2)}, u32[]{:S(2)}) collective-permute-start(bf16[2,256,384]{2,1,0:T(8,128)(2,1)S(1)} %get-tuple-element.8), channel_id=1, source_target_pairs={{0,1},{1,2},{2,3},{3,4},{4,5},{5,6},{6,7},{7,0},{8,9},{9,10},{10,1... | collective-permute-start | bytes 1179656 | tf_op jit(solution)/shard_map/ppermute | solution.py:17
  147.7 9.5 %collective-permute-start.22 = (bf16[2,256,384]{2,1,0:T(8,128)(2,1)S(1)}, bf16[2,256,384]{2,1,0:T(8,128)(2,1)S(1)}, u32[]{:S(2)}, u32[]{:S(2)}) collective-permute-start(bf16[2,256,384]{2,1,0:T(8,128)(2,1)S(1)} %get-tuple-element.9), channel_id=1, source_target_pairs={{0,7},{1,0},{2,1},{3,2},{4,3},{5,4},{6,5},{7,6},{8,15},{9,8},{10,9... | collective-permute-start | bytes 1179656 | tf_op jit(solution)/shard_map/ppermute | solution.py:17
  158.5 7.3 %collective-permute-start.23 = (bf16[256,384]{1,0:T(8,128)(2,1)S(1)}, bf16[256,384]{1,0:T(8,128)(2,1)S(1)}, u32[]{:S(2)}, u32[]{:S(2)}) collective-permute-start(bf16[256,384]{1,0:T(8,128)(2,1)S(1)} %fusion.9), channel_id=1, source_target_pairs={{0,8},{8,0},{1,9},{9,1},{2,10},{10,2},{3,11},{11,3},{4,12},{12,4},... | collective-permute-start | bytes 589832 | tf_op jit(solution)/shard_map/ppermute | solution.py:17
Sparse Core Ops, SparseCore 0:
  10.4 72.0 all-gather.1

commit v2 on v1

v2 whole, which is shorter than its diff:
```python
import functools

import jax
import jax.numpy as jnp
import numpy as np
from jax import lax
from jax.experimental import pallas as pl
from jax.experimental.pallas import tpu as pltpu
from jax.sharding import Mesh, PartitionSpec as P

AXES = ("y", "x_lo", "core", "x_hi", "z")
ROW = ("y", "x_lo", "core")
COL = ("x_hi", "z")
SIZES = {"y": 4, "x_lo": 2, "core": 2, "x_hi": 2, "z": 8}
SIDE = 128
EARLY_CHUNKS = 10
ORDER = (4, 3, -3, 2, -2, 1, -1, 0)
VMEM_LIMIT = 10 * 1024 * 1024
ON_CHIP = pl.BlockSpec(memory_space=pltpu.VMEM)
ANYWHERE = pl.BlockSpec(memory_space=pl.ANY)
SCALARS = pl.BlockSpec(memory_space=pltpu.SMEM)


TILES = [
    (0, 0, 0), (0, 0, 1), (-1, 0, 0), (-1, 0, 1), (0, 1, 0), (-2, 0, 0), (1, 1, 0), (-3, 0, 0), (-1, 1, 0),
    (0, 1, 1), (-2, 0, 1), (1, 1, 1), (-3, 0, 1), (-1, 1, 1), (2, 1, 0), (2, 1, 1),
]
CHUNKS = [(hi, dz) for dz in (0, -1, 1, -2, 2, -3, 3, 4) for hi in (0, 1)]


def plans():
    table = []
    for y, x_lo, core, x_hi, z in np.ndindex(*(SIZES[a] for a in AXES)):
        tiles = []
        for step, other_x, other_core in TILES:
            c = (core + other_core) % 2
            tiles.append((y + step * (1 - 2 * c)) % 4 * 4 + (x_lo + other_x) % 2 * 2 + c)
        chunks = [(x_hi + other) % 2 * 8 + (z + dz) % 8 for other, dz in CHUNKS]
        columns = [(x_hi + other) % 2 * 8 + (z + dz) % 8 for other in (1, 0) for dz in ORDER]
        table.append([chunks.index(k) for k in tiles] + [tiles.index(k) for k in columns])
    return np.array(table, np.int32)


PLANS = plans()


def shift(value, axis, step):
    size = SIZES[axis]
    return lax.ppermute(value, axis, [(i, (i + step) % size) for i in range(size)])


def turn(value, sign):
    pairs = []
    for y in range(4):
        for core, step in ((0, sign), (1, -sign)):
            pairs.append((y * 2 + core, (y + step) % 4 * 2 + core))
    return lax.ppermute(value, ("y", "core"), pairs)


def slot_of(ref, tile, slot):
    return ref[tile, slot * SIDE:(slot + 1) * SIDE]


def load(parts, whole, sems, first=0):
    copies = []
    for number, part in enumerate(parts):
        if len(part.shape) == len(whole.shape):
            place, first = whole.at[pl.ds(first, part.shape[0])], first + part.shape[0]
        else:
            place, first = whole.at[first], first + 1
        copy = pltpu.make_async_copy(part, place, sems.at[number])
        copy.start()
        copies.append(copy)
    return copies


def add_tile(tile, pick, names, x_ref, w_ref, acc):
    slots = names.shape[1] // 2
    for slot in range(slots):
        row = jnp.minimum(names[tile, slot], 2)
        col = names[tile, slots + slot]
        taken = x_ref[pick[tile], :, pl.ds(pl.multiple_of(row * SIDE, SIDE), SIDE)]
        acc[col] += jnp.dot(taken, slot_of(w_ref, tile, slot), preferred_element_type=jnp.float32)


def early_kernel(n_x, n_w, pick, names, *refs):
    x_parts, w_parts = refs[:n_x], refs[n_x:n_x + n_w]
    x_ref, w_ref, acc, x_sems, w_sems = refs[n_x + n_w:]
    x_copies = load(x_parts, x_ref, x_sems)
    w_copies = load(w_parts, w_ref, w_sems)
    acc[...] = jnp.zeros_like(acc)
    for copy in x_copies:
        copy.wait()

    def tile_step(tile, carry):
        pltpu.make_async_copy(w_parts[0], w_ref.at[tile], w_sems.at[tile]).wait()

        @pl.when(pick[tile] < EARLY_CHUNKS)
        def _():
            add_tile(tile, pick, names, x_ref, w_ref, acc)

        return carry

    lax.fori_loop(0, len(w_copies), tile_step, 0)


def late_kernel(n_x, n_w, pick, names, up_ref, *refs):
    x_parts, w_parts = refs[:n_x], refs[n_x:n_x + n_w]
    hidden_ref, grads_ref, x_ref, w_ref, acc, x_sems, w_sems = refs[n_x + n_w + 3:]
    first = w_ref.shape[0] - n_w
    copies = load(x_parts, x_ref, x_sems, EARLY_CHUNKS) + load(w_parts, w_ref, w_sems, first)
    for copy in copies:
        copy.wait()

    def tile_step(tile, carry):
        @pl.when((tile >= first) | (pick[tile] >= EARLY_CHUNKS))
        def _():
            add_tile(tile, pick, names, x_ref, w_ref, acc)

        return carry

    lax.fori_loop(0, w_ref.shape[0], tile_step, 0)
    for j in range(grads_ref.shape[0]):
        columns = slice(j * SIDE, (j + 1) * SIDE)
        gate = acc[j, :, :SIDE]
        up = acc[j, :, SIDE:]
        sig = 1.0 / (1.0 + jnp.exp(-gate))
        silu = gate * sig
        hidden_ref[:, columns] = (silu * up).astype(jnp.bfloat16)
        upstream = up_ref[:, columns].astype(jnp.float32)
        grads_ref[j, :, :SIDE] = (
            upstream * up * sig * (1.0 + gate * (1.0 - sig))
        ).astype(jnp.bfloat16)
        grads_ref[j, :, SIDE:] = (upstream * silu).astype(jnp.bfloat16)


def cost(tiles, slots, tokens, read, exps):
    return pl.CostEstimate(
        flops=2 * tiles * slots * tokens * SIDE * 2 * SIDE,
        bytes_accessed=read,
        transcendentals=exps,
    )


def forward_early(pick, names, x_parts, w_parts, col_count):
    tokens, span = x_parts[0].shape[1:]
    depth, pair = w_parts[0].shape
    return pl.pallas_call(
        functools.partial(early_kernel, len(x_parts), len(w_parts)),
        in_specs=[SCALARS] * 2 + [ANYWHERE] * (len(x_parts) + len(w_parts)),
        out_specs=[ON_CHIP] * 3,
        out_shape=[
            pltpu.VMEM((16, tokens, span), jnp.bfloat16),
            pltpu.VMEM((16, depth, pair), jnp.bfloat16),
            pltpu.VMEM((col_count + 1, tokens, pair), jnp.float32),
        ],
        scratch_shapes=[
            pltpu.SemaphoreType.DMA((len(x_parts),)),
            pltpu.SemaphoreType.DMA((len(w_parts),)),
        ],
        compiler_params=pltpu.CompilerParams(vmem_limit_bytes=VMEM_LIMIT),
        cost_estimate=pl.CostEstimate(flops=0, bytes_accessed=0, transcendentals=0),
        name="forward_early",
    )(pick, names, *x_parts, *w_parts)


def forward_late(pick, names, upstream, x_parts, w_parts, x, w, acc):
    tokens, width = upstream.shape
    col_count = width // SIDE
    parts = len(x_parts) + len(w_parts)
    hidden, grads, _, w, _ = pl.pallas_call(
        functools.partial(late_kernel, len(x_parts), len(w_parts)),
        in_specs=[SCALARS] * 2 + [ON_CHIP] + [ANYWHERE] * parts + [ON_CHIP] * 3,
        out_specs=[ON_CHIP] * 5,
        out_shape=[
            jax.ShapeDtypeStruct((tokens, width), jnp.bfloat16),
            pltpu.VMEM((col_count, tokens, 2 * SIDE), jnp.bfloat16),
        ] + [pltpu.VMEM(kept.shape, kept.dtype) for kept in (x, w, acc)],
        input_output_aliases={3 + parts: 2, 4 + parts: 3, 5 + parts: 4},
        scratch_shapes=[
            pltpu.SemaphoreType.DMA((len(x_parts),)),
            pltpu.SemaphoreType.DMA((len(w_parts),)),
        ],
        compiler_params=pltpu.CompilerParams(vmem_limit_bytes=VMEM_LIMIT),
        cost_estimate=cost(len(w_parts) + 2, names.shape[1] // 2, tokens, 10 * upstream.size, 2 * upstream.size),
        name="forward_late",
    )(pick, names, upstream, *x_parts, *w_parts, x, w, acc)
    return hidden, grads, w


def backward_kernel(jobs, places, names, grads_ref, w_ref, *refs):
    slots = names.shape[1] // 2
    col_count = grads_ref.shape[0]
    outs = [k for k, _, _ in jobs]
    n_out = max(outs) + 1
    acc = refs[-1]
    added, outs = refs[:-1 - n_out], refs[-1 - n_out:-1]
    filled = [0] * n_out
    for k, position, sources in jobs:
        for j in range(3):
            columns = slice(j * SIDE, (j + 1) * SIDE)
            start = jnp.zeros(acc.shape[1:], jnp.float32)
            for number, part in sources:
                start += added[number][part, :, columns].astype(jnp.float32)
            acc[j] = start
        tile = places[position]
        for slot in range(slots):
            row = names[tile, slot]
            col = jnp.minimum(names[tile, slots + slot], col_count - 1)
            acc[row] += lax.dot_general(
                grads_ref[col],
                slot_of(w_ref, tile, slot),
                (((1,), (1,)), ((), ())),
                preferred_element_type=jnp.float32,
            )
        for j in range(3):
            outs[k][filled[k], :, j * SIDE:(j + 1) * SIDE] = acc[j].astype(outs[k].dtype)
        filled[k] += 1


def backward(jobs, added, places, names, grads, w):
    tokens = grads.shape[1]
    n_out = max(k for k, _, _ in jobs) + 1
    sizes = [sum(k == out for k, _, _ in jobs) for out in range(n_out)]
    return pl.pallas_call(
        functools.partial(backward_kernel, jobs),
        in_specs=[SCALARS] * 2 + [ON_CHIP] * (2 + len(added)),
        out_specs=[ON_CHIP] * n_out,
        out_shape=[jax.ShapeDtypeStruct((size, tokens, 3 * SIDE), jnp.bfloat16) for size in sizes],
        scratch_shapes=[pltpu.VMEM((4, tokens, SIDE), jnp.float32)],
        compiler_params=pltpu.CompilerParams(vmem_limit_bytes=VMEM_LIMIT),
        cost_estimate=cost(len(jobs), names.shape[1] // 2, tokens, 2 * len(jobs) * w.size // w.shape[0], 0),
        name="backward",
    )(places, names, grads, w, *added)


def after(value, *others):
    return lax.optimization_barrier((value,) + others)[0]


def gather(own, tokens):
    def swap(value):
        return shift(value, "core", 1)

    barrier = lax.optimization_barrier
    across = shift(tokens, "x_hi", 1)
    a1, t0 = turn(own, 1), swap(own)
    b1 = shift(after(own, t0), "x_lo", 1)
    a1, across = barrier((a1, across))
    both = jnp.stack([tokens, across])
    a2 = turn(a1, 1)
    p1, m1 = shift(both, "z", 1), shift(both, "z", -1)
    t1 = swap(a1)
    a2, p1, m1, b1, t1 = barrier((a2, p1, m1, b1, t1))
    c1, a3, b2 = turn(b1, -1), turn(a2, 1), shift(a1, "x_lo", 1)
    p2, m2 = shift(p1, "z", 1), shift(m1, "z", -1)
    c1, a3, b2, p2, m2, b1, a2 = barrier((c1, a3, b2, p2, m2, b1, a2))
    c2 = turn(c1, -1)
    p3, m3 = shift(p2, "z", 1), shift(m2, "z", -1)
    p4, m4 = shift(p3[0], "z", 1), shift(m3[1], "z", -1)
    return (own, t0, a1, t1, b1, a2, c1, a3, b2), c2, (both, p1, m1, p2, m2), (p3, m3, p4, m4)


def on_device(tokens, gate_blocks, up_blocks, block_row, block_col, upstream):
    table = lax.dynamic_slice_in_dim(jnp.asarray(PLANS), lax.axis_index(AXES), 1)[0]
    tokens, gate_blocks, table = lax.optimization_barrier((tokens, gate_blocks, table))
    pick, places = table[:16], table[16:]
    slots = gate_blocks.shape[0]
    i32, bf16 = jnp.int32, jnp.bfloat16
    ids = jnp.concatenate([
        jnp.where(block_row < 0, 3, block_row % 3),
        jnp.where(block_row < 0, 12, block_col % 12),
    ]).astype(bf16)
    ids = jnp.broadcast_to(jnp.pad(ids, (0, 2 * SIDE - 2 * slots))[None], (16, 2 * SIDE))
    blocks = jnp.concatenate([gate_blocks, up_blocks], axis=2).reshape(slots * SIDE, 2 * SIDE)
    w_early, c2, x_early, x_late = gather(jnp.concatenate([blocks, ids]), tokens)

    line = lax.broadcasted_iota(i32, (16, 2 * slots), 0)

    def names_of(parts):
        names = jnp.zeros((16, 2 * slots), jnp.float32)
        for place, part in enumerate(parts):
            name = part[slots * SIDE:slots * SIDE + 1, :2 * slots].astype(jnp.float32)
            names = jnp.where(line == place, name, names)
        return names.astype(i32)

    x, w, acc = forward_early(pick, names_of(w_early), x_early, w_early, upstream.shape[1] // SIDE)
    moved, acc = lax.optimization_barrier((w_early[4:], acc))
    w_late = [shift(part, "core", 1) for part in moved] + [c2, shift(c2, "core", 1)]
    names = names_of(w_early + tuple(w_late))
    hidden, grads, w = forward_late(pick, names, upstream, x_late, w_late, x, w, acc)

    def share(jobs, added):
        return backward(jobs, added, places, names, grads, w)

    x4, x3 = share([(0, 0, ()), (1, 1, ()), (1, 2, ())], [])
    x4, x3 = shift(x4, "x_hi", 1), shift(x3, "x_hi", 1)
    plus, x2 = share([(0, 8, ((0, 0),)), (1, 3, ()), (1, 4, ())], [x4])
    plus, x2 = shift(plus, "z", 1), shift(x2, "x_hi", 1)
    plus, minus, x1 = share(
        [(0, 9, ((0, 0), (1, 0))), (1, 10, ((0, 1),)), (2, 5, ()), (2, 6, ())], [x3, plus])
    plus, minus, x1 = shift(plus, "z", 1), shift(minus, "z", -1), shift(x1, "x_hi", 1)
    plus, minus, x0 = share(
        [(0, 11, ((0, 0), (1, 0))), (1, 12, ((0, 1), (2, 0))), (2, 7, ())], [x2, plus, minus])
    plus, minus, x0 = shift(plus, "z", 1), shift(minus, "z", -1), shift(x0, "x_hi", 1)
    plus, minus = share(
        [(0, 13, ((0, 0), (1, 0))), (1, 14, ((0, 1), (2, 0)))], [x1, plus, minus])
    plus, minus = shift(plus, "z", 1), shift(minus, "z", -1)
    grad_tokens, = share([(0, 15, ((0, 0), (1, 0), (2, 0)))], [x0, plus, minus])
    return hidden, grad_tokens[0]


def solution(mesh):
    fine = Mesh(mesh.devices.reshape([SIZES[a] for a in AXES]), AXES)
    both = P(ROW, COL)
    return jax.shard_map(
        on_device,
        mesh=fine,
        in_specs=(both, P(ROW + COL, None, None), P(ROW + COL, None, None), P(ROW + COL), P(ROW + COL), both),
        out_specs=(both, both),
        check_vma=False,
    )
```

time: 174 us -> 150 us (0.86)
  waiting for transfers between devices: 42.4 us -> 59.2 us
  starting transfers between devices: 37.8 us -> 52.5 us
  between operations: 14.9 us -> 0.89 us
  Pallas kernels: 46.3 us -> 32.6 us
  blocking collectives: 11.9 us -> 0 us
  other arithmetic: 14 us -> 2.34 us
  local copies, waits for them, and re-layouts: 6.08 us -> 0.88 us
    ppermute x24 -> x31, waiting for transfers between devices: 32.7 us -> 53.6 us  [shift(): lax.ppermute(value, axis, [(i, (i + step) % size) for i in range(size)])]
    pallas_call x6 -> x8, Pallas kernels: 46.3 us -> 32.6 us  [the longest x6 12.8 us: backward(): pl.pallas_call(functools.partial(backward_kernel, jobs), in_specs=[SCALAR...]
    unnamed x1 -> x0, blocking collectives: 11.9 us -> none
    all_gather x1 -> x0, waiting for transfers between devices: 9.6 us -> none  [on_device(): lax.all_gather(pairs, ROW, axis=0, tiled=True)]
    ppermute x0 -> x5, starting transfers between devices: none -> 8.57 us  [turn(): return lax.ppermute(value, ('y', 'core'), pairs)]
    ppermute x24 -> x31, starting transfers between devices: 37.7 us -> 44 us  [shift(): lax.ppermute(value, axis, [(i, (i + step) % size) for i in range(size)])]
    ppermute x0 -> x5, waiting for transfers between devices: none -> 5.6 us  [turn(): return lax.ppermute(value, ('y', 'core'), pairs)]
    convert_element_type x5 -> x3, other arithmetic: 5.03 us -> 0.29 us  [the longest x2 0.21 us: names_of(): return names.astype(i32)]
  transfers between devices with their start and end apart: 25 -> 36, of which waited for: 14 -> 18; matrix products, arithmetic and copies ran while one was open for 7% -> 0% of each run, Pallas kernels for 13% -> 11%
where the time goes in v2:
time: 150 us; the launch traced here: 148 us
  waiting for transfers between devices  59.2 us (39%)
  starting transfers between devices  52.5 us (35%)
  Pallas kernels  32.6 us (22%)
  other arithmetic  2.34 us (2%)
    ppermute x31, waiting for transfers between devices, shift(): lax.ppermute(value, axis, [(i, (i + step) % size) for i in range(size)])  53.6 us
    ppermute x31, starting transfers between devices, shift(): lax.ppermute(value, axis, [(i, (i + step) % size) for i in range(size)])  44 us
    pallas_call x6, Pallas kernels, backward(): pl.pallas_call(functools.partial(backward_kernel, jobs), in_specs=[SCALAR...  12.8 us
    pallas_call x1, Pallas kernels, forward_late(): pl.pallas_call(functools.partial(late_kernel, len(x_parts), len(w_parts))...  12.5 us
    ppermute x5, starting transfers between devices, turn(): return lax.ppermute(value, ('y', 'core'), pairs)  8.57 us
    pallas_call x1, Pallas kernels, forward_early(): pl.pallas_call(functools.partial(early_kernel, len(x_parts), len(w_parts)...  7.24 us
    ppermute x5, waiting for transfers between devices, turn(): return lax.ppermute(value, ('y', 'core'), pairs)  5.6 us
  transfers between devices with their start and end apart: 36, of which 18 were waited for; matrix products, arithmetic and copies ran while one was open for 0% of the time, Pallas kernels for 11%

profile of v2, /device:TPU:32, one launch (start us, length us, event | category | flops | bytes accessed | tf_op | source)
XLA Modules:
  0.0 148.5 jit_solution(1779723200989815463)
XLA Ops:
  0.7 0.7 dynamic-slice_bitcast_fusion
  1.4 0.7 fusion.9
  2.1 0.1 fusion.11
  2.2 1.2 pad_maximum_fusion.1
  3.4 1.7 %collective-permute-start = (bf16[1424,256]{1,0:T(8,128)(2,1)S(1)}, bf16[1424,256]{1,0:T(8,128)(2,1)S(1)}, u32[]{:S(2)}, u32[]{:S(2)}) collective-permute-start(bf16[1424,256]{1,0:T(8,128)(2,1)S(1)} %pad_maximum_fusion.refs_5_), channel_id=1, source_target_pairs={{0,64},{16,208},{64,128},{80,16},{128,192},{144,80},{192,0},{208,1... | collective-permute-start | bytes 2187272 | tf_op jit(solution)/shard_map/ppermute | solution.py:57
  5.1 1.0 collective-permute-start.5
  6.1 3.0 %collective-permute-start.1 = (bf16[256,384]{1,0:T(8,128)(2,1)S(1)}, bf16[256,384]{1,0:T(8,128)(2,1)S(1)}, u32[]{:S(2)}, u32[]{:S(2)}) collective-permute-start(bf16[256,384]{1,0:T(8,128)(2,1)S(1)} %copy-done.1), channel_id=1, source_target_pairs={{0,8},{8,0},{1,9},{9,1},{2,10},{10,2},{3,11},{11,3},{4,12},{12,4},... | collective-permute-start | bytes 589832 | tf_op jit(solution)/shard_map/ppermute | solution.py:49
  9.1 5.3 %collective-permute-done.1 = bf16[256,384]{1,0:T(8,128)(2,1)S(1)} collective-permute-done((bf16[256,384]{1,0:T(8,128)(2,1)S(1)}, bf16[256,384]{1,0:T(8,128)(2,1)S(1)}, u32[]{:S(2)}, u32[]{:S(2)}) %collective-permute-start.1) | collective-permute-done | bytes 196640 | tf_op jit(solution)/shard_map/ppermute | solution.py:49
  14.4 1.7 %collective-permute-done.refs_7_ = bf16[1424,256]{1,0:T(8,128)(2,1)S(1)} collective-permute-done((bf16[1424,256]{1,0:T(8,128)(2,1)S(1)}, bf16[1424,256]{1,0:T(8,128)(2,1)S(1)}, u32[]{:S(2)}, u32[]{:S(2)}) %collective-permute-start) | collective-permute-done | bytes 729120 | tf_op jit(solution)/shard_map/ppermute | solution.py:57
  16.1 0.4 collective-permute-start.2
  16.5 1.5 %collective-permute-start.6 = (bf16[1424,256]{1,0:T(8,128)(2,1)S(1)}, bf16[1424,256]{1,0:T(8,128)(2,1)S(1)}, u32[]{:S(2)}, u32[]{:S(2)}) collective-permute-start(bf16[1424,256]{1,0:T(8,128)(2,1)S(1)} %pad_maximum_fusion.refs_5_), channel_id=1, source_target_pairs={{0,32},{32,0},{1,33},{33,1},{2,34},{34,2},{3,35},{35,3},{4,36},{36... | collective-permute-start | bytes 2187272 | tf_op jit(solution)/shard_map/ppermute | solution.py:49
  18.0 0.2 collective-permute-start.4
  18.2 1.9 %collective-permute-start.3 = (bf16[2,256,384]{2,1,0:T(8,128)(2,1)S(1)}, bf16[2,256,384]{2,1,0:T(8,128)(2,1)S(1)}, u32[]{:S(2)}, u32[]{:S(2)}) collective-permute-start(bf16[2,256,384]{2,1,0:T(8,128)(2,1)S(1)} %pad_maximum_fusion.2.refs_0_), channel_id=1, source_target_pairs={{0,1},{1,2},{2,3},{3,4},{4,5},{5,6},{6,7},{7,0},{8,9},{9,10},{10,1... | collective-permute-start | bytes 1179656 | tf_op jit(solution)/shard_map/ppermute | solution.py:49
  20.1 0.1 fusion.12
  20.2 9.3 %collective-permute-done.4.refs_2_ = bf16[2,256,384]{2,1,0:T(8,128)(2,1)S(1)} collective-permute-done((bf16[2,256,384]{2,1,0:T(8,128)(2,1)S(1)}, bf16[2,256,384]{2,1,0:T(8,128)(2,1)S(1)}, u32[]{:S(2)}, u32[]{:S(2)}) %collective-permute-start.4) | collective-permute-done | bytes 393248 | tf_op jit(solution)/shard_map/ppermute | solution.py:49
  29.6 0.5 collective-permute-start.10
  30.1 3.6 %collective-permute-done.3.refs_1_ = bf16[2,256,384]{2,1,0:T(8,128)(2,1)S(1)} collective-permute-done((bf16[2,256,384]{2,1,0:T(8,128)(2,1)S(1)}, bf16[2,256,384]{2,1,0:T(8,128)(2,1)S(1)}, u32[]{:S(2)}, u32[]{:S(2)}) %collective-permute-start.3) | collective-permute-done | bytes 393248 | tf_op jit(solution)/shard_map/ppermute | solution.py:49
  33.7 1.3 collective-permute-done.6.refs_9_
  35.0 3.6 %collective-permute-start.8 = (bf16[1424,256]{1,0:T(8,128)(2,1)S(1)}, bf16[1424,256]{1,0:T(8,128)(2,1)S(1)}, u32[]{:S(2)}, u32[]{:S(2)}) collective-permute-start(bf16[1424,256]{1,0:T(8,128)(2,1)S(1)} %collective-permute-done.6.refs_9_), channel_id=1, source_target_pairs={{0,192},{16,80},{64,0},{80,144},{128,64},{144,208},{192,128},{208,... | collective-permute-start | bytes 2187272 | tf_op jit(solution)/shard_map/ppermute | solution.py:57
  38.6 2.0 %collective-permute-start.11 = (bf16[2,256,384]{2,1,0:T(8,128)(2,1)S(1)}, bf16[2,256,384]{2,1,0:T(8,128)(2,1)S(1)}, u32[]{:S(2)}, u32[]{:S(2)}) collective-permute-start(bf16[2,256,384]{2,1,0:T(8,128)(2,1)S(1)} %collective-permute-done.3.refs_1_), channel_id=1, source_target_pairs={{0,1},{1,2},{2,3},{3,4},{4,5},{5,6},{6,7},{7,0},{8,9},{9,10},{10,1... | collective-permute-start | bytes 1179656 | tf_op jit(solution)/shard_map/ppermute | solution.py:49
  40.6 0.1 collective-permute-start.12
  40.7 9.9 %collective-permute-done.10.refs_13_ = bf16[1424,256]{1,0:T(8,128)(2,1)S(1)} collective-permute-done((bf16[1424,256]{1,0:T(8,128)(2,1)S(1)}, bf16[1424,256]{1,0:T(8,128)(2,1)S(1)}, u32[]{:S(2)}, u32[]{:S(2)}) %collective-permute-start.10) | collective-permute-done | bytes 729120 | tf_op jit(solution)/shard_map/ppermute | solution.py:49
  50.6 1.3 collective-permute-done.12.refs_4_
  52.0 3.2 %collective-permute-done.8.refs_11_ = bf16[1424,256]{1,0:T(8,128)(2,1)S(1)} collective-permute-done((bf16[1424,256]{1,0:T(8,128)(2,1)S(1)}, bf16[1424,256]{1,0:T(8,128)(2,1)S(1)}, u32[]{:S(2)}, u32[]{:S(2)}) %collective-permute-start.8) | collective-permute-done | bytes 729120 | tf_op jit(solution)/shard_map/ppermute | solution.py:57
  55.1 0.7 collective-permute-done.9.refs_12_
  55.9 3.0 %collective-permute-start.13 = (bf16[1424,256]{1,0:T(8,128)(2,1)S(1)}, bf16[1424,256]{1,0:T(8,128)(2,1)S(1)}, u32[]{:S(2)}, u32[]{:S(2)}) collective-permute-start(bf16[1424,256]{1,0:T(8,128)(2,1)S(1)} %collective-permute-done.8.refs_11_), channel_id=1, source_target_pairs={{0,192},{16,80},{64,0},{80,144},{128,64},{144,208},{192,128},{208,... | collective-permute-start | bytes 2187272 | tf_op jit(solution)/shard_map/ppermute | solution.py:57
  58.8 1.9 %collective-permute-start.20 = (bf16[2,256,384]{2,1,0:T(8,128)(2,1)S(1)}, bf16[2,256,384]{2,1,0:T(8,128)(2,1)S(1)}, u32[]{:S(2)}, u32[]{:S(2)}) collective-permute-start(bf16[2,256,384]{2,1,0:T(8,128)(2,1)S(1)} %collective-permute-done.11.refs_3_), channel_id=1, source_target_pairs={{0,1},{1,2},{2,3},{3,4},{4,5},{5,6},{6,7},{7,0},{8,9},{9,10},{10,1... | collective-permute-start | bytes 1179656 | tf_op jit(solution)/shard_map/ppermute | solution.py:49
  60.7 0.1 collective-permute-start.21
  60.8 0.1 fusion.names
  61.0 7.2 %forward_early.1 = (bf16[16,256,384]{2,1,0:T(8,128)(2,1)S(1)}, bf16[16,1424,256]{2,1,0:T(8,128)(2,1)S(1)}, f32[13,256,256]{2,1,0:T(8,128)S(1)}) custom-call(s32[16]{0:T(128)S(1)} %get-tuple-element.89.pick, s32[16,22]{1,0:T(8,128)S(1)} %fusion.names, bf16[2,256,384]{2,1,0:T(8,128)(2,1)S(1)} %pad_maximum_fusion.2.refs_0_, ...), custom_call_target="tpu_custom_call" | custom-call | tf_op jit(solution)/shard_map/forward_early/pallas_call | solution.py:148
  68.2 0.1 collective-permute-start.15
  68.3 0.5 collective-permute-start.16
  68.8 0.1 collective-permute-start.17
  69.0 0.5 collective-permute-start.18
  69.5 0.2 collective-permute-start.19
  69.7 0.8 collective-permute-done.15.refs_8_
  70.5 3.1 %collective-permute-start.22 = (bf16[256,384]{1,0:T(8,128)(2,1)S(1)}, bf16[256,384]{1,0:T(8,128)(2,1)S(1)}, u32[]{:S(2)}, u32[]{:S(2)}) collective-permute-start(bf16[256,384]{1,0:T(8,128)(2,1)S(1)} %slice_bitcast_fusion.1), channel_id=1, source_target_pairs={{0,1},{1,2},{2,3},{3,4},{4,5},{5,6},{6,7},{7,0},{8,9},{9,10},{10,1... | collective-permute-start | bytes 589832 | tf_op jit(solution)/shard_map/ppermute | solution.py:49
  73.6 4.1 %collective-permute-start.23 = (bf16[256,384]{1,0:T(8,128)(2,1)S(1)}, bf16[256,384]{1,0:T(8,128)(2,1)S(1)}, u32[]{:S(2)}, u32[]{:S(2)}) collective-permute-start(bf16[256,384]{1,0:T(8,128)(2,1)S(1)} %slice_bitcast_fusion), channel_id=1, source_target_pairs={{0,7},{1,0},{2,1},{3,2},{4,3},{5,4},{6,5},{7,6},{8,15},{9,8},{10,9... | collective-permute-start | bytes 589832 | tf_op jit(solution)/shard_map/ppermute | solution.py:49
  77.7 0.1 select_convert_fusion.names
  77.9 2.9 %collective-permute-done.22.refs_2_ = bf16[256,384]{1,0:T(8,128)(2,1)S(1)} collective-permute-done((bf16[256,384]{1,0:T(8,128)(2,1)S(1)}, bf16[256,384]{1,0:T(8,128)(2,1)S(1)}, u32[]{:S(2)}, u32[]{:S(2)}) %collective-permute-start.22) | collective-permute-done | bytes 196640 | tf_op jit(solution)/shard_map/ppermute | solution.py:49
  80.8 1.3 collective-permute-done.23.refs_3_
  82.1 12.5 %forward_late.1 = (bf16[256,1536]{1,0:T(8,128)(2,1)}, bf16[12,256,256]{2,1,0:T(8,128)(2,1)S(1)}, bf16[16,256,384]{2,1,0:T(8,128)(2,1)S(1)}, bf16[16,1424,256]{2,1,0:T(8,128)(2,1)S(1)}, f32[13,256,256]{2,1,0:T(8,128)S(1)}) custom-call(s32[16]{0:T(128)S(1)} %get-tuple-element.89.pick, ...), custom_call_target="tpu_custom_call", output_to_operand_aliasing={{2}: (14, {}), {3}: (15, {}), {4}: (16, {})} | custom-call | flops 1660944384 | bytes 3932160 | tf_op jit(solution)/shard_map/forward_late/pallas_call | solution.py:171
  94.7 2.2 %backward.6 = (bf16[1,256,384]{2,1,0:T(8,128)(2,1)S(1)}, bf16[2,256,384]{2,1,0:T(8,128)(2,1)S(1)}) custom-call(s32[16]{0:T(128)S(1)} %get-tuple-element.88.places, s32[16,22]{1,0:T(8,128)S(1)} %select_convert_fusion.names, bf16[12,256,256]{2,1,0:T(8,128)(2,1)S(1)} %get-tuple-element.72.grads_ref, bf16[16,1424,256]{2,1,0:T(8,128)(2,1)S(1)} %get-tuple-element.73.w_ref), custom_call_target="tpu_custom_call" | custom-call | flops 553648128 | bytes 2187264 | tf_op jit(solution)/shard_map/backward/pallas_call | solution.py:225
  96.9 3.1 %collective-permute-start.24 = (bf16[1,256,384]{2,1,0:T(8,128)(2,1)S(1)}, bf16[1,256,384]{2,1,0:T(8,128)(2,1)S(1)}, u32[]{:S(2)}, u32[]{:S(2)}) collective-permute-start(bf16[1,256,384]{2,1,0:T(8,128)(2,1)S(1)} %get-tuple-element.74), channel_id=1, source_target_pairs={{0,8},{8,0},{1,9},{9,1},{2,10},{10,2},{3,11},{11,3},{4,12},{12,4},... | collective-permute-start | bytes 589832 | tf_op jit(solution)/shard_map/ppermute | solution.py:49
  100.0 0.5 collective-permute-start.26
  100.5 5.7 %collective-permute-done.24.refs_0_ = bf16[1,256,384]{2,1,0:T(8,128)(2,1)S(1)} collective-permute-done((bf16[1,256,384]{2,1,0:T(8,128)(2,1)S(1)}, bf16[1,256,384]{2,1,0:T(8,128)(2,1)S(1)}, u32[]{:S(2)}, u32[]{:S(2)}) %collective-permute-start.24) | collective-permute-done | bytes 196640 | tf_op jit(solution)/shard_map/ppermute | solution.py:49
  106.2 2.2 %backward.7 = (bf16[1,256,384]{2,1,0:T(8,128)(2,1)S(1)}, bf16[2,256,384]{2,1,0:T(8,128)(2,1)S(1)}) custom-call(s32[16]{0:T(128)S(1)} %get-tuple-element.88.places, s32[16,22]{1,0:T(8,128)S(1)} %select_convert_fusion.names, bf16[12,256,256]{2,1,0:T(8,128)(2,1)S(1)} %get-tuple-element.72.grads_ref, bf16[16,1424,256]{2,1,0:T(8,128)(2,1)S(1)} %get-tuple-element.73.w_ref, ...), custom_call_target="tpu_custom_call" | custom-call | flops 553648128 | bytes 2187264 | tf_op jit(solution)/shard_map/backward/pallas_call | solution.py:225
  108.4 2.4 %collective-permute-start.27 = (bf16[1,256,384]{2,1,0:T(8,128)(2,1)S(1)}, bf16[1,256,384]{2,1,0:T(8,128)(2,1)S(1)}, u32[]{:S(2)}, u32[]{:S(2)}) collective-permute-start(bf16[1,256,384]{2,1,0:T(8,128)(2,1)S(1)} %get-tuple-element.77), channel_id=1, source_target_pairs={{0,1},{1,2},{2,3},{3,4},{4,5},{5,6},{6,7},{7,0},{8,9},{9,10},{10,1... | collective-permute-start | bytes 589832 | tf_op jit(solution)/shard_map/ppermute | solution.py:49
  110.7 3.0 %collective-permute-start.25 = (bf16[2,256,384]{2,1,0:T(8,128)(2,1)S(1)}, bf16[2,256,384]{2,1,0:T(8,128)(2,1)S(1)}, u32[]{:S(2)}, u32[]{:S(2)}) collective-permute-start(bf16[2,256,384]{2,1,0:T(8,128)(2,1)S(1)} %get-tuple-element.75), channel_id=1, source_target_pairs={{0,8},{8,0},{1,9},{9,1},{2,10},{10,2},{3,11},{11,3},{4,12},{12,4},... | collective-permute-start | bytes 1179656 | tf_op jit(solution)/shard_map/ppermute | solution.py:49
  113.7 0.6 collective-permute-done.27.refs_1_
  114.4 2.6 %backward.8 = (bf16[1,256,384]{2,1,0:T(8,128)(2,1)S(1)}, bf16[1,256,384]{2,1,0:T(8,128)(2,1)S(1)}, bf16[2,256,384]{2,1,0:T(8,128)(2,1)S(1)}) custom-call(s32[16]{0:T(128)S(1)} %get-tuple-element.88.places, s32[16,22]{1,0:T(8,128)S(1)} %select_convert_fusion.names, bf16[12,256,256]{2,1,0:T(8,128)(2,1)S(1)} %get-tuple-element.72.grads_ref, ...), custom_call_target="tpu_custom_call" | custom-call | flops 738197504 | bytes 2916352 | tf_op jit(solution)/shard_map/backward/pallas_call | solution.py:225
  116.9 3.2 %collective-permute-start.28 = (bf16[1,256,384]{2,1,0:T(8,128)(2,1)S(1)}, bf16[1,256,384]{2,1,0:T(8,128)(2,1)S(1)}, u32[]{:S(2)}, u32[]{:S(2)}) collective-permute-start(bf16[1,256,384]{2,1,0:T(8,128)(2,1)S(1)} %get-tuple-element.78), channel_id=1, source_target_pairs={{0,1},{1,2},{2,3},{3,4},{4,5},{5,6},{6,7},{7,0},{8,9},{9,10},{10,1... | collective-permute-start | bytes 589832 | tf_op jit(solution)/shard_map/ppermute | solution.py:49
  120.1 3.2 %collective-permute-start.31 = (bf16[2,256,384]{2,1,0:T(8,128)(2,1)S(1)}, bf16[2,256,384]{2,1,0:T(8,128)(2,1)S(1)}, u32[]{:S(2)}, u32[]{:S(2)}) collective-permute-start(bf16[2,256,384]{2,1,0:T(8,128)(2,1)S(1)} %get-tuple-element.81), channel_id=1, source_target_pairs={{0,8},{8,0},{1,9},{9,1},{2,10},{10,2},{3,11},{11,3},{4,12},{12,4},... | collective-permute-start | bytes 1179656 | tf_op jit(solution)/shard_map/ppermute | solution.py:49
  123.3 2.5 %collective-permute-done.29.refs_2_ = bf16[1,256,384]{2,1,0:T(8,128)(2,1)S(1)} collective-permute-done((bf16[1,256,384]{2,1,0:T(8,128)(2,1)S(1)}, bf16[1,256,384]{2,1,0:T(8,128)(2,1)S(1)}, u32[]{:S(2)}, u32[]{:S(2)}) %collective-permute-start.29) | collective-permute-done | bytes 196640 | tf_op jit(solution)/shard_map/ppermute | solution.py:49
  125.8 2.2 %backward.9 = (bf16[1,256,384]{2,1,0:T(8,128)(2,1)S(1)}, bf16[1,256,384]{2,1,0:T(8,128)(2,1)S(1)}, bf16[1,256,384]{2,1,0:T(8,128)(2,1)S(1)}) custom-call(s32[16]{0:T(128)S(1)} %get-tuple-element.88.places, s32[16,22]{1,0:T(8,128)S(1)} %select_convert_fusion.names, bf16[12,256,256]{2,1,0:T(8,128)(2,1)S(1)} %get-tuple-element.72.grads_ref, ...), custom_call_target="tpu_custom_call" | custom-call | flops 553648128 | bytes 2187264 | tf_op jit(solution)/shard_map/backward/pallas_call | solution.py:225
  128.1 2.1 %collective-permute-start.32 = (bf16[1,256,384]{2,1,0:T(8,128)(2,1)S(1)}, bf16[1,256,384]{2,1,0:T(8,128)(2,1)S(1)}, u32[]{:S(2)}, u32[]{:S(2)}) collective-permute-start(bf16[1,256,384]{2,1,0:T(8,128)(2,1)S(1)} %get-tuple-element.82), channel_id=1, source_target_pairs={{0,1},{1,2},{2,3},{3,4},{4,5},{5,6},{6,7},{7,0},{8,9},{9,10},{10,1... | collective-permute-start | bytes 589832 | tf_op jit(solution)/shard_map/ppermute | solution.py:49
  130.2 3.6 %collective-permute-start.30 = (bf16[1,256,384]{2,1,0:T(8,128)(2,1)S(1)}, bf16[1,256,384]{2,1,0:T(8,128)(2,1)S(1)}, u32[]{:S(2)}, u32[]{:S(2)}) collective-permute-start(bf16[1,256,384]{2,1,0:T(8,128)(2,1)S(1)} %get-tuple-element.80), channel_id=1, source_target_pairs={{0,8},{8,0},{1,9},{9,1},{2,10},{10,2},{3,11},{11,3},{4,12},{12,4},... | collective-permute-start | bytes 589832 | tf_op jit(solution)/shard_map/ppermute | solution.py:49
  133.8 0.0 collective-permute-done.32.refs_1_
  133.8 3.2 %collective-permute-done.33.refs_2_ = bf16[1,256,384]{2,1,0:T(8,128)(2,1)S(1)} collective-permute-done((bf16[1,256,384]{2,1,0:T(8,128)(2,1)S(1)}, bf16[1,256,384]{2,1,0:T(8,128)(2,1)S(1)}, u32[]{:S(2)}, u32[]{:S(2)}) %collective-permute-start.33) | collective-permute-done | bytes 196640 | tf_op jit(solution)/shard_map/ppermute | solution.py:49
  137.0 1.7 %backward.10 = (bf16[1,256,384]{2,1,0:T(8,128)(2,1)S(1)}, bf16[1,256,384]{2,1,0:T(8,128)(2,1)S(1)}) custom-call(s32[16]{0:T(128)S(1)} %get-tuple-element.88.places, s32[16,22]{1,0:T(8,128)S(1)} %select_convert_fusion.names, bf16[12,256,256]{2,1,0:T(8,128)(2,1)S(1)} %get-tuple-element.72.grads_ref, bf16[16,1424,256]{2,1,0:T(8,128)(2,1)S(1)} %get-tuple-element.73.w_ref, ...), custom_call_target="tpu_custom_call" | custom-call | flops 369098752 | bytes 1458176 | tf_op jit(solution)/shard_map/backward/pallas_call | solution.py:225
  138.7 2.1 %collective-permute-start.34 = (bf16[1,256,384]{2,1,0:T(8,128)(2,1)S(1)}, bf16[1,256,384]{2,1,0:T(8,128)(2,1)S(1)}, u32[]{:S(2)}, u32[]{:S(2)}) collective-permute-start(bf16[1,256,384]{2,1,0:T(8,128)(2,1)S(1)} %get-tuple-element.84), channel_id=1, source_target_pairs={{0,1},{1,2},{2,3},{3,4},{4,5},{5,6},{6,7},{7,0},{8,9},{9,10},{10,1... | collective-permute-start | bytes 589832 | tf_op jit(solution)/shard_map/ppermute | solution.py:49
  140.8 3.6 %collective-permute-done.34.refs_1_ = bf16[1,256,384]{2,1,0:T(8,128)(2,1)S(1)} collective-permute-done((bf16[1,256,384]{2,1,0:T(8,128)(2,1)S(1)}, bf16[1,256,384]{2,1,0:T(8,128)(2,1)S(1)}, u32[]{:S(2)}, u32[]{:S(2)}) %collective-permute-start.34) | collective-permute-done | bytes 196640 | tf_op jit(solution)/shard_map/ppermute | solution.py:49
  144.5 2.0 %collective-permute-done.35.refs_2_ = bf16[1,256,384]{2,1,0:T(8,128)(2,1)S(1)} collective-permute-done((bf16[1,256,384]{2,1,0:T(8,128)(2,1)S(1)}, bf16[1,256,384]{2,1,0:T(8,128)(2,1)S(1)}, u32[]{:S(2)}, u32[]{:S(2)}) %collective-permute-start.35) | collective-permute-done | bytes 196640 | tf_op jit(solution)/shard_map/ppermute | solution.py:49
  146.5 2.0 %backward.11 = bf16[1,256,384]{2,1,0:T(8,128)(2,1)} custom-call(s32[16]{0:T(128)S(1)} %get-tuple-element.88.places, s32[16,22]{1,0:T(8,128)S(1)} %select_convert_fusion.names, bf16[12,256,256]{2,1,0:T(8,128)(2,1)S(1)} %get-tuple-element.72.grads_ref, bf16[16,1424,256]{2,1,0:T(8,128)(2,1)S(1)} %get-tuple-element.73.w_ref, ...), custom_call_target="tpu_custom_call" | custom-call | flops 184549376 | bytes 729088 | tf_op jit(solution)/shard_map/backward/pallas_call | solution.py:225
  (55 shorter events, 0.3 us)
Async XLA Ops:
  0.6 5.4 %copy-start.1 = (bf16[256,384]{1,0:T(8,128)(2,1)S(1)}, bf16[256,384]{1,0:T(8,128)(2,1)}, u32[]{:S(2)}) copy-start(bf16[256,384]{1,0:T(8,128)(2,1)} %param.7) | copy-start | bytes 589828
  3.4 12.7 %collective-permute-start = (bf16[1424,256]{1,0:T(8,128)(2,1)S(1)}, bf16[1424,256]{1,0:T(8,128)(2,1)S(1)}, u32[]{:S(2)}, u32[]{:S(2)}) collective-permute-start(bf16[1424,256]{1,0:T(8,128)(2,1)S(1)} %pad_maximum_fusion.refs_5_), channel_id=1, source_target_pairs={{0,64},{16,208},{64,128},{80,16},{128,192},{144,80},{192,0},{208,1... | collective-permute-start | bytes 2187272 | tf_op jit(solution)/shard_map/ppermute | solution.py:57
  5.1 11.4 %collective-permute-start.5 = (bf16[1424,256]{1,0:T(8,128)(2,1)S(1)}, bf16[1424,256]{1,0:T(8,128)(2,1)S(1)}, u32[]{:S(2)}, u32[]{:S(2)}) collective-permute-start(bf16[1424,256]{1,0:T(8,128)(2,1)S(1)} %pad_maximum_fusion.refs_5_), channel_id=1, source_target_pairs={{0,16},{16,0},{1,17},{17,1},{2,18},{18,2},{3,19},{19,3},{4,20},{20... | collective-permute-start | bytes 2187272 | tf_op jit(solution)/shard_map/ppermute | solution.py:49
  6.1 8.3 %collective-permute-start.1 = (bf16[256,384]{1,0:T(8,128)(2,1)S(1)}, bf16[256,384]{1,0:T(8,128)(2,1)S(1)}, u32[]{:S(2)}, u32[]{:S(2)}) collective-permute-start(bf16[256,384]{1,0:T(8,128)(2,1)S(1)} %copy-done.1), channel_id=1, source_target_pairs={{0,8},{8,0},{1,9},{9,1},{2,10},{10,2},{3,11},{11,3},{4,12},{12,4},... | collective-permute-start | bytes 589832 | tf_op jit(solution)/shard_map/ppermute | solution.py:49
  16.1 18.9 %collective-permute-start.7 = (bf16[1424,256]{1,0:T(8,128)(2,1)S(1)}, bf16[1424,256]{1,0:T(8,128)(2,1)S(1)}, u32[]{:S(2)}, u32[]{:S(2)}) collective-permute-start(bf16[1424,256]{1,0:T(8,128)(2,1)S(1)} %collective-permute-done.refs_7_), channel_id=1, source_target_pairs={{0,16},{16,0},{1,17},{17,1},{2,18},{18,2},{3,19},{19,3},{4,20},{20... | collective-permute-start | bytes 2187272 | tf_op jit(solution)/shard_map/ppermute | solution.py:49
  16.1 18.9 %collective-permute-start.2 = (bf16[1424,256]{1,0:T(8,128)(2,1)S(1)}, bf16[1424,256]{1,0:T(8,128)(2,1)S(1)}, u32[]{:S(2)}, u32[]{:S(2)}) collective-permute-start(bf16[1424,256]{1,0:T(8,128)(2,1)S(1)} %collective-permute-done.refs_7_), channel_id=1, source_target_pairs={{0,64},{16,208},{64,128},{80,16},{128,192},{144,80},{192,0},{208,1... | collective-permute-start | bytes 2187272 | tf_op jit(solution)/shard_map/ppermute | solution.py:57
  16.5 18.5 %collective-permute-start.6 = (bf16[1424,256]{1,0:T(8,128)(2,1)S(1)}, bf16[1424,256]{1,0:T(8,128)(2,1)S(1)}, u32[]{:S(2)}, u32[]{:S(2)}) collective-permute-start(bf16[1424,256]{1,0:T(8,128)(2,1)S(1)} %pad_maximum_fusion.refs_5_), channel_id=1, source_target_pairs={{0,32},{32,0},{1,33},{33,1},{2,34},{34,2},{3,35},{35,3},{4,36},{36... | collective-permute-start | bytes 2187272 | tf_op jit(solution)/shard_map/ppermute | solution.py:49
  18.0 11.5 %collective-permute-start.4 = (bf16[2,256,384]{2,1,0:T(8,128)(2,1)S(1)}, bf16[2,256,384]{2,1,0:T(8,128)(2,1)S(1)}, u32[]{:S(2)}, u32[]{:S(2)}) collective-permute-start(bf16[2,256,384]{2,1,0:T(8,128)(2,1)S(1)} %pad_maximum_fusion.2.refs_0_), channel_id=1, source_target_pairs={{0,7},{1,0},{2,1},{3,2},{4,3},{5,4},{6,5},{7,6},{8,15},{9,8},{10,9... | collective-permute-start | bytes 1179656 | tf_op jit(solution)/shard_map/ppermute | solution.py:49
  18.2 15.5 %collective-permute-start.3 = (bf16[2,256,384]{2,1,0:T(8,128)(2,1)S(1)}, bf16[2,256,384]{2,1,0:T(8,128)(2,1)S(1)}, u32[]{:S(2)}, u32[]{:S(2)}) collective-permute-start(bf16[2,256,384]{2,1,0:T(8,128)(2,1)S(1)} %pad_maximum_fusion.2.refs_0_), channel_id=1, source_target_pairs={{0,1},{1,2},{2,3},{3,4},{4,5},{5,6},{6,7},{7,0},{8,9},{9,10},{10,1... | collective-permute-start | bytes 1179656 | tf_op jit(solution)/shard_map/ppermute | solution.py:49
  29.6 21.1 %collective-permute-start.10 = (bf16[1424,256]{1,0:T(8,128)(2,1)S(1)}, bf16[1424,256]{1,0:T(8,128)(2,1)S(1)}, u32[]{:S(2)}, u32[]{:S(2)}) collective-permute-start(bf16[1424,256]{1,0:T(8,128)(2,1)S(1)} %collective-permute-done.refs_7_), channel_id=1, source_target_pairs={{0,32},{32,0},{1,33},{33,1},{2,34},{34,2},{3,35},{35,3},{4,36},{36... | collective-permute-start | bytes 2187272 | tf_op jit(solution)/shard_map/ppermute | solution.py:49
  35.0 20.1 %collective-permute-start.8 = (bf16[1424,256]{1,0:T(8,128)(2,1)S(1)}, bf16[1424,256]{1,0:T(8,128)(2,1)S(1)}, u32[]{:S(2)}, u32[]{:S(2)}) collective-permute-start(bf16[1424,256]{1,0:T(8,128)(2,1)S(1)} %collective-permute-done.6.refs_9_), channel_id=1, source_target_pairs={{0,192},{16,80},{64,0},{80,144},{128,64},{144,208},{192,128},{208,... | collective-permute-start | bytes 2187272 | tf_op jit(solution)/shard_map/ppermute | solution.py:57
  38.6 17.3 %collective-permute-start.9 = (bf16[1424,256]{1,0:T(8,128)(2,1)S(1)}, bf16[1424,256]{1,0:T(8,128)(2,1)S(1)}, u32[]{:S(2)}, u32[]{:S(2)}) collective-permute-start(bf16[1424,256]{1,0:T(8,128)(2,1)S(1)} %collective-permute-done.2.refs_10_), channel_id=1, source_target_pairs={{0,64},{16,208},{64,128},{80,16},{128,192},{144,80},{192,0},{208,1... | collective-permute-start | bytes 2187272 | tf_op jit(solution)/shard_map/ppermute | solution.py:57
  38.6 12.0 %collective-permute-start.11 = (bf16[2,256,384]{2,1,0:T(8,128)(2,1)S(1)}, bf16[2,256,384]{2,1,0:T(8,128)(2,1)S(1)}, u32[]{:S(2)}, u32[]{:S(2)}) collective-permute-start(bf16[2,256,384]{2,1,0:T(8,128)(2,1)S(1)} %collective-permute-done.3.refs_1_), channel_id=1, source_target_pairs={{0,1},{1,2},{2,3},{3,4},{4,5},{5,6},{6,7},{7,0},{8,9},{9,10},{10,1... | collective-permute-start | bytes 1179656 | tf_op jit(solution)/shard_map/ppermute | solution.py:49
  40.6 11.4 %collective-permute-start.12 = (bf16[2,256,384]{2,1,0:T(8,128)(2,1)S(1)}, bf16[2,256,384]{2,1,0:T(8,128)(2,1)S(1)}, u32[]{:S(2)}, u32[]{:S(2)}) collective-permute-start(bf16[2,256,384]{2,1,0:T(8,128)(2,1)S(1)} %collective-permute-done.4.refs_2_), channel_id=1, source_target_pairs={{0,7},{1,0},{2,1},{3,2},{4,3},{5,4},{6,5},{7,6},{8,15},{9,8},{10,9... | collective-permute-start | bytes 1179656 | tf_op jit(solution)/shard_map/ppermute | solution.py:49
  55.9 13.6 %collective-permute-start.13 = (bf16[1424,256]{1,0:T(8,128)(2,1)S(1)}, bf16[1424,256]{1,0:T(8,128)(2,1)S(1)}, u32[]{:S(2)}, u32[]{:S(2)}) collective-permute-start(bf16[1424,256]{1,0:T(8,128)(2,1)S(1)} %collective-permute-done.8.refs_11_), channel_id=1, source_target_pairs={{0,192},{16,80},{64,0},{80,144},{128,64},{144,208},{192,128},{208,... | collective-permute-start | bytes 2187272 | tf_op jit(solution)/shard_map/ppermute | solution.py:57
  58.8 10.0 %collective-permute-start.20 = (bf16[2,256,384]{2,1,0:T(8,128)(2,1)S(1)}, bf16[2,256,384]{2,1,0:T(8,128)(2,1)S(1)}, u32[]{:S(2)}, u32[]{:S(2)}) collective-permute-start(bf16[2,256,384]{2,1,0:T(8,128)(2,1)S(1)} %collective-permute-done.11.refs_3_), channel_id=1, source_target_pairs={{0,1},{1,2},{2,3},{3,4},{4,5},{5,6},{6,7},{7,0},{8,9},{9,10},{10,1... | collective-permute-start | bytes 1179656 | tf_op jit(solution)/shard_map/ppermute | solution.py:49
  60.7 8.2 %collective-permute-start.21 = (bf16[2,256,384]{2,1,0:T(8,128)(2,1)S(1)}, bf16[2,256,384]{2,1,0:T(8,128)(2,1)S(1)}, u32[]{:S(2)}, u32[]{:S(2)}) collective-permute-start(bf16[2,256,384]{2,1,0:T(8,128)(2,1)S(1)} %collective-permute-done.12.refs_4_), channel_id=1, source_target_pairs={{0,7},{1,0},{2,1},{3,2},{4,3},{5,4},{6,5},{7,6},{8,15},{9,8},{10,9... | collective-permute-start | bytes 1179656 | tf_op jit(solution)/shard_map/ppermute | solution.py:49
  60.9 21.2 %copy-start = (bf16[256,1536]{1,0:T(8,128)(2,1)S(1)}, bf16[256,1536]{1,0:T(8,128)(2,1)}, u32[]{:S(2)}) copy-start(bf16[256,1536]{1,0:T(8,128)(2,1)} %up_ref.1) | copy-start | bytes 2359300
  68.2 2.3 %collective-permute-start.15 = (bf16[1424,256]{1,0:T(8,128)(2,1)S(1)}, bf16[1424,256]{1,0:T(8,128)(2,1)S(1)}, u32[]{:S(2)}, u32[]{:S(2)}) collective-permute-start(bf16[1424,256]{1,0:T(8,128)(2,1)S(1)} %collective-permute-done.10.refs_13_), channel_id=1, source_target_pairs={{0,16},{16,0},{1,17},{17,1},{2,18},{18,2},{3,19},{19,3},{4,20},{20... | collective-permute-start | bytes 2187272 | tf_op jit(solution)/shard_map/ppermute | solution.py:49
  68.3 5.3 %collective-permute-start.16 = (bf16[1424,256]{1,0:T(8,128)(2,1)S(1)}, bf16[1424,256]{1,0:T(8,128)(2,1)S(1)}, u32[]{:S(2)}, u32[]{:S(2)}) collective-permute-start(bf16[1424,256]{1,0:T(8,128)(2,1)S(1)} %collective-permute-done.9.refs_12_), channel_id=1, source_target_pairs={{0,16},{16,0},{1,17},{17,1},{2,18},{18,2},{3,19},{19,3},{4,20},{20... | collective-permute-start | bytes 2187272 | tf_op jit(solution)/shard_map/ppermute | solution.py:49
  68.8 4.8 %collective-permute-start.17 = (bf16[1424,256]{1,0:T(8,128)(2,1)S(1)}, bf16[1424,256]{1,0:T(8,128)(2,1)S(1)}, u32[]{:S(2)}, u32[]{:S(2)}) collective-permute-start(bf16[1424,256]{1,0:T(8,128)(2,1)S(1)} %collective-permute-done.8.refs_11_), channel_id=1, source_target_pairs={{0,16},{16,0},{1,17},{17,1},{2,18},{18,2},{3,19},{19,3},{4,20},{20... | collective-permute-start | bytes 2187272 | tf_op jit(solution)/shard_map/ppermute | solution.py:49
  69.0 8.7 %collective-permute-start.18 = (bf16[1424,256]{1,0:T(8,128)(2,1)S(1)}, bf16[1424,256]{1,0:T(8,128)(2,1)S(1)}, u32[]{:S(2)}, u32[]{:S(2)}) collective-permute-start(bf16[1424,256]{1,0:T(8,128)(2,1)S(1)} %collective-permute-done.2.refs_10_), channel_id=1, source_target_pairs={{0,16},{16,0},{1,17},{17,1},{2,18},{18,2},{3,19},{19,3},{4,20},{20... | collective-permute-start | bytes 2187272 | tf_op jit(solution)/shard_map/ppermute | solution.py:49
  69.5 8.2 %collective-permute-start.19 = (bf16[1424,256]{1,0:T(8,128)(2,1)S(1)}, bf16[1424,256]{1,0:T(8,128)(2,1)S(1)}, u32[]{:S(2)}, u32[]{:S(2)}) collective-permute-start(bf16[1424,256]{1,0:T(8,128)(2,1)S(1)} %collective-permute-done.6.refs_9_), channel_id=1, source_target_pairs={{0,16},{16,0},{1,17},{17,1},{2,18},{18,2},{3,19},{19,3},{4,20},{20... | collective-permute-start | bytes 2187272 | tf_op jit(solution)/shard_map/ppermute | solution.py:49
  70.5 10.3 %collective-permute-start.22 = (bf16[256,384]{1,0:T(8,128)(2,1)S(1)}, bf16[256,384]{1,0:T(8,128)(2,1)S(1)}, u32[]{:S(2)}, u32[]{:S(2)}) collective-permute-start(bf16[256,384]{1,0:T(8,128)(2,1)S(1)} %slice_bitcast_fusion.1), channel_id=1, source_target_pairs={{0,1},{1,2},{2,3},{3,4},{4,5},{5,6},{6,7},{7,0},{8,9},{9,10},{10,1... | collective-permute-start | bytes 589832 | tf_op jit(solution)/shard_map/ppermute | solution.py:49
  73.6 4.1 %collective-permute-start.14 = (bf16[1424,256]{1,0:T(8,128)(2,1)S(1)}, bf16[1424,256]{1,0:T(8,128)(2,1)S(1)}, u32[]{:S(2)}, u32[]{:S(2)}) collective-permute-start(bf16[1424,256]{1,0:T(8,128)(2,1)S(1)} %collective-permute-done.13.refs_9_), channel_id=1, source_target_pairs={{0,16},{16,0},{1,17},{17,1},{2,18},{18,2},{3,19},{19,3},{4,20},{20... | collective-permute-start | bytes 2187272 | tf_op jit(solution)/shard_map/ppermute | solution.py:49
  73.6 8.5 %collective-permute-start.23 = (bf16[256,384]{1,0:T(8,128)(2,1)S(1)}, bf16[256,384]{1,0:T(8,128)(2,1)S(1)}, u32[]{:S(2)}, u32[]{:S(2)}) collective-permute-start(bf16[256,384]{1,0:T(8,128)(2,1)S(1)} %slice_bitcast_fusion), channel_id=1, source_target_pairs={{0,7},{1,0},{2,1},{3,2},{4,3},{5,4},{6,5},{7,6},{8,15},{9,8},{10,9... | collective-permute-start | bytes 589832 | tf_op jit(solution)/shard_map/ppermute | solution.py:49
  96.9 9.4 %collective-permute-start.24 = (bf16[1,256,384]{2,1,0:T(8,128)(2,1)S(1)}, bf16[1,256,384]{2,1,0:T(8,128)(2,1)S(1)}, u32[]{:S(2)}, u32[]{:S(2)}) collective-permute-start(bf16[1,256,384]{2,1,0:T(8,128)(2,1)S(1)} %get-tuple-element.74), channel_id=1, source_target_pairs={{0,8},{8,0},{1,9},{9,1},{2,10},{10,2},{3,11},{11,3},{4,12},{12,4},... | collective-permute-start | bytes 589832 | tf_op jit(solution)/shard_map/ppermute | solution.py:49
  100.0 14.4 %collective-permute-start.26 = (bf16[2,256,384]{2,1,0:T(8,128)(2,1)S(1)}, bf16[2,256,384]{2,1,0:T(8,128)(2,1)S(1)}, u32[]{:S(2)}, u32[]{:S(2)}) collective-permute-start(bf16[2,256,384]{2,1,0:T(8,128)(2,1)S(1)} %get-tuple-element.76), channel_id=1, source_target_pairs={{0,8},{8,0},{1,9},{9,1},{2,10},{10,2},{3,11},{11,3},{4,12},{12,4},... | collective-permute-start | bytes 1179656 | tf_op jit(solution)/shard_map/ppermute | solution.py:49
  108.4 6.0 %collective-permute-start.27 = (bf16[1,256,384]{2,1,0:T(8,128)(2,1)S(1)}, bf16[1,256,384]{2,1,0:T(8,128)(2,1)S(1)}, u32[]{:S(2)}, u32[]{:S(2)}) collective-permute-start(bf16[1,256,384]{2,1,0:T(8,128)(2,1)S(1)} %get-tuple-element.77), channel_id=1, source_target_pairs={{0,1},{1,2},{2,3},{3,4},{4,5},{5,6},{6,7},{7,0},{8,9},{9,10},{10,1... | collective-permute-start | bytes 589832 | tf_op jit(solution)/shard_map/ppermute | solution.py:49
  110.7 12.6 %collective-permute-start.25 = (bf16[2,256,384]{2,1,0:T(8,128)(2,1)S(1)}, bf16[2,256,384]{2,1,0:T(8,128)(2,1)S(1)}, u32[]{:S(2)}, u32[]{:S(2)}) collective-permute-start(bf16[2,256,384]{2,1,0:T(8,128)(2,1)S(1)} %get-tuple-element.75), channel_id=1, source_target_pairs={{0,8},{8,0},{1,9},{9,1},{2,10},{10,2},{3,11},{11,3},{4,12},{12,4},... | collective-permute-start | bytes 1179656 | tf_op jit(solution)/shard_map/ppermute | solution.py:49
  116.9 6.4 %collective-permute-start.28 = (bf16[1,256,384]{2,1,0:T(8,128)(2,1)S(1)}, bf16[1,256,384]{2,1,0:T(8,128)(2,1)S(1)}, u32[]{:S(2)}, u32[]{:S(2)}) collective-permute-start(bf16[1,256,384]{2,1,0:T(8,128)(2,1)S(1)} %get-tuple-element.78), channel_id=1, source_target_pairs={{0,1},{1,2},{2,3},{3,4},{4,5},{5,6},{6,7},{7,0},{8,9},{9,10},{10,1... | collective-permute-start | bytes 589832 | tf_op jit(solution)/shard_map/ppermute | solution.py:49
  120.1 5.7 %collective-permute-start.29 = (bf16[1,256,384]{2,1,0:T(8,128)(2,1)S(1)}, bf16[1,256,384]{2,1,0:T(8,128)(2,1)S(1)}, u32[]{:S(2)}, u32[]{:S(2)}) collective-permute-start(bf16[1,256,384]{2,1,0:T(8,128)(2,1)S(1)} %get-tuple-element.79), channel_id=1, source_target_pairs={{0,7},{1,0},{2,1},{3,2},{4,3},{5,4},{6,5},{7,6},{8,15},{9,8},{10,9... | collective-permute-start | bytes 589832 | tf_op jit(solution)/shard_map/ppermute | solution.py:49
  120.1 16.8 %collective-permute-start.31 = (bf16[2,256,384]{2,1,0:T(8,128)(2,1)S(1)}, bf16[2,256,384]{2,1,0:T(8,128)(2,1)S(1)}, u32[]{:S(2)}, u32[]{:S(2)}) collective-permute-start(bf16[2,256,384]{2,1,0:T(8,128)(2,1)S(1)} %get-tuple-element.81), channel_id=1, source_target_pairs={{0,8},{8,0},{1,9},{9,1},{2,10},{10,2},{3,11},{11,3},{4,12},{12,4},... | collective-permute-start | bytes 1179656 | tf_op jit(solution)/shard_map/ppermute | solution.py:49
  128.1 5.7 %collective-permute-start.32 = (bf16[1,256,384]{2,1,0:T(8,128)(2,1)S(1)}, bf16[1,256,384]{2,1,0:T(8,128)(2,1)S(1)}, u32[]{:S(2)}, u32[]{:S(2)}) collective-permute-start(bf16[1,256,384]{2,1,0:T(8,128)(2,1)S(1)} %get-tuple-element.82), channel_id=1, source_target_pairs={{0,1},{1,2},{2,3},{3,4},{4,5},{5,6},{6,7},{7,0},{8,9},{9,10},{10,1... | collective-permute-start | bytes 589832 | tf_op jit(solution)/shard_map/ppermute | solution.py:49
  130.1 6.8 %collective-permute-start.33 = (bf16[1,256,384]{2,1,0:T(8,128)(2,1)S(1)}, bf16[1,256,384]{2,1,0:T(8,128)(2,1)S(1)}, u32[]{:S(2)}, u32[]{:S(2)}) collective-permute-start(bf16[1,256,384]{2,1,0:T(8,128)(2,1)S(1)} %get-tuple-element.83), channel_id=1, source_target_pairs={{0,7},{1,0},{2,1},{3,2},{4,3},{5,4},{6,5},{7,6},{8,15},{9,8},{10,9... | collective-permute-start | bytes 589832 | tf_op jit(solution)/shard_map/ppermute | solution.py:49
  130.2 10.7 %collective-permute-start.30 = (bf16[1,256,384]{2,1,0:T(8,128)(2,1)S(1)}, bf16[1,256,384]{2,1,0:T(8,128)(2,1)S(1)}, u32[]{:S(2)}, u32[]{:S(2)}) collective-permute-start(bf16[1,256,384]{2,1,0:T(8,128)(2,1)S(1)} %get-tuple-element.80), channel_id=1, source_target_pairs={{0,8},{8,0},{1,9},{9,1},{2,10},{10,2},{3,11},{11,3},{4,12},{12,4},... | collective-permute-start | bytes 589832 | tf_op jit(solution)/shard_map/ppermute | solution.py:49
  138.7 5.7 %collective-permute-start.34 = (bf16[1,256,384]{2,1,0:T(8,128)(2,1)S(1)}, bf16[1,256,384]{2,1,0:T(8,128)(2,1)S(1)}, u32[]{:S(2)}, u32[]{:S(2)}) collective-permute-start(bf16[1,256,384]{2,1,0:T(8,128)(2,1)S(1)} %get-tuple-element.84), channel_id=1, source_target_pairs={{0,1},{1,2},{2,3},{3,4},{4,5},{5,6},{6,7},{7,0},{8,9},{9,10},{10,1... | collective-permute-start | bytes 589832 | tf_op jit(solution)/shard_map/ppermute | solution.py:49
  140.8 5.7 %collective-permute-start.35 = (bf16[1,256,384]{2,1,0:T(8,128)(2,1)S(1)}, bf16[1,256,384]{2,1,0:T(8,128)(2,1)S(1)}, u32[]{:S(2)}, u32[]{:S(2)}) collective-permute-start(bf16[1,256,384]{2,1,0:T(8,128)(2,1)S(1)} %get-tuple-element.85), channel_id=1, source_target_pairs={{0,7},{1,0},{2,1},{3,2},{4,3},{5,4},{6,5},{7,6},{8,15},{9,8},{10,9... | collective-permute-start | bytes 589832 | tf_op jit(solution)/shard_map/ppermute | solution.py:49

commit v3 on v2

--- a/solution.py
+++ b/solution.py
@@ -13,7 +13,7 @@
 COL = ("x_hi", "z")
 SIZES = {"y": 4, "x_lo": 2, "core": 2, "x_hi": 2, "z": 8}
 SIDE = 128
-EARLY_CHUNKS = 10
+EARLY_CHUNKS = 14
 ORDER = (4, 3, -3, 2, -2, 1, -1, 0)
 VMEM_LIMIT = 10 * 1024 * 1024
 ON_CHIP = pl.BlockSpec(memory_space=pltpu.VMEM)
@@ -22,8 +22,10 @@
 
 
 TILES = [
-    (0, 0, 0), (0, 0, 1), (-1, 0, 0), (-1, 0, 1), (0, 1, 0), (-2, 0, 0), (1, 1, 0), (-3, 0, 0), (-1, 1, 0),
-    (0, 1, 1), (-2, 0, 1), (1, 1, 1), (-3, 0, 1), (-1, 1, 1), (2, 1, 0), (2, 1, 1),
+    (0, 0, 0), (0, 0, 1), (-1, 0, 0), (-1, 0, 1), (0, 1, 0), (-2, 0, 0),
+    (1, 1, 0), (-3, 0, 0), (-1, 1, 0),
+    (0, 1, 1), (-2, 0, 1), (1, 1, 1), (-3, 0, 1), (-1, 1, 1),
+    (2, 1, 0), (2, 1, 1),
 ]
 CHUNKS = [(hi, dz) for dz in (0, -1, 1, -2, 2, -3, 3, 4) for hi in (0, 1)]
 
@@ -61,7 +63,7 @@
     return ref[tile, slot * SIDE:(slot + 1) * SIDE]
 
 
-def load(parts, whole, sems, first=0):
+def load(parts, whole, sems, first):
     copies = []
     for number, part in enumerate(parts):
         if len(part.shape) == len(whole.shape):
@@ -74,6 +76,35 @@
     return copies
 
 
+def store_kernel(n_x, n_w, first_x, first_w, *refs):
+    x_parts, w_parts = refs[:n_x], refs[n_x:n_x + n_w]
+    x_ref, w_ref, x_sems, w_sems = refs[-4:]
+    copies = load(x_parts, x_ref, x_sems, first_x) + load(w_parts, w_ref, w_sems, first_w)
+    for copy in copies:
+        copy.wait()
+
+
+def store(x_parts, w_parts, first_x, first_w, kept=()):
+    parts = len(x_parts) + len(w_parts)
+    return pl.pallas_call(
+        functools.partial(store_kernel, len(x_parts), len(w_parts), first_x, first_w),
+        in_specs=[ANYWHERE] * parts + [ON_CHIP] * len(kept),
+        out_specs=[ON_CHIP] * 2,
+        out_shape=[
+            pltpu.VMEM((len(CHUNKS),) + x_parts[0].shape[1:], jnp.bfloat16),
+            pltpu.VMEM((len(TILES),) + w_parts[0].shape, jnp.bfloat16),
+        ],
+        input_output_aliases={parts + number: number for number in range(len(kept))},
+        scratch_shapes=[
+            pltpu.SemaphoreType.DMA((len(x_parts),)),
+            pltpu.SemaphoreType.DMA((len(w_parts),)),
+        ],
+        compiler_params=pltpu.CompilerParams(vmem_limit_bytes=VMEM_LIMIT),
+        cost_estimate=pl.CostEstimate(flops=0, bytes_accessed=4 * parts * w_parts[0].size, transcendentals=0),
+        name="store",
+    )(*x_parts, *w_parts, *kept)
+
+
 def add_tile(tile, pick, names, x_ref, w_ref, acc):
     slots = names.shape[1] // 2
     for slot in range(slots):
@@ -83,25 +114,22 @@
         acc[col] += jnp.dot(taken, slot_of(w_ref, tile, slot), preferred_element_type=jnp.float32)
 
 
-def early_kernel(n_x, n_w, pick, names, *refs):
+def early_kernel(n_x, n_w, first_x, first_w, pick, names, *refs):
     x_parts, w_parts = refs[:n_x], refs[n_x:n_x + n_w]
-    x_ref, w_ref, acc, x_sems, w_sems = refs[n_x + n_w:]
-    x_copies = load(x_parts, x_ref, x_sems)
-    w_copies = load(w_parts, w_ref, w_sems)
+    x_ref, w_ref, acc, x_sems, w_sems = refs[n_x + n_w + 2:]
+    copies = load(x_parts, x_ref, x_sems, first_x) + load(w_parts, w_ref, w_sems, first_w)
     acc[...] = jnp.zeros_like(acc)
-    for copy in x_copies:
+    for copy in copies:
         copy.wait()
 
     def tile_step(tile, carry):
-        pltpu.make_async_copy(w_parts[0], w_ref.at[tile], w_sems.at[tile]).wait()
-
         @pl.when(pick[tile] < EARLY_CHUNKS)
         def _():
             add_tile(tile, pick, names, x_ref, w_ref, acc)
 
         return carry
 
-    lax.fori_loop(0, len(w_copies), tile_step, 0)
+    lax.fori_loop(0, first_w + n_w, tile_step, 0)
 
 
 def late_kernel(n_x, n_w, pick, names, up_ref, *refs):
@@ -142,18 +170,20 @@
     )
 
 
-def forward_early(pick, names, x_parts, w_parts, col_count):
-    tokens, span = x_parts[0].shape[1:]
+def forward_early(pick, names, x_parts, w_parts, x, w, col_count):
+    tokens = x.shape[1]
     depth, pair = w_parts[0].shape
+    parts = len(x_parts) + len(w_parts)
+    first_w = len(TILES) - 2 - len(w_parts)
+    first_x = EARLY_CHUNKS - 2 * len(x_parts)
     return pl.pallas_call(
-        functools.partial(early_kernel, len(x_parts), len(w_parts)),
-        in_specs=[SCALARS] * 2 + [ANYWHERE] * (len(x_parts) + len(w_parts)),
+        functools.partial(early_kernel, len(x_parts), len(w_parts), first_x, first_w),
+        in_specs=[SCALARS] * 2 + [ANYWHERE] * parts + [ON_CHIP] * 2,
         out_specs=[ON_CHIP] * 3,
-        out_shape=[
-            pltpu.VMEM((16, tokens, span), jnp.bfloat16),
-            pltpu.VMEM((16, depth, pair), jnp.bfloat16),
+        out_shape=[pltpu.VMEM(kept.shape, kept.dtype) for kept in (x, w)] + [
             pltpu.VMEM((col_count + 1, tokens, pair), jnp.float32),
         ],
+        input_output_aliases={2 + parts: 0, 3 + parts: 1},
         scratch_shapes=[
             pltpu.SemaphoreType.DMA((len(x_parts),)),
             pltpu.SemaphoreType.DMA((len(w_parts),)),
@@ -161,7 +191,7 @@
         compiler_params=pltpu.CompilerParams(vmem_limit_bytes=VMEM_LIMIT),
         cost_estimate=pl.CostEstimate(flops=0, bytes_accessed=0, transcendentals=0),
         name="forward_early",
-    )(pick, names, *x_parts, *w_parts)
+    )(pick, names, *x_parts, *w_parts, x, w)
 
 
 def forward_late(pick, names, upstream, x_parts, w_parts, x, w, acc):
@@ -253,12 +283,18 @@
     t1 = swap(a1)
     a2, p1, m1, b1, t1 = barrier((a2, p1, m1, b1, t1))
     c1, a3, b2 = turn(b1, -1), turn(a2, 1), shift(a1, "x_lo", 1)
+    kept = store((both, p1, m1), (own, t0, a1, t1, b1, a2), 0, 0)
     p2, m2 = shift(p1, "z", 1), shift(m1, "z", -1)
-    c1, a3, b2, p2, m2, b1, a2 = barrier((c1, a3, b2, p2, m2, b1, a2))
+    p2, m2, kept = barrier((p2, m2, kept))
+    p3, m3 = shift(p2, "z", 1), shift(m2, "z", -1)
+    x, w = store((p2, m2), (c1, a3, b2), 6, 6, kept)
     c2 = turn(c1, -1)
-    p3, m3 = shift(p2, "z", 1), shift(m2, "z", -1)
+    t2, t3 = swap(b1), swap(a2)
+    p3, m3, c1, a3, b2, t2, t3 = barrier((p3, m3, c1, a3, b2, t2, t3))
+    t5, t6, t4 = swap(c1), swap(a3), swap(b2)
     p4, m4 = shift(p3[0], "z", 1), shift(m3[1], "z", -1)
-    return (own, t0, a1, t1, b1, a2, c1, a3, b2), c2, (both, p1, m1, p2, m2), (p3, m3, p4, m4)
+    known = (own, t0, a1, t1, b1, a2, c1, a3, b2, t2, t3, t5, t6, t4)
+    return x, w, (p3, m3), (t2, t3, t5, t6, t4), (p4, m4), c2, known
 
 
 def on_device(tokens, gate_blocks, up_blocks, block_row, block_col, upstream):
@@ -273,7 +309,7 @@
     ]).astype(bf16)
     ids = jnp.broadcast_to(jnp.pad(ids, (0, 2 * SIDE - 2 * slots))[None], (16, 2 * SIDE))
     blocks = jnp.concatenate([gate_blocks, up_blocks], axis=2).reshape(slots * SIDE, 2 * SIDE)
-    w_early, c2, x_early, x_late = gather(jnp.concatenate([blocks, ids]), tokens)
+    x, w, x_early, w_early, x_late, c2, known = gather(jnp.concatenate([blocks, ids]), tokens)
 
     line = lax.broadcasted_iota(i32, (16, 2 * slots), 0)
 
@@ -284,10 +320,10 @@
             names = jnp.where(line == place, name, names)
         return names.astype(i32)
 
-    x, w, acc = forward_early(pick, names_of(w_early), x_early, w_early, upstream.shape[1] // SIDE)
-    moved, acc = lax.optimization_barrier((w_early[4:], acc))
-    w_late = [shift(part, "core", 1) for part in moved] + [c2, shift(c2, "core", 1)]
-    names = names_of(w_early + tuple(w_late))
+    x, w, acc = forward_early(pick, names_of(known), x_early, w_early, x, w, upstream.shape[1] // SIDE)
+    c2, acc, x_late = lax.optimization_barrier((c2, acc, x_late))
+    w_late = (c2, shift(c2, "core", 1))
+    names = names_of(known + w_late)
     hidden, grads, w = forward_late(pick, names, upstream, x_late, w_late, x, w, acc)
 
     def share(jobs, added):

time: 150 us -> 141 us (0.940)
  starting transfers between devices: 52.5 us -> 44.8 us
    pallas_call x1, Pallas kernels: 12.5 us -> 5.8 us  [forward_late(): pl.pallas_call(functools.partial(late_kernel, len(x_parts), len(w_parts))...]
    ppermute x5, starting transfers between devices: 8.57 us -> 3.52 us  [turn(): return lax.ppermute(value, ('y', 'core'), pairs)]
    pallas_call x0 -> x2, Pallas kernels: none -> 3.77 us  [store(): pl.pallas_call(functools.partial(store_kernel, len(x_parts), len(w_parts)...]
    pallas_call x1, Pallas kernels: 7.24 us -> 9.94 us  [forward_early(): pl.pallas_call(functools.partial(early_kernel, len(x_parts), len(w_parts)...]
    ppermute x31, starting transfers between devices: 44 us -> 41.3 us  [shift(): lax.ppermute(value, axis, [(i, (i + step) % size) for i in range(size)])]
    ppermute x5, waiting for transfers between devices: 5.6 us -> 3.04 us  [turn(): return lax.ppermute(value, ('y', 'core'), pairs)]
  transfers between devices with their start and end apart: 36 -> 36, of which waited for: 18 -> 18; matrix products, arithmetic and copies ran while one was open for 0% -> 1% of each run, Pallas kernels for 11% -> 16%
where the time goes in v3:
time: 141 us; the launch traced here: 140 us
  waiting for transfers between devices  58 us (41%)
  starting transfers between devices  44.8 us (32%)
  Pallas kernels  32.3 us (23%)
  other arithmetic  3.25 us (2%)
    ppermute x31, waiting for transfers between devices, shift(): lax.ppermute(value, axis, [(i, (i + step) % size) for i in range(size)])  55 us
    ppermute x31, starting transfers between devices, shift(): lax.ppermute(value, axis, [(i, (i + step) % size) for i in range(size)])  41.3 us
    pallas_call x6, Pallas kernels, backward(): pl.pallas_call(functools.partial(backward_kernel, jobs), in_specs=[SCALAR...  12.8 us
    pallas_call x1, Pallas kernels, forward_early(): pl.pallas_call(functools.partial(early_kernel, len(x_parts), len(w_parts)...  9.94 us
    pallas_call x1, Pallas kernels, forward_late(): pl.pallas_call(functools.partial(late_kernel, len(x_parts), len(w_parts))...  5.8 us
    pallas_call x2, Pallas kernels, store(): pl.pallas_call(functools.partial(store_kernel, len(x_parts), len(w_parts)...  3.77 us
    ppermute x5, starting transfers between devices, turn(): return lax.ppermute(value, ('y', 'core'), pairs)  3.52 us
    ppermute x5, waiting for transfers between devices, turn(): return lax.ppermute(value, ('y', 'core'), pairs)  3.04 us
  transfers between devices with their start and end apart: 36, of which 18 were waited for; matrix products, arithmetic and copies ran while one was open for 1% of the time, Pallas kernels for 16%

profile of v3, /device:TPU:32, one launch (start us, length us, event | category | flops | bytes accessed | tf_op | source)
XLA Modules:
  0.0 140.2 jit_solution(10113289954793888353)
XLA Ops:
  0.6 0.7 dynamic-slice_bitcast_fusion
  1.3 0.7 fusion.6
  2.0 0.1 fusion.8
  2.1 1.2 pad_maximum_fusion.1
  3.4 0.1 collective-permute-start.5
  3.5 1.7 %collective-permute-start = (bf16[1424,256]{1,0:T(8,128)(2,1)S(1)}, bf16[1424,256]{1,0:T(8,128)(2,1)S(1)}, u32[]{:S(2)}, u32[]{:S(2)}) collective-permute-start(bf16[1424,256]{1,0:T(8,128)(2,1)S(1)} %pad_maximum_fusion.refs_3_), channel_id=1, source_target_pairs={{0,64},{16,208},{64,128},{80,16},{128,192},{144,80},{192,0},{208,1... | collective-permute-start | bytes 2187272 | tf_op jit(solution)/shard_map/ppermute | solution.py:59
  5.1 3.0 %collective-permute-start.1 = (bf16[256,384]{1,0:T(8,128)(2,1)}, bf16[256,384]{1,0:T(8,128)(2,1)S(1)}, u32[]{:S(2)}, u32[]{:S(2)}) collective-permute-start(bf16[256,384]{1,0:T(8,128)(2,1)} %param.7), channel_id=1, source_target_pairs={{0,8},{8,0},{1,9},{9,1},{2,10},{10,2},{3,11},{11,3},{4,12},{12,4},... | collective-permute-start | bytes 589832 | tf_op jit(solution)/shard_map/ppermute | solution.py:51
  8.2 0.6 collective-permute-start.6
  8.7 5.3 %collective-permute-done.1 = bf16[256,384]{1,0:T(8,128)(2,1)S(1)} collective-permute-done((bf16[256,384]{1,0:T(8,128)(2,1)}, bf16[256,384]{1,0:T(8,128)(2,1)S(1)}, u32[]{:S(2)}, u32[]{:S(2)}) %collective-permute-start.1) | collective-permute-done | bytes 196640 | tf_op jit(solution)/shard_map/ppermute | solution.py:51
  14.1 2.1 %collective-permute-done.refs_5_ = bf16[1424,256]{1,0:T(8,128)(2,1)S(1)} collective-permute-done((bf16[1424,256]{1,0:T(8,128)(2,1)S(1)}, bf16[1424,256]{1,0:T(8,128)(2,1)S(1)}, u32[]{:S(2)}, u32[]{:S(2)}) %collective-permute-start) | collective-permute-done | bytes 729120 | tf_op jit(solution)/shard_map/ppermute | solution.py:59
  16.1 0.4 collective-permute-start.2
  16.5 1.0 pad_maximum_fusion.2.refs_0_
  17.5 1.6 %collective-permute-start.4 = (bf16[2,256,384]{2,1,0:T(8,128)(2,1)S(1)}, bf16[2,256,384]{2,1,0:T(8,128)(2,1)S(1)}, u32[]{:S(2)}, u32[]{:S(2)}) collective-permute-start(bf16[2,256,384]{2,1,0:T(8,128)(2,1)S(1)} %pad_maximum_fusion.2.refs_0_), channel_id=1, source_target_pairs={{0,7},{1,0},{2,1},{3,2},{4,3},{5,4},{6,5},{7,6},{8,15},{9,8},{10,9... | collective-permute-start | bytes 1179656 | tf_op jit(solution)/shard_map/ppermute | solution.py:51
  19.0 0.5 collective-permute-start.3
  19.6 9.1 %collective-permute-done.4.refs_2_ = bf16[2,256,384]{2,1,0:T(8,128)(2,1)S(1)} collective-permute-done((bf16[2,256,384]{2,1,0:T(8,128)(2,1)S(1)}, bf16[2,256,384]{2,1,0:T(8,128)(2,1)S(1)}, u32[]{:S(2)}, u32[]{:S(2)}) %collective-permute-start.4) | collective-permute-done | bytes 393248 | tf_op jit(solution)/shard_map/ppermute | solution.py:51
  28.7 4.1 %collective-permute-done.3.refs_1_ = bf16[2,256,384]{2,1,0:T(8,128)(2,1)S(1)} collective-permute-done((bf16[2,256,384]{2,1,0:T(8,128)(2,1)S(1)}, bf16[2,256,384]{2,1,0:T(8,128)(2,1)S(1)}, u32[]{:S(2)}, u32[]{:S(2)}) %collective-permute-start.3) | collective-permute-done | bytes 393248 | tf_op jit(solution)/shard_map/ppermute | solution.py:51
  32.9 0.1 collective-permute-start.10
  32.9 3.6 %collective-permute-start.11 = (bf16[2,256,384]{2,1,0:T(8,128)(2,1)S(1)}, bf16[2,256,384]{2,1,0:T(8,128)(2,1)S(1)}, u32[]{:S(2)}, u32[]{:S(2)}) collective-permute-start(bf16[2,256,384]{2,1,0:T(8,128)(2,1)S(1)} %collective-permute-done.4.refs_2_), channel_id=1, source_target_pairs={{0,7},{1,0},{2,1},{3,2},{4,3},{5,4},{6,5},{7,6},{8,15},{9,8},{10,9... | collective-permute-start | bytes 1179656 | tf_op jit(solution)/shard_map/ppermute | solution.py:51
  36.6 1.5 %collective-permute-start.15 = (bf16[1424,256]{1,0:T(8,128)(2,1)S(1)}, bf16[1424,256]{1,0:T(8,128)(2,1)S(1)}, u32[]{:S(2)}, u32[]{:S(2)}) collective-permute-start(bf16[1424,256]{1,0:T(8,128)(2,1)S(1)} %collective-permute-done.refs_5_), channel_id=1, source_target_pairs={{0,32},{32,0},{1,33},{33,1},{2,34},{34,2},{3,35},{35,3},{4,36},{36... | collective-permute-start | bytes 2187272 | tf_op jit(solution)/shard_map/ppermute | solution.py:51
  38.1 1.5 %collective-permute-start.8 = (bf16[1424,256]{1,0:T(8,128)(2,1)S(1)}, bf16[1424,256]{1,0:T(8,128)(2,1)S(1)}, u32[]{:S(2)}, u32[]{:S(2)}) collective-permute-start(bf16[1424,256]{1,0:T(8,128)(2,1)S(1)} %collective-permute-done.6.refs_7_), channel_id=1, source_target_pairs={{0,192},{16,80},{64,0},{80,144},{128,64},{144,208},{192,128},{208,... | collective-permute-start | bytes 2187272 | tf_op jit(solution)/shard_map/ppermute | solution.py:59
  39.7 6.2 %collective-permute-done.10.refs_0_ = bf16[2,256,384]{2,1,0:T(8,128)(2,1)S(1)} collective-permute-done((bf16[2,256,384]{2,1,0:T(8,128)(2,1)S(1)}, bf16[2,256,384]{2,1,0:T(8,128)(2,1)S(1)}, u32[]{:S(2)}, u32[]{:S(2)}) %collective-permute-start.10) | collective-permute-done | bytes 393248 | tf_op jit(solution)/shard_map/ppermute | solution.py:51
  46.0 2.5 %store.2 = (bf16[16,256,384]{2,1,0:T(8,128)(2,1)S(1)}, bf16[16,1424,256]{2,1,0:T(8,128)(2,1)S(1)}) custom-call(bf16[2,256,384]{2,1,0:T(8,128)(2,1)S(1)} %pad_maximum_fusion.2.refs_0_, bf16[2,256,384]{2,1,0:T(8,128)(2,1)S(1)} %collective-permute-done.3.refs_1_, bf16[2,256,384]{2,1,0:T(8,128)(2,1)S(1)} %collective-permute-done.4.refs_2_, ...), custom_call_target="tpu_custom_call" | custom-call | bytes 13123584 | tf_op jit(solution)/shard_map/store/pallas_call | solution.py:89
  48.4 6.3 %collective-permute-done.15.refs_4_ = bf16[1424,256]{1,0:T(8,128)(2,1)S(1)} collective-permute-done((bf16[1424,256]{1,0:T(8,128)(2,1)S(1)}, bf16[1424,256]{1,0:T(8,128)(2,1)S(1)}, u32[]{:S(2)}, u32[]{:S(2)}) %collective-permute-start.15) | collective-permute-done | bytes 729120 | tf_op jit(solution)/shard_map/ppermute | solution.py:51
  54.7 2.9 %collective-permute-start.13 = (bf16[2,256,384]{2,1,0:T(8,128)(2,1)S(1)}, bf16[2,256,384]{2,1,0:T(8,128)(2,1)S(1)}, u32[]{:S(2)}, u32[]{:S(2)}) collective-permute-start(bf16[2,256,384]{2,1,0:T(8,128)(2,1)S(1)} %collective-permute-done.11.refs_1_), channel_id=1, source_target_pairs={{0,7},{1,0},{2,1},{3,2},{4,3},{5,4},{6,5},{7,6},{8,15},{9,8},{10,9... | collective-permute-start | bytes 1179656 | tf_op jit(solution)/shard_map/ppermute | solution.py:51
  57.6 1.0 collective-permute-done.14.refs_3_
  58.5 1.3 store.3
  59.9 5.6 %collective-permute-done.12.refs_0_ = bf16[2,256,384]{2,1,0:T(8,128)(2,1)S(1)} collective-permute-done((bf16[2,256,384]{2,1,0:T(8,128)(2,1)S(1)}, bf16[2,256,384]{2,1,0:T(8,128)(2,1)S(1)}, u32[]{:S(2)}, u32[]{:S(2)}) %collective-permute-start.12) | collective-permute-done | bytes 393248 | tf_op jit(solution)/shard_map/ppermute | solution.py:51
  65.5 0.1 collective-permute-start.18
  65.6 0.5 collective-permute-start.19
  66.1 0.1 collective-permute-start.20
  66.2 3.0 %collective-permute-start.22 = (bf16[256,384]{1,0:T(8,128)(2,1)S(1)}, bf16[256,384]{1,0:T(8,128)(2,1)S(1)}, u32[]{:S(2)}, u32[]{:S(2)}) collective-permute-start(bf16[256,384]{1,0:T(8,128)(2,1)S(1)} %slice_bitcast_fusion), channel_id=1, source_target_pairs={{0,7},{1,0},{2,1},{3,2},{4,3},{5,4},{6,5},{7,6},{8,15},{9,8},{10,9... | collective-permute-start | bytes 589832 | tf_op jit(solution)/shard_map/ppermute | solution.py:51
  69.3 0.1 collective-permute-start.21
  69.4 0.5 collective-permute-done.20.refs_4_
  69.9 0.1 fusion.names
  70.0 9.9 %forward_early.1 = (bf16[16,256,384]{2,1,0:T(8,128)(2,1)S(1)}, bf16[16,1424,256]{2,1,0:T(8,128)(2,1)S(1)}, f32[13,256,256]{2,1,0:T(8,128)S(1)}) custom-call(s32[16]{0:T(128)S(1)} %get-tuple-element.101.pick, s32[16,22]{1,0:T(8,128)S(1)} %fusion.names, ...), custom_call_target="tpu_custom_call", output_to_operand_aliasing={{0}: (9, {}), {1}: (10, {})} | custom-call | tf_op jit(solution)/shard_map/forward_early/pallas_call | solution.py:179
  80.0 0.2 collective-permute-start.23
  80.3 2.0 %collective-permute-done.23.refs_3_ = bf16[1424,256]{1,0:T(8,128)(2,1)S(1)} collective-permute-done((bf16[1424,256]{1,0:T(8,128)(2,1)S(1)}, bf16[1424,256]{1,0:T(8,128)(2,1)S(1)}, u32[]{:S(2)}, u32[]{:S(2)}) %collective-permute-start.23) | collective-permute-done | bytes 729120 | tf_op jit(solution)/shard_map/ppermute | solution.py:51
  82.3 0.1 select_convert_fusion.names
  82.4 5.8 %forward_late.1 = (bf16[256,1536]{1,0:T(8,128)(2,1)}, bf16[12,256,256]{2,1,0:T(8,128)(2,1)S(1)}, bf16[16,256,384]{2,1,0:T(8,128)(2,1)S(1)}, bf16[16,1424,256]{2,1,0:T(8,128)(2,1)S(1)}, f32[13,256,256]{2,1,0:T(8,128)S(1)}) custom-call(s32[16]{0:T(128)S(1)} %get-tuple-element.101.pick, ...), custom_call_target="tpu_custom_call", output_to_operand_aliasing={{2}: (7, {}), {3}: (8, {}), {4}: (9, {})} | custom-call | flops 738197504 | bytes 3932160 | tf_op jit(solution)/shard_map/forward_late/pallas_call | solution.py:201
  88.2 2.2 %backward.6 = (bf16[1,256,384]{2,1,0:T(8,128)(2,1)S(1)}, bf16[2,256,384]{2,1,0:T(8,128)(2,1)S(1)}) custom-call(s32[16]{0:T(128)S(1)} %get-tuple-element.100.places, s32[16,22]{1,0:T(8,128)S(1)} %select_convert_fusion.names, bf16[12,256,256]{2,1,0:T(8,128)(2,1)S(1)} %get-tuple-element.84.grads_ref, bf16[16,1424,256]{2,1,0:T(8,128)(2,1)S(1)} %get-tuple-element.85.w_ref), custom_call_target="tpu_custom_call" | custom-call | flops 553648128 | bytes 2187264 | tf_op jit(solution)/shard_map/backward/pallas_call | solution.py:255
  90.4 3.1 %collective-permute-start.24 = (bf16[1,256,384]{2,1,0:T(8,128)(2,1)S(1)}, bf16[1,256,384]{2,1,0:T(8,128)(2,1)S(1)}, u32[]{:S(2)}, u32[]{:S(2)}) collective-permute-start(bf16[1,256,384]{2,1,0:T(8,128)(2,1)S(1)} %get-tuple-element.86), channel_id=1, source_target_pairs={{0,8},{8,0},{1,9},{9,1},{2,10},{10,2},{3,11},{11,3},{4,12},{12,4},... | collective-permute-start | bytes 589832 | tf_op jit(solution)/shard_map/ppermute | solution.py:51
  93.5 0.5 collective-permute-start.26
  94.0 5.7 %collective-permute-done.24.refs_0_ = bf16[1,256,384]{2,1,0:T(8,128)(2,1)S(1)} collective-permute-done((bf16[1,256,384]{2,1,0:T(8,128)(2,1)S(1)}, bf16[1,256,384]{2,1,0:T(8,128)(2,1)S(1)}, u32[]{:S(2)}, u32[]{:S(2)}) %collective-permute-start.24) | collective-permute-done | bytes 196640 | tf_op jit(solution)/shard_map/ppermute | solution.py:51
  99.8 2.1 %backward.7 = (bf16[1,256,384]{2,1,0:T(8,128)(2,1)S(1)}, bf16[2,256,384]{2,1,0:T(8,128)(2,1)S(1)}) custom-call(s32[16]{0:T(128)S(1)} %get-tuple-element.100.places, s32[16,22]{1,0:T(8,128)S(1)} %select_convert_fusion.names, bf16[12,256,256]{2,1,0:T(8,128)(2,1)S(1)} %get-tuple-element.84.grads_ref, bf16[16,1424,256]{2,1,0:T(8,128)(2,1)S(1)} %get-tuple-element.85.w_ref, ...), custom_call_target="tpu_custom_call" | custom-call | flops 553648128 | bytes 2187264 | tf_op jit(solution)/shard_map/backward/pallas_call | solution.py:255
  101.9 2.1 %collective-permute-start.27 = (bf16[1,256,384]{2,1,0:T(8,128)(2,1)S(1)}, bf16[1,256,384]{2,1,0:T(8,128)(2,1)S(1)}, u32[]{:S(2)}, u32[]{:S(2)}) collective-permute-start(bf16[1,256,384]{2,1,0:T(8,128)(2,1)S(1)} %get-tuple-element.89), channel_id=1, source_target_pairs={{0,1},{1,2},{2,3},{3,4},{4,5},{5,6},{6,7},{7,0},{8,9},{9,10},{10,1... | collective-permute-start | bytes 589832 | tf_op jit(solution)/shard_map/ppermute | solution.py:51
  104.0 3.0 %collective-permute-start.25 = (bf16[2,256,384]{2,1,0:T(8,128)(2,1)S(1)}, bf16[2,256,384]{2,1,0:T(8,128)(2,1)S(1)}, u32[]{:S(2)}, u32[]{:S(2)}) collective-permute-start(bf16[2,256,384]{2,1,0:T(8,128)(2,1)S(1)} %get-tuple-element.87), channel_id=1, source_target_pairs={{0,8},{8,0},{1,9},{9,1},{2,10},{10,2},{3,11},{11,3},{4,12},{12,4},... | collective-permute-start | bytes 1179656 | tf_op jit(solution)/shard_map/ppermute | solution.py:51
  107.1 1.5 %collective-permute-done.27.refs_1_ = bf16[1,256,384]{2,1,0:T(8,128)(2,1)S(1)} collective-permute-done((bf16[1,256,384]{2,1,0:T(8,128)(2,1)S(1)}, bf16[1,256,384]{2,1,0:T(8,128)(2,1)S(1)}, u32[]{:S(2)}, u32[]{:S(2)}) %collective-permute-start.27) | collective-permute-done | bytes 196640 | tf_op jit(solution)/shard_map/ppermute | solution.py:51
  108.6 2.6 %backward.8 = (bf16[1,256,384]{2,1,0:T(8,128)(2,1)S(1)}, bf16[1,256,384]{2,1,0:T(8,128)(2,1)S(1)}, bf16[2,256,384]{2,1,0:T(8,128)(2,1)S(1)}) custom-call(s32[16]{0:T(128)S(1)} %get-tuple-element.100.places, s32[16,22]{1,0:T(8,128)S(1)} %select_convert_fusion.names, bf16[12,256,256]{2,1,0:T(8,128)(2,1)S(1)} %get-tuple-element.84.grads_ref, ...), custom_call_target="tpu_custom_call" | custom-call | flops 738197504 | bytes 2916352 | tf_op jit(solution)/shard_map/backward/pallas_call | solution.py:255
  111.2 1.7 %collective-permute-start.28 = (bf16[1,256,384]{2,1,0:T(8,128)(2,1)S(1)}, bf16[1,256,384]{2,1,0:T(8,128)(2,1)S(1)}, u32[]{:S(2)}, u32[]{:S(2)}) collective-permute-start(bf16[1,256,384]{2,1,0:T(8,128)(2,1)S(1)} %get-tuple-element.90), channel_id=1, source_target_pairs={{0,1},{1,2},{2,3},{3,4},{4,5},{5,6},{6,7},{7,0},{8,9},{9,10},{10,1... | collective-permute-start | bytes 589832 | tf_op jit(solution)/shard_map/ppermute | solution.py:51
  112.9 1.7 %collective-permute-start.29 = (bf16[1,256,384]{2,1,0:T(8,128)(2,1)S(1)}, bf16[1,256,384]{2,1,0:T(8,128)(2,1)S(1)}, u32[]{:S(2)}, u32[]{:S(2)}) collective-permute-start(bf16[1,256,384]{2,1,0:T(8,128)(2,1)S(1)} %get-tuple-element.91), channel_id=1, source_target_pairs={{0,7},{1,0},{2,1},{3,2},{4,3},{5,4},{6,5},{7,6},{8,15},{9,8},{10,9... | collective-permute-start | bytes 589832 | tf_op jit(solution)/shard_map/ppermute | solution.py:51
  114.6 3.0 %collective-permute-start.31 = (bf16[2,256,384]{2,1,0:T(8,128)(2,1)S(1)}, bf16[2,256,384]{2,1,0:T(8,128)(2,1)S(1)}, u32[]{:S(2)}, u32[]{:S(2)}) collective-permute-start(bf16[2,256,384]{2,1,0:T(8,128)(2,1)S(1)} %get-tuple-element.93), channel_id=1, source_target_pairs={{0,8},{8,0},{1,9},{9,1},{2,10},{10,2},{3,11},{11,3},{4,12},{12,4},... | collective-permute-start | bytes 1179656 | tf_op jit(solution)/shard_map/ppermute | solution.py:51
  117.6 0.5 collective-permute-done.28.refs_1_
  118.2 0.4 collective-permute-done.29.refs_2_
  118.6 2.2 %backward.9 = (bf16[1,256,384]{2,1,0:T(8,128)(2,1)S(1)}, bf16[1,256,384]{2,1,0:T(8,128)(2,1)S(1)}, bf16[1,256,384]{2,1,0:T(8,128)(2,1)S(1)}) custom-call(s32[16]{0:T(128)S(1)} %get-tuple-element.100.places, s32[16,22]{1,0:T(8,128)S(1)} %select_convert_fusion.names, bf16[12,256,256]{2,1,0:T(8,128)(2,1)S(1)} %get-tuple-element.84.grads_ref, ...), custom_call_target="tpu_custom_call" | custom-call | flops 553648128 | bytes 2187264 | tf_op jit(solution)/shard_map/backward/pallas_call | solution.py:255
  120.8 2.1 %collective-permute-start.32 = (bf16[1,256,384]{2,1,0:T(8,128)(2,1)S(1)}, bf16[1,256,384]{2,1,0:T(8,128)(2,1)S(1)}, u32[]{:S(2)}, u32[]{:S(2)}) collective-permute-start(bf16[1,256,384]{2,1,0:T(8,128)(2,1)S(1)} %get-tuple-element.94), channel_id=1, source_target_pairs={{0,1},{1,2},{2,3},{3,4},{4,5},{5,6},{6,7},{7,0},{8,9},{9,10},{10,1... | collective-permute-start | bytes 589832 | tf_op jit(solution)/shard_map/ppermute | solution.py:51
  122.9 0.9 collective-permute-start.33
  123.8 3.0 %collective-permute-start.30 = (bf16[1,256,384]{2,1,0:T(8,128)(2,1)S(1)}, bf16[1,256,384]{2,1,0:T(8,128)(2,1)S(1)}, u32[]{:S(2)}, u32[]{:S(2)}) collective-permute-start(bf16[1,256,384]{2,1,0:T(8,128)(2,1)S(1)} %get-tuple-element.92), channel_id=1, source_target_pairs={{0,8},{8,0},{1,9},{9,1},{2,10},{10,2},{3,11},{11,3},{4,12},{12,4},... | collective-permute-start | bytes 589832 | tf_op jit(solution)/shard_map/ppermute | solution.py:51
  126.8 0.5 collective-permute-done.32.refs_1_
  127.3 1.4 collective-permute-done.33.refs_2_
  128.7 1.7 %backward.10 = (bf16[1,256,384]{2,1,0:T(8,128)(2,1)S(1)}, bf16[1,256,384]{2,1,0:T(8,128)(2,1)S(1)}) custom-call(s32[16]{0:T(128)S(1)} %get-tuple-element.100.places, s32[16,22]{1,0:T(8,128)S(1)} %select_convert_fusion.names, bf16[12,256,256]{2,1,0:T(8,128)(2,1)S(1)} %get-tuple-element.84.grads_ref, bf16[16,1424,256]{2,1,0:T(8,128)(2,1)S(1)} %get-tuple-element.85.w_ref, ...), custom_call_target="tpu_custom_call" | custom-call | flops 369098752 | bytes 1458176 | tf_op jit(solution)/shard_map/backward/pallas_call | solution.py:255
  130.5 2.1 %collective-permute-start.34 = (bf16[1,256,384]{2,1,0:T(8,128)(2,1)S(1)}, bf16[1,256,384]{2,1,0:T(8,128)(2,1)S(1)}, u32[]{:S(2)}, u32[]{:S(2)}) collective-permute-start(bf16[1,256,384]{2,1,0:T(8,128)(2,1)S(1)} %get-tuple-element.96), channel_id=1, source_target_pairs={{0,1},{1,2},{2,3},{3,4},{4,5},{5,6},{6,7},{7,0},{8,9},{9,10},{10,1... | collective-permute-start | bytes 589832 | tf_op jit(solution)/shard_map/ppermute | solution.py:51
  132.6 3.6 %collective-permute-done.34.refs_1_ = bf16[1,256,384]{2,1,0:T(8,128)(2,1)S(1)} collective-permute-done((bf16[1,256,384]{2,1,0:T(8,128)(2,1)S(1)}, bf16[1,256,384]{2,1,0:T(8,128)(2,1)S(1)}, u32[]{:S(2)}, u32[]{:S(2)}) %collective-permute-start.34) | collective-permute-done | bytes 196640 | tf_op jit(solution)/shard_map/ppermute | solution.py:51
  136.2 2.0 %collective-permute-done.35.refs_2_ = bf16[1,256,384]{2,1,0:T(8,128)(2,1)S(1)} collective-permute-done((bf16[1,256,384]{2,1,0:T(8,128)(2,1)S(1)}, bf16[1,256,384]{2,1,0:T(8,128)(2,1)S(1)}, u32[]{:S(2)}, u32[]{:S(2)}) %collective-permute-start.35) | collective-permute-done | bytes 196640 | tf_op jit(solution)/shard_map/ppermute | solution.py:51
  138.2 2.0 %backward.11 = bf16[1,256,384]{2,1,0:T(8,128)(2,1)} custom-call(s32[16]{0:T(128)S(1)} %get-tuple-element.100.places, s32[16,22]{1,0:T(8,128)S(1)} %select_convert_fusion.names, bf16[12,256,256]{2,1,0:T(8,128)(2,1)S(1)} %get-tuple-element.84.grads_ref, bf16[16,1424,256]{2,1,0:T(8,128)(2,1)S(1)} %get-tuple-element.85.w_ref, ...), custom_call_target="tpu_custom_call" | custom-call | flops 184549376 | bytes 729088 | tf_op jit(solution)/shard_map/backward/pallas_call | solution.py:255
  (53 shorter events, 0.4 us)
Async XLA Ops:
  3.4 4.8 %collective-permute-start.5 = (bf16[1424,256]{1,0:T(8,128)(2,1)S(1)}, bf16[1424,256]{1,0:T(8,128)(2,1)S(1)}, u32[]{:S(2)}, u32[]{:S(2)}) collective-permute-start(bf16[1424,256]{1,0:T(8,128)(2,1)S(1)} %pad_maximum_fusion.refs_3_), channel_id=1, source_target_pairs={{0,16},{16,0},{1,17},{17,1},{2,18},{18,2},{3,19},{19,3},{4,20},{20... | collective-permute-start | bytes 2187272 | tf_op jit(solution)/shard_map/ppermute | solution.py:51
  3.5 12.7 %collective-permute-start = (bf16[1424,256]{1,0:T(8,128)(2,1)S(1)}, bf16[1424,256]{1,0:T(8,128)(2,1)S(1)}, u32[]{:S(2)}, u32[]{:S(2)}) collective-permute-start(bf16[1424,256]{1,0:T(8,128)(2,1)S(1)} %pad_maximum_fusion.refs_3_), channel_id=1, source_target_pairs={{0,64},{16,208},{64,128},{80,16},{128,192},{144,80},{192,0},{208,1... | collective-permute-start | bytes 2187272 | tf_op jit(solution)/shard_map/ppermute | solution.py:59
  5.1 8.9 %collective-permute-start.1 = (bf16[256,384]{1,0:T(8,128)(2,1)}, bf16[256,384]{1,0:T(8,128)(2,1)S(1)}, u32[]{:S(2)}, u32[]{:S(2)}) collective-permute-start(bf16[256,384]{1,0:T(8,128)(2,1)} %param.7), channel_id=1, source_target_pairs={{0,8},{8,0},{1,9},{9,1},{2,10},{10,2},{3,11},{11,3},{4,12},{12,4},... | collective-permute-start | bytes 589832 | tf_op jit(solution)/shard_map/ppermute | solution.py:51
  8.2 24.7 %collective-permute-start.6 = (bf16[1424,256]{1,0:T(8,128)(2,1)S(1)}, bf16[1424,256]{1,0:T(8,128)(2,1)S(1)}, u32[]{:S(2)}, u32[]{:S(2)}) collective-permute-start(bf16[1424,256]{1,0:T(8,128)(2,1)S(1)} %pad_maximum_fusion.refs_3_), channel_id=1, source_target_pairs={{0,32},{32,0},{1,33},{33,1},{2,34},{34,2},{3,35},{35,3},{4,36},{36... | collective-permute-start | bytes 2187272 | tf_op jit(solution)/shard_map/ppermute | solution.py:51
  16.1 16.7 %collective-permute-start.7 = (bf16[1424,256]{1,0:T(8,128)(2,1)S(1)}, bf16[1424,256]{1,0:T(8,128)(2,1)S(1)}, u32[]{:S(2)}, u32[]{:S(2)}) collective-permute-start(bf16[1424,256]{1,0:T(8,128)(2,1)S(1)} %collective-permute-done.refs_5_), channel_id=1, source_target_pairs={{0,16},{16,0},{1,17},{17,1},{2,18},{18,2},{3,19},{19,3},{4,20},{20... | collective-permute-start | bytes 2187272 | tf_op jit(solution)/shard_map/ppermute | solution.py:51
  16.1 16.7 %collective-permute-start.2 = (bf16[1424,256]{1,0:T(8,128)(2,1)S(1)}, bf16[1424,256]{1,0:T(8,128)(2,1)S(1)}, u32[]{:S(2)}, u32[]{:S(2)}) collective-permute-start(bf16[1424,256]{1,0:T(8,128)(2,1)S(1)} %collective-permute-done.refs_5_), channel_id=1, source_target_pairs={{0,64},{16,208},{64,128},{80,16},{128,192},{144,80},{192,0},{208,1... | collective-permute-start | bytes 2187272 | tf_op jit(solution)/shard_map/ppermute | solution.py:59
  17.5 11.2 %collective-permute-start.4 = (bf16[2,256,384]{2,1,0:T(8,128)(2,1)S(1)}, bf16[2,256,384]{2,1,0:T(8,128)(2,1)S(1)}, u32[]{:S(2)}, u32[]{:S(2)}) collective-permute-start(bf16[2,256,384]{2,1,0:T(8,128)(2,1)S(1)} %pad_maximum_fusion.2.refs_0_), channel_id=1, source_target_pairs={{0,7},{1,0},{2,1},{3,2},{4,3},{5,4},{6,5},{7,6},{8,15},{9,8},{10,9... | collective-permute-start | bytes 1179656 | tf_op jit(solution)/shard_map/ppermute | solution.py:51
  19.0 13.8 %collective-permute-start.3 = (bf16[2,256,384]{2,1,0:T(8,128)(2,1)S(1)}, bf16[2,256,384]{2,1,0:T(8,128)(2,1)S(1)}, u32[]{:S(2)}, u32[]{:S(2)}) collective-permute-start(bf16[2,256,384]{2,1,0:T(8,128)(2,1)S(1)} %pad_maximum_fusion.2.refs_0_), channel_id=1, source_target_pairs={{0,1},{1,2},{2,3},{3,4},{4,5},{5,6},{6,7},{7,0},{8,9},{9,10},{10,1... | collective-permute-start | bytes 1179656 | tf_op jit(solution)/shard_map/ppermute | solution.py:51
  32.9 13.1 %collective-permute-start.10 = (bf16[2,256,384]{2,1,0:T(8,128)(2,1)S(1)}, bf16[2,256,384]{2,1,0:T(8,128)(2,1)S(1)}, u32[]{:S(2)}, u32[]{:S(2)}) collective-permute-start(bf16[2,256,384]{2,1,0:T(8,128)(2,1)S(1)} %collective-permute-done.3.refs_1_), channel_id=1, source_target_pairs={{0,1},{1,2},{2,3},{3,4},{4,5},{5,6},{6,7},{7,0},{8,9},{9,10},{10,1... | collective-permute-start | bytes 1179656 | tf_op jit(solution)/shard_map/ppermute | solution.py:51
  32.9 13.0 %collective-permute-start.11 = (bf16[2,256,384]{2,1,0:T(8,128)(2,1)S(1)}, bf16[2,256,384]{2,1,0:T(8,128)(2,1)S(1)}, u32[]{:S(2)}, u32[]{:S(2)}) collective-permute-start(bf16[2,256,384]{2,1,0:T(8,128)(2,1)S(1)} %collective-permute-done.4.refs_2_), channel_id=1, source_target_pairs={{0,7},{1,0},{2,1},{3,2},{4,3},{5,4},{6,5},{7,6},{8,15},{9,8},{10,9... | collective-permute-start | bytes 1179656 | tf_op jit(solution)/shard_map/ppermute | solution.py:51
  36.6 18.1 %collective-permute-start.15 = (bf16[1424,256]{1,0:T(8,128)(2,1)S(1)}, bf16[1424,256]{1,0:T(8,128)(2,1)S(1)}, u32[]{:S(2)}, u32[]{:S(2)}) collective-permute-start(bf16[1424,256]{1,0:T(8,128)(2,1)S(1)} %collective-permute-done.refs_5_), channel_id=1, source_target_pairs={{0,32},{32,0},{1,33},{33,1},{2,34},{34,2},{3,35},{35,3},{4,36},{36... | collective-permute-start | bytes 2187272 | tf_op jit(solution)/shard_map/ppermute | solution.py:51
  38.1 16.6 %collective-permute-start.8 = (bf16[1424,256]{1,0:T(8,128)(2,1)S(1)}, bf16[1424,256]{1,0:T(8,128)(2,1)S(1)}, u32[]{:S(2)}, u32[]{:S(2)}) collective-permute-start(bf16[1424,256]{1,0:T(8,128)(2,1)S(1)} %collective-permute-done.6.refs_7_), channel_id=1, source_target_pairs={{0,192},{16,80},{64,0},{80,144},{128,64},{144,208},{192,128},{208,... | collective-permute-start | bytes 2187272 | tf_op jit(solution)/shard_map/ppermute | solution.py:59
  39.6 20.2 %collective-permute-start.16 = (bf16[1424,256]{1,0:T(8,128)(2,1)S(1)}, bf16[1424,256]{1,0:T(8,128)(2,1)S(1)}, u32[]{:S(2)}, u32[]{:S(2)}) collective-permute-start(bf16[1424,256]{1,0:T(8,128)(2,1)S(1)} %collective-permute-done.6.refs_7_), channel_id=1, source_target_pairs={{0,16},{16,0},{1,17},{17,1},{2,18},{18,2},{3,19},{19,3},{4,20},{20... | collective-permute-start | bytes 2187272 | tf_op jit(solution)/shard_map/ppermute | solution.py:51
  45.9 13.9 %collective-permute-start.17 = (bf16[1424,256]{1,0:T(8,128)(2,1)S(1)}, bf16[1424,256]{1,0:T(8,128)(2,1)S(1)}, u32[]{:S(2)}, u32[]{:S(2)}) collective-permute-start(bf16[1424,256]{1,0:T(8,128)(2,1)S(1)} %collective-permute-done.2.refs_8_), channel_id=1, source_target_pairs={{0,16},{16,0},{1,17},{17,1},{2,18},{18,2},{3,19},{19,3},{4,20},{20... | collective-permute-start | bytes 2187272 | tf_op jit(solution)/shard_map/ppermute | solution.py:51
  45.9 12.6 %collective-permute-start.14 = (bf16[1424,256]{1,0:T(8,128)(2,1)S(1)}, bf16[1424,256]{1,0:T(8,128)(2,1)S(1)}, u32[]{:S(2)}, u32[]{:S(2)}) collective-permute-start(bf16[1424,256]{1,0:T(8,128)(2,1)S(1)} %collective-permute-done.2.refs_8_), channel_id=1, source_target_pairs={{0,64},{16,208},{64,128},{80,16},{128,192},{144,80},{192,0},{208,1... | collective-permute-start | bytes 2187272 | tf_op jit(solution)/shard_map/ppermute | solution.py:59
  54.7 10.8 %collective-permute-start.12 = (bf16[2,256,384]{2,1,0:T(8,128)(2,1)S(1)}, bf16[2,256,384]{2,1,0:T(8,128)(2,1)S(1)}, u32[]{:S(2)}, u32[]{:S(2)}) collective-permute-start(bf16[2,256,384]{2,1,0:T(8,128)(2,1)S(1)} %collective-permute-done.10.refs_0_), channel_id=1, source_target_pairs={{0,1},{1,2},{2,3},{3,4},{4,5},{5,6},{6,7},{7,0},{8,9},{9,10},{10,1... | collective-permute-start | bytes 1179656 | tf_op jit(solution)/shard_map/ppermute | solution.py:51
  54.7 10.8 %collective-permute-start.13 = (bf16[2,256,384]{2,1,0:T(8,128)(2,1)S(1)}, bf16[2,256,384]{2,1,0:T(8,128)(2,1)S(1)}, u32[]{:S(2)}, u32[]{:S(2)}) collective-permute-start(bf16[2,256,384]{2,1,0:T(8,128)(2,1)S(1)} %collective-permute-done.11.refs_1_), channel_id=1, source_target_pairs={{0,7},{1,0},{2,1},{3,2},{4,3},{5,4},{6,5},{7,6},{8,15},{9,8},{10,9... | collective-permute-start | bytes 1179656 | tf_op jit(solution)/shard_map/ppermute | solution.py:51
  58.5 21.5 %collective-permute-start.9 = (bf16[1424,256]{1,0:T(8,128)(2,1)S(1)}, bf16[1424,256]{1,0:T(8,128)(2,1)S(1)}, u32[]{:S(2)}, u32[]{:S(2)}) collective-permute-start(bf16[1424,256]{1,0:T(8,128)(2,1)S(1)} %collective-permute-done.8.refs_2_), channel_id=1, source_target_pairs={{0,192},{16,80},{64,0},{80,144},{128,64},{144,208},{192,128},{208,... | collective-permute-start | bytes 2187272 | tf_op jit(solution)/shard_map/ppermute | solution.py:59
  65.5 3.8 %collective-permute-start.18 = (bf16[1424,256]{1,0:T(8,128)(2,1)S(1)}, bf16[1424,256]{1,0:T(8,128)(2,1)S(1)}, u32[]{:S(2)}, u32[]{:S(2)}) collective-permute-start(bf16[1424,256]{1,0:T(8,128)(2,1)S(1)} %collective-permute-done.15.refs_4_), channel_id=1, source_target_pairs={{0,16},{16,0},{1,17},{17,1},{2,18},{18,2},{3,19},{19,3},{4,20},{20... | collective-permute-start | bytes 2187272 | tf_op jit(solution)/shard_map/ppermute | solution.py:51
  65.6 3.8 %collective-permute-start.19 = (bf16[1424,256]{1,0:T(8,128)(2,1)S(1)}, bf16[1424,256]{1,0:T(8,128)(2,1)S(1)}, u32[]{:S(2)}, u32[]{:S(2)}) collective-permute-start(bf16[1424,256]{1,0:T(8,128)(2,1)S(1)} %collective-permute-done.14.refs_3_), channel_id=1, source_target_pairs={{0,16},{16,0},{1,17},{17,1},{2,18},{18,2},{3,19},{19,3},{4,20},{20... | collective-permute-start | bytes 2187272 | tf_op jit(solution)/shard_map/ppermute | solution.py:51
  66.1 3.8 %collective-permute-start.20 = (bf16[1424,256]{1,0:T(8,128)(2,1)S(1)}, bf16[1424,256]{1,0:T(8,128)(2,1)S(1)}, u32[]{:S(2)}, u32[]{:S(2)}) collective-permute-start(bf16[1424,256]{1,0:T(8,128)(2,1)S(1)} %collective-permute-done.8.refs_2_), channel_id=1, source_target_pairs={{0,16},{16,0},{1,17},{17,1},{2,18},{18,2},{3,19},{19,3},{4,20},{20... | collective-permute-start | bytes 2187272 | tf_op jit(solution)/shard_map/ppermute | solution.py:51
  66.2 13.7 %collective-permute-start.22 = (bf16[256,384]{1,0:T(8,128)(2,1)S(1)}, bf16[256,384]{1,0:T(8,128)(2,1)S(1)}, u32[]{:S(2)}, u32[]{:S(2)}) collective-permute-start(bf16[256,384]{1,0:T(8,128)(2,1)S(1)} %slice_bitcast_fusion), channel_id=1, source_target_pairs={{0,7},{1,0},{2,1},{3,2},{4,3},{5,4},{6,5},{7,6},{8,15},{9,8},{10,9... | collective-permute-start | bytes 589832 | tf_op jit(solution)/shard_map/ppermute | solution.py:51
  69.3 10.7 %collective-permute-start.21 = (bf16[256,384]{1,0:T(8,128)(2,1)S(1)}, bf16[256,384]{1,0:T(8,128)(2,1)S(1)}, u32[]{:S(2)}, u32[]{:S(2)}) collective-permute-start(bf16[256,384]{1,0:T(8,128)(2,1)S(1)} %slice_bitcast_fusion.1), channel_id=1, source_target_pairs={{0,1},{1,2},{2,3},{3,4},{4,5},{5,6},{6,7},{7,0},{8,9},{9,10},{10,1... | collective-permute-start | bytes 589832 | tf_op jit(solution)/shard_map/ppermute | solution.py:51
  70.0 12.4 %copy-start = (bf16[256,1536]{1,0:T(8,128)(2,1)S(1)}, bf16[256,1536]{1,0:T(8,128)(2,1)}, u32[]{:S(2)}) copy-start(bf16[256,1536]{1,0:T(8,128)(2,1)} %up_ref.1) | copy-start | bytes 2359300
  80.0 2.3 %collective-permute-start.23 = (bf16[1424,256]{1,0:T(8,128)(2,1)S(1)}, bf16[1424,256]{1,0:T(8,128)(2,1)S(1)}, u32[]{:S(2)}, u32[]{:S(2)}) collective-permute-start(bf16[1424,256]{1,0:T(8,128)(2,1)S(1)} %collective-permute-done.9.refs_2_), channel_id=1, source_target_pairs={{0,16},{16,0},{1,17},{17,1},{2,18},{18,2},{3,19},{19,3},{4,20},{20... | collective-permute-start | bytes 2187272 | tf_op jit(solution)/shard_map/ppermute | solution.py:51
  90.4 9.3 %collective-permute-start.24 = (bf16[1,256,384]{2,1,0:T(8,128)(2,1)S(1)}, bf16[1,256,384]{2,1,0:T(8,128)(2,1)S(1)}, u32[]{:S(2)}, u32[]{:S(2)}) collective-permute-start(bf16[1,256,384]{2,1,0:T(8,128)(2,1)S(1)} %get-tuple-element.86), channel_id=1, source_target_pairs={{0,8},{8,0},{1,9},{9,1},{2,10},{10,2},{3,11},{11,3},{4,12},{12,4},... | collective-permute-start | bytes 589832 | tf_op jit(solution)/shard_map/ppermute | solution.py:51
  93.5 15.1 %collective-permute-start.26 = (bf16[2,256,384]{2,1,0:T(8,128)(2,1)S(1)}, bf16[2,256,384]{2,1,0:T(8,128)(2,1)S(1)}, u32[]{:S(2)}, u32[]{:S(2)}) collective-permute-start(bf16[2,256,384]{2,1,0:T(8,128)(2,1)S(1)} %get-tuple-element.88), channel_id=1, source_target_pairs={{0,8},{8,0},{1,9},{9,1},{2,10},{10,2},{3,11},{11,3},{4,12},{12,4},... | collective-permute-start | bytes 1179656 | tf_op jit(solution)/shard_map/ppermute | solution.py:51
  101.9 6.7 %collective-permute-start.27 = (bf16[1,256,384]{2,1,0:T(8,128)(2,1)S(1)}, bf16[1,256,384]{2,1,0:T(8,128)(2,1)S(1)}, u32[]{:S(2)}, u32[]{:S(2)}) collective-permute-start(bf16[1,256,384]{2,1,0:T(8,128)(2,1)S(1)} %get-tuple-element.89), channel_id=1, source_target_pairs={{0,1},{1,2},{2,3},{3,4},{4,5},{5,6},{6,7},{7,0},{8,9},{9,10},{10,1... | collective-permute-start | bytes 589832 | tf_op jit(solution)/shard_map/ppermute | solution.py:51
  104.0 13.6 %collective-permute-start.25 = (bf16[2,256,384]{2,1,0:T(8,128)(2,1)S(1)}, bf16[2,256,384]{2,1,0:T(8,128)(2,1)S(1)}, u32[]{:S(2)}, u32[]{:S(2)}) collective-permute-start(bf16[2,256,384]{2,1,0:T(8,128)(2,1)S(1)} %get-tuple-element.87), channel_id=1, source_target_pairs={{0,8},{8,0},{1,9},{9,1},{2,10},{10,2},{3,11},{11,3},{4,12},{12,4},... | collective-permute-start | bytes 1179656 | tf_op jit(solution)/shard_map/ppermute | solution.py:51
  111.2 7.0 %collective-permute-start.28 = (bf16[1,256,384]{2,1,0:T(8,128)(2,1)S(1)}, bf16[1,256,384]{2,1,0:T(8,128)(2,1)S(1)}, u32[]{:S(2)}, u32[]{:S(2)}) collective-permute-start(bf16[1,256,384]{2,1,0:T(8,128)(2,1)S(1)} %get-tuple-element.90), channel_id=1, source_target_pairs={{0,1},{1,2},{2,3},{3,4},{4,5},{5,6},{6,7},{7,0},{8,9},{9,10},{10,1... | collective-permute-start | bytes 589832 | tf_op jit(solution)/shard_map/ppermute | solution.py:51
  112.9 5.7 %collective-permute-start.29 = (bf16[1,256,384]{2,1,0:T(8,128)(2,1)S(1)}, bf16[1,256,384]{2,1,0:T(8,128)(2,1)S(1)}, u32[]{:S(2)}, u32[]{:S(2)}) collective-permute-start(bf16[1,256,384]{2,1,0:T(8,128)(2,1)S(1)} %get-tuple-element.91), channel_id=1, source_target_pairs={{0,7},{1,0},{2,1},{3,2},{4,3},{5,4},{6,5},{7,6},{8,15},{9,8},{10,9... | collective-permute-start | bytes 589832 | tf_op jit(solution)/shard_map/ppermute | solution.py:51
  114.6 14.1 %collective-permute-start.31 = (bf16[2,256,384]{2,1,0:T(8,128)(2,1)S(1)}, bf16[2,256,384]{2,1,0:T(8,128)(2,1)S(1)}, u32[]{:S(2)}, u32[]{:S(2)}) collective-permute-start(bf16[2,256,384]{2,1,0:T(8,128)(2,1)S(1)} %get-tuple-element.93), channel_id=1, source_target_pairs={{0,8},{8,0},{1,9},{9,1},{2,10},{10,2},{3,11},{11,3},{4,12},{12,4},... | collective-permute-start | bytes 1179656 | tf_op jit(solution)/shard_map/ppermute | solution.py:51
  120.8 6.6 %collective-permute-start.32 = (bf16[1,256,384]{2,1,0:T(8,128)(2,1)S(1)}, bf16[1,256,384]{2,1,0:T(8,128)(2,1)S(1)}, u32[]{:S(2)}, u32[]{:S(2)}) collective-permute-start(bf16[1,256,384]{2,1,0:T(8,128)(2,1)S(1)} %get-tuple-element.94), channel_id=1, source_target_pairs={{0,1},{1,2},{2,3},{3,4},{4,5},{5,6},{6,7},{7,0},{8,9},{9,10},{10,1... | collective-permute-start | bytes 589832 | tf_op jit(solution)/shard_map/ppermute | solution.py:51
  122.9 5.8 %collective-permute-start.33 = (bf16[1,256,384]{2,1,0:T(8,128)(2,1)S(1)}, bf16[1,256,384]{2,1,0:T(8,128)(2,1)S(1)}, u32[]{:S(2)}, u32[]{:S(2)}) collective-permute-start(bf16[1,256,384]{2,1,0:T(8,128)(2,1)S(1)} %get-tuple-element.95), channel_id=1, source_target_pairs={{0,7},{1,0},{2,1},{3,2},{4,3},{5,4},{6,5},{7,6},{8,15},{9,8},{10,9... | collective-permute-start | bytes 589832 | tf_op jit(solution)/shard_map/ppermute | solution.py:51
  123.8 8.8 %collective-permute-start.30 = (bf16[1,256,384]{2,1,0:T(8,128)(2,1)S(1)}, bf16[1,256,384]{2,1,0:T(8,128)(2,1)S(1)}, u32[]{:S(2)}, u32[]{:S(2)}) collective-permute-start(bf16[1,256,384]{2,1,0:T(8,128)(2,1)S(1)} %get-tuple-element.92), channel_id=1, source_target_pairs={{0,8},{8,0},{1,9},{9,1},{2,10},{10,2},{3,11},{11,3},{4,12},{12,4},... | collective-permute-start | bytes 589832 | tf_op jit(solution)/shard_map/ppermute | solution.py:51
  130.5 5.7 %collective-permute-start.34 = (bf16[1,256,384]{2,1,0:T(8,128)(2,1)S(1)}, bf16[1,256,384]{2,1,0:T(8,128)(2,1)S(1)}, u32[]{:S(2)}, u32[]{:S(2)}) collective-permute-start(bf16[1,256,384]{2,1,0:T(8,128)(2,1)S(1)} %get-tuple-element.96), channel_id=1, source_target_pairs={{0,1},{1,2},{2,3},{3,4},{4,5},{5,6},{6,7},{7,0},{8,9},{9,10},{10,1... | collective-permute-start | bytes 589832 | tf_op jit(solution)/shard_map/ppermute | solution.py:51
  132.5 5.7 %collective-permute-start.35 = (bf16[1,256,384]{2,1,0:T(8,128)(2,1)S(1)}, bf16[1,256,384]{2,1,0:T(8,128)(2,1)S(1)}, u32[]{:S(2)}, u32[]{:S(2)}) collective-permute-start(bf16[1,256,384]{2,1,0:T(8,128)(2,1)S(1)} %get-tuple-element.97), channel_id=1, source_target_pairs={{0,7},{1,0},{2,1},{3,2},{4,3},{5,4},{6,5},{7,6},{8,15},{9,8},{10,9... | collective-permute-start | bytes 589832 | tf_op jit(solution)/shard_map/ppermute | solution.py:51

commit v4 on v3

--- a/solution.py
+++ b/solution.py
@@ -13,7 +13,7 @@
 COL = ("x_hi", "z")
 SIZES = {"y": 4, "x_lo": 2, "core": 2, "x_hi": 2, "z": 8}
 SIDE = 128
-EARLY_CHUNKS = 14
+READY = ((9, 10), (14, 14), (16, 16))
 ORDER = (4, 3, -3, 2, -2, 1, -1, 0)
 VMEM_LIMIT = 10 * 1024 * 1024
 ON_CHIP = pl.BlockSpec(memory_space=pltpu.VMEM)
@@ -114,40 +114,43 @@
         acc[col] += jnp.dot(taken, slot_of(w_ref, tile, slot), preferred_element_type=jnp.float32)
 
 
-def early_kernel(n_x, n_w, first_x, first_w, pick, names, *refs):
-    x_parts, w_parts = refs[:n_x], refs[n_x:n_x + n_w]
-    x_ref, w_ref, acc, x_sems, w_sems = refs[n_x + n_w + 2:]
-    copies = load(x_parts, x_ref, x_sems, first_x) + load(w_parts, w_ref, w_sems, first_w)
-    acc[...] = jnp.zeros_like(acc)
+def ready(tile, pick, stage):
+    tiles, chunks = READY[stage]
+    return (tile < tiles) & (pick[tile] < chunks)
+
+
+def add_stage(stage, x_parts, w_parts, pick, names, x_ref, w_ref, acc, x_sems, w_sems):
+    tiles, chunks = READY[stage]
+    count = sum(part.shape[0] if len(part.shape) == 3 else 1 for part in x_parts)
+    copies = load(x_parts, x_ref, x_sems, chunks - count)
+    copies += load(w_parts, w_ref, w_sems, tiles - len(w_parts))
+    if stage == 0:
+        acc[...] = jnp.zeros_like(acc)
     for copy in copies:
         copy.wait()
 
     def tile_step(tile, carry):
-        @pl.when(pick[tile] < EARLY_CHUNKS)
+        new = ready(tile, pick, stage)
+        if stage > 0:
+            new = new & jnp.logical_not(ready(tile, pick, stage - 1))
+
+        @pl.when(new)
         def _():
             add_tile(tile, pick, names, x_ref, w_ref, acc)
 
         return carry
 
-    lax.fori_loop(0, first_w + n_w, tile_step, 0)
+    lax.fori_loop(0, tiles, tile_step, 0)
+
+
+def early_kernel(stage, n_x, n_w, n_kept, pick, names, *refs):
+    add_stage(stage, refs[:n_x], refs[n_x:n_x + n_w], pick, names, *refs[n_x + n_w + n_kept:])
 
 
 def late_kernel(n_x, n_w, pick, names, up_ref, *refs):
-    x_parts, w_parts = refs[:n_x], refs[n_x:n_x + n_w]
-    hidden_ref, grads_ref, x_ref, w_ref, acc, x_sems, w_sems = refs[n_x + n_w + 3:]
-    first = w_ref.shape[0] - n_w
-    copies = load(x_parts, x_ref, x_sems, EARLY_CHUNKS) + load(w_parts, w_ref, w_sems, first)
-    for copy in copies:
-        copy.wait()
-
-    def tile_step(tile, carry):
-        @pl.when((tile >= first) | (pick[tile] >= EARLY_CHUNKS))
-        def _():
-            add_tile(tile, pick, names, x_ref, w_ref, acc)
-
-        return carry
-
-    lax.fori_loop(0, w_ref.shape[0], tile_step, 0)
+    hidden_ref, grads_ref, *rest = refs[n_x + n_w + 3:]
+    acc = rest[2]
+    add_stage(2, refs[:n_x], refs[n_x:n_x + n_w], pick, names, *rest)
     for j in range(grads_ref.shape[0]):
         columns = slice(j * SIDE, (j + 1) * SIDE)
         gate = acc[j, :, :SIDE]
@@ -170,28 +173,25 @@
     )
 
 
-def forward_early(pick, names, x_parts, w_parts, x, w, col_count):
-    tokens = x.shape[1]
-    depth, pair = w_parts[0].shape
+def forward_early(stage, pick, names, x_parts, w_parts, kept, col_count):
+    tokens = kept[0].shape[1]
     parts = len(x_parts) + len(w_parts)
-    first_w = len(TILES) - 2 - len(w_parts)
-    first_x = EARLY_CHUNKS - 2 * len(x_parts)
     return pl.pallas_call(
-        functools.partial(early_kernel, len(x_parts), len(w_parts), first_x, first_w),
-        in_specs=[SCALARS] * 2 + [ANYWHERE] * parts + [ON_CHIP] * 2,
+        functools.partial(early_kernel, stage, len(x_parts), len(w_parts), len(kept)),
+        in_specs=[SCALARS] * 2 + [ANYWHERE] * parts + [ON_CHIP] * len(kept),
         out_specs=[ON_CHIP] * 3,
-        out_shape=[pltpu.VMEM(kept.shape, kept.dtype) for kept in (x, w)] + [
-            pltpu.VMEM((col_count + 1, tokens, pair), jnp.float32),
-        ],
-        input_output_aliases={2 + parts: 0, 3 + parts: 1},
+        out_shape=[pltpu.VMEM(array.shape, array.dtype) for array in kept[:2]] + [
+            pltpu.VMEM((col_count + 1, tokens, 2 * SIDE), jnp.float32),
+        ],
+        input_output_aliases={2 + parts + number: number for number in range(len(kept))},
         scratch_shapes=[
             pltpu.SemaphoreType.DMA((len(x_parts),)),
             pltpu.SemaphoreType.DMA((len(w_parts),)),
         ],
         compiler_params=pltpu.CompilerParams(vmem_limit_bytes=VMEM_LIMIT),
-        cost_estimate=pl.CostEstimate(flops=0, bytes_accessed=0, transcendentals=0),
+        cost_estimate=cost(6 * (1 - stage), names.shape[1] // 2, tokens, 6 * (1 - stage) << 20, 0),
         name="forward_early",
-    )(pick, names, *x_parts, *w_parts, x, w)
+    )(pick, names, *x_parts, *w_parts, *kept)
 
 
 def forward_late(pick, names, upstream, x_parts, w_parts, x, w, acc):
@@ -268,7 +268,7 @@
     return lax.optimization_barrier((value,) + others)[0]
 
 
-def gather(own, tokens):
+def gather(own, tokens, first):
     def swap(value):
         return shift(value, "core", 1)
 
@@ -276,25 +276,26 @@
     across = shift(tokens, "x_hi", 1)
     a1, t0 = turn(own, 1), swap(own)
     b1 = shift(after(own, t0), "x_lo", 1)
-    a1, across = barrier((a1, across))
+    a1, across, t0 = barrier((a1, across, t0))
     both = jnp.stack([tokens, across])
     a2 = turn(a1, 1)
     p1, m1 = shift(both, "z", 1), shift(both, "z", -1)
     t1 = swap(a1)
-    a2, p1, m1, b1, t1 = barrier((a2, p1, m1, b1, t1))
+    a2, p1, m1, t1 = barrier((a2, p1, m1, t1))
     c1, a3, b2 = turn(b1, -1), turn(a2, 1), shift(a1, "x_lo", 1)
     kept = store((both, p1, m1), (own, t0, a1, t1, b1, a2), 0, 0)
     p2, m2 = shift(p1, "z", 1), shift(m1, "z", -1)
     p2, m2, kept = barrier((p2, m2, kept))
     p3, m3 = shift(p2, "z", 1), shift(m2, "z", -1)
-    x, w = store((p2, m2), (c1, a3, b2), 6, 6, kept)
     c2 = turn(c1, -1)
+    b1, a2, p2, m2 = barrier((b1, a2, p2, m2))
     t2, t3 = swap(b1), swap(a2)
-    p3, m3, c1, a3, b2, t2, t3 = barrier((p3, m3, c1, a3, b2, t2, t3))
+    known = (own, t0, a1, t1, b1, a2, c1, a3, b2)
+    kept = first(kept, known, (p2, m2), (c1, a3, b2))
+    p3, m3, c1, a3, b2, t2, t3, kept = barrier((p3, m3, c1, a3, b2, t2, t3, kept))
     t5, t6, t4 = swap(c1), swap(a3), swap(b2)
     p4, m4 = shift(p3[0], "z", 1), shift(m3[1], "z", -1)
-    known = (own, t0, a1, t1, b1, a2, c1, a3, b2, t2, t3, t5, t6, t4)
-    return x, w, (p3, m3), (t2, t3, t5, t6, t4), (p4, m4), c2, known
+    return kept, known, (p3, m3), (t2, t3, t5, t6, t4), (p4, m4), c2
 
 
 def on_device(tokens, gate_blocks, up_blocks, block_row, block_col, upstream):
@@ -309,8 +310,6 @@
     ]).astype(bf16)
     ids = jnp.broadcast_to(jnp.pad(ids, (0, 2 * SIDE - 2 * slots))[None], (16, 2 * SIDE))
     blocks = jnp.concatenate([gate_blocks, up_blocks], axis=2).reshape(slots * SIDE, 2 * SIDE)
-    x, w, x_early, w_early, x_late, c2, known = gather(jnp.concatenate([blocks, ids]), tokens)
-
     line = lax.broadcasted_iota(i32, (16, 2 * slots), 0)
 
     def names_of(parts):
@@ -320,7 +319,14 @@
             names = jnp.where(line == place, name, names)
         return names.astype(i32)
 
-    x, w, acc = forward_early(pick, names_of(known), x_early, w_early, x, w, upstream.shape[1] // SIDE)
+    col_count = upstream.shape[1] // SIDE
+
+    def first(kept, known, x_parts, w_parts):
+        return forward_early(0, pick, names_of(known), x_parts, w_parts, kept, col_count)
+
+    kept, known, x_early, w_early, x_late, c2 = gather(jnp.concatenate([blocks, ids]), tokens, first)
+    known += w_early
+    x, w, acc = forward_early(1, pick, names_of(known), x_early, w_early, kept, col_count)
     c2, acc, x_late = lax.optimization_barrier((c2, acc, x_late))
     w_late = (c2, shift(c2, "core", 1))
     names = names_of(known + w_late)

time: 141 us -> 139 us (0.986)
  waiting for transfers between devices: 58 us -> 48 us
  starting transfers between devices: 44.8 us -> 52.4 us
    ppermute x31, waiting for transfers between devices: 55 us -> 42.5 us  [shift(): lax.ppermute(value, axis, [(i, (i + step) % size) for i in range(size)])]
    ppermute x5, starting transfers between devices: 3.52 us -> 7.97 us  [turn(): return lax.ppermute(value, ('y', 'core'), pairs)]
    ppermute x31, starting transfers between devices: 41.3 us -> 44.5 us  [shift(): lax.ppermute(value, axis, [(i, (i + step) % size) for i in range(size)])]
    ppermute x5, waiting for transfers between devices: 3.04 us -> 5.53 us  [turn(): return lax.ppermute(value, ('y', 'core'), pairs)]
    pallas_call x1 -> x2, Pallas kernels: 9.94 us -> 12 us  [forward_early(): pl.pallas_call(functools.partial(early_kernel, stage, len(x_parts), len(w...]
    pallas_call x2 -> x1, Pallas kernels: 3.77 us -> 2.44 us  [store(): pl.pallas_call(functools.partial(store_kernel, len(x_parts), len(w_parts)...]
  transfers between devices with their start and end apart: 36 -> 36, of which waited for: 18 -> 19; matrix products, arithmetic and copies ran while one was open for 1% -> 1% of each run, Pallas kernels for 16% -> 17%
where the time goes in v4:
time: 139 us
  starting transfers between devices  52.4 us (38%)
  waiting for transfers between devices  48 us (35%)
  Pallas kernels  33.1 us (24%)
  other arithmetic  3.35 us (2%)
    ppermute x31, starting transfers between devices, shift(): lax.ppermute(value, axis, [(i, (i + step) % size) for i in range(size)])  44.5 us
    ppermute x31, waiting for transfers between devices, shift(): lax.ppermute(value, axis, [(i, (i + step) % size) for i in range(size)])  42.5 us
    pallas_call x6, Pallas kernels, backward(): pl.pallas_call(functools.partial(backward_kernel, jobs), in_specs=[SCALAR...  12.8 us
    pallas_call x2, Pallas kernels, forward_early(): pl.pallas_call(functools.partial(early_kernel, stage, len(x_parts), len(w...  12 us
    ppermute x5, starting transfers between devices, turn(): return lax.ppermute(value, ('y', 'core'), pairs)  7.97 us
    pallas_call x1, Pallas kernels, forward_late(): pl.pallas_call(functools.partial(late_kernel, len(x_parts), len(w_parts))...  5.8 us
    ppermute x5, waiting for transfers between devices, turn(): return lax.ppermute(value, ('y', 'core'), pairs)  5.53 us
  transfers between devices with their start and end apart: 36, of which 19 were waited for; matrix products, arithmetic and copies ran while one was open for 1% of the time, Pallas kernels for 17%

profile of v4, /device:TPU:32, one launch (start us, length us, event | category | flops | bytes accessed | tf_op | source)
XLA Modules:
  0.0 138.7 jit_solution(5167355563650075559)
XLA Ops:
  0.6 0.7 dynamic-slice_bitcast_fusion
  1.3 1.2 pad_maximum_fusion.1
  2.5 0.7 fusion.9
  3.5 1.7 %collective-permute-start.4 = (bf16[1424,256]{1,0:T(8,128)(2,1)S(1)}, bf16[1424,256]{1,0:T(8,128)(2,1)S(1)}, u32[]{:S(2)}, u32[]{:S(2)}) collective-permute-start(bf16[1424,256]{1,0:T(8,128)(2,1)S(1)} %pad_maximum_fusion.refs_3_), channel_id=1, source_target_pairs={{0,64},{16,208},{64,128},{80,16},{128,192},{144,80},{192,0},{208,1... | collective-permute-start | bytes 2187272 | tf_op jit(solution)/shard_map/ppermute | solution.py:59
  5.1 3.0 %collective-permute-start.5 = (bf16[256,384]{1,0:T(8,128)(2,1)}, bf16[256,384]{1,0:T(8,128)(2,1)S(1)}, u32[]{:S(2)}, u32[]{:S(2)}) collective-permute-start(bf16[256,384]{1,0:T(8,128)(2,1)} %param.7), channel_id=1, source_target_pairs={{0,8},{8,0},{1,9},{9,1},{2,10},{10,2},{3,11},{11,3},{4,12},{12,4},... | collective-permute-start | bytes 589832 | tf_op jit(solution)/shard_map/ppermute | solution.py:51
  8.2 5.9 %collective-permute-done.5 = bf16[256,384]{1,0:T(8,128)(2,1)S(1)} collective-permute-done((bf16[256,384]{1,0:T(8,128)(2,1)}, bf16[256,384]{1,0:T(8,128)(2,1)S(1)}, u32[]{:S(2)}, u32[]{:S(2)}) %collective-permute-start.5) | collective-permute-done | bytes 196640 | tf_op jit(solution)/shard_map/ppermute | solution.py:51
  14.1 2.1 %collective-permute-done.4.refs_5_ = bf16[1424,256]{1,0:T(8,128)(2,1)S(1)} collective-permute-done((bf16[1424,256]{1,0:T(8,128)(2,1)S(1)}, bf16[1424,256]{1,0:T(8,128)(2,1)S(1)}, u32[]{:S(2)}, u32[]{:S(2)}) %collective-permute-start.4) | collective-permute-done | bytes 729120 | tf_op jit(solution)/shard_map/ppermute | solution.py:59
  16.1 1.5 %collective-permute-start.1 = (bf16[1424,256]{1,0:T(8,128)(2,1)S(1)}, bf16[1424,256]{1,0:T(8,128)(2,1)S(1)}, u32[]{:S(2)}, u32[]{:S(2)}) collective-permute-start(bf16[1424,256]{1,0:T(8,128)(2,1)S(1)} %pad_maximum_fusion.refs_3_), channel_id=1, source_target_pairs={{0,32},{32,0},{1,33},{33,1},{2,34},{34,2},{3,35},{35,3},{4,36},{36... | collective-permute-start | bytes 2187272 | tf_op jit(solution)/shard_map/ppermute | solution.py:51
  17.6 1.0 pad_maximum_fusion.2.refs_0_
  18.6 2.0 %collective-permute-start.7 = (bf16[2,256,384]{2,1,0:T(8,128)(2,1)S(1)}, bf16[2,256,384]{2,1,0:T(8,128)(2,1)S(1)}, u32[]{:S(2)}, u32[]{:S(2)}) collective-permute-start(bf16[2,256,384]{2,1,0:T(8,128)(2,1)S(1)} %pad_maximum_fusion.2.refs_0_), channel_id=1, source_target_pairs={{0,1},{1,2},{2,3},{3,4},{4,5},{5,6},{6,7},{7,0},{8,9},{9,10},{10,1... | collective-permute-start | bytes 1179656 | tf_op jit(solution)/shard_map/ppermute | solution.py:51
  20.6 0.4 collective-permute-start.6
  21.0 1.1 collective-permute-start.9
  22.1 0.6 collective-permute-start.15
  22.7 5.6 %collective-permute-done.7.refs_1_ = bf16[2,256,384]{2,1,0:T(8,128)(2,1)S(1)} collective-permute-done((bf16[2,256,384]{2,1,0:T(8,128)(2,1)S(1)}, bf16[2,256,384]{2,1,0:T(8,128)(2,1)S(1)}, u32[]{:S(2)}, u32[]{:S(2)}) %collective-permute-start.7) | collective-permute-done | bytes 393248 | tf_op jit(solution)/shard_map/ppermute | solution.py:51
  28.3 4.2 %collective-permute-start.8 = (bf16[2,256,384]{2,1,0:T(8,128)(2,1)S(1)}, bf16[2,256,384]{2,1,0:T(8,128)(2,1)S(1)}, u32[]{:S(2)}, u32[]{:S(2)}) collective-permute-start(bf16[2,256,384]{2,1,0:T(8,128)(2,1)S(1)} %pad_maximum_fusion.2.refs_0_), channel_id=1, source_target_pairs={{0,7},{1,0},{2,1},{3,2},{4,3},{5,4},{6,5},{7,6},{8,15},{9,8},{10,9... | collective-permute-start | bytes 1179656 | tf_op jit(solution)/shard_map/ppermute | solution.py:51
  32.6 2.8 %collective-permute-done.1.refs_7_ = bf16[1424,256]{1,0:T(8,128)(2,1)S(1)} collective-permute-done((bf16[1424,256]{1,0:T(8,128)(2,1)S(1)}, bf16[1424,256]{1,0:T(8,128)(2,1)S(1)}, u32[]{:S(2)}, u32[]{:S(2)}) %collective-permute-start.1) | collective-permute-done | bytes 729120 | tf_op jit(solution)/shard_map/ppermute | solution.py:51
  35.4 1.7 %collective-permute-start.2 = (bf16[1424,256]{1,0:T(8,128)(2,1)S(1)}, bf16[1424,256]{1,0:T(8,128)(2,1)S(1)}, u32[]{:S(2)}, u32[]{:S(2)}) collective-permute-start(bf16[1424,256]{1,0:T(8,128)(2,1)S(1)} %collective-permute-done.1.refs_7_), channel_id=1, source_target_pairs={{0,192},{16,80},{64,0},{80,144},{128,64},{144,208},{192,128},{208,... | collective-permute-start | bytes 2187272 | tf_op jit(solution)/shard_map/ppermute | solution.py:59
  37.0 2.2 %collective-permute-done.8.refs_2_ = bf16[2,256,384]{2,1,0:T(8,128)(2,1)S(1)} collective-permute-done((bf16[2,256,384]{2,1,0:T(8,128)(2,1)S(1)}, bf16[2,256,384]{2,1,0:T(8,128)(2,1)S(1)}, u32[]{:S(2)}, u32[]{:S(2)}) %collective-permute-start.8) | collective-permute-done | bytes 393248 | tf_op jit(solution)/shard_map/ppermute | solution.py:51
  39.2 0.5 collective-permute-start.10
  39.8 2.1 %collective-permute-start.11 = (bf16[2,256,384]{2,1,0:T(8,128)(2,1)S(1)}, bf16[2,256,384]{2,1,0:T(8,128)(2,1)S(1)}, u32[]{:S(2)}, u32[]{:S(2)}) collective-permute-start(bf16[2,256,384]{2,1,0:T(8,128)(2,1)S(1)} %collective-permute-done.8.refs_2_), channel_id=1, source_target_pairs={{0,7},{1,0},{2,1},{3,2},{4,3},{5,4},{6,5},{7,6},{8,15},{9,8},{10,9... | collective-permute-start | bytes 1179656 | tf_op jit(solution)/shard_map/ppermute | solution.py:51
  41.8 1.5 %collective-permute-start.14 = (bf16[1424,256]{1,0:T(8,128)(2,1)S(1)}, bf16[1424,256]{1,0:T(8,128)(2,1)S(1)}, u32[]{:S(2)}, u32[]{:S(2)}) collective-permute-start(bf16[1424,256]{1,0:T(8,128)(2,1)S(1)} %collective-permute-done.6.refs_8_), channel_id=1, source_target_pairs={{0,64},{16,208},{64,128},{80,16},{128,192},{144,80},{192,0},{208,1... | collective-permute-start | bytes 2187272 | tf_op jit(solution)/shard_map/ppermute | solution.py:59
  43.3 2.4 %store.1 = (bf16[16,256,384]{2,1,0:T(8,128)(2,1)S(1)}, bf16[16,1424,256]{2,1,0:T(8,128)(2,1)S(1)}) custom-call(bf16[2,256,384]{2,1,0:T(8,128)(2,1)S(1)} %pad_maximum_fusion.2.refs_0_, bf16[2,256,384]{2,1,0:T(8,128)(2,1)S(1)} %collective-permute-done.7.refs_1_, bf16[2,256,384]{2,1,0:T(8,128)(2,1)S(1)} %collective-permute-done.8.refs_2_, ...), custom_call_target="tpu_custom_call" | custom-call | bytes 13123584 | tf_op jit(solution)/shard_map/store/pallas_call | solution.py:89
  45.8 3.1 %collective-permute-done.15.refs_4_ = bf16[1424,256]{1,0:T(8,128)(2,1)S(1)} collective-permute-done((bf16[1424,256]{1,0:T(8,128)(2,1)S(1)}, bf16[1424,256]{1,0:T(8,128)(2,1)S(1)}, u32[]{:S(2)}, u32[]{:S(2)}) %collective-permute-start.15) | collective-permute-done | bytes 729120 | tf_op jit(solution)/shard_map/ppermute | solution.py:51
  48.9 0.6 collective-permute-done.11.refs_1_
  49.5 1.9 %collective-permute-start.12 = (bf16[2,256,384]{2,1,0:T(8,128)(2,1)S(1)}, bf16[2,256,384]{2,1,0:T(8,128)(2,1)S(1)}, u32[]{:S(2)}, u32[]{:S(2)}) collective-permute-start(bf16[2,256,384]{2,1,0:T(8,128)(2,1)S(1)} %collective-permute-done.10.refs_0_), channel_id=1, source_target_pairs={{0,1},{1,2},{2,3},{3,4},{4,5},{5,6},{6,7},{7,0},{8,9},{9,10},{10,1... | collective-permute-start | bytes 1179656 | tf_op jit(solution)/shard_map/ppermute | solution.py:51
  51.4 0.5 collective-permute-start.17
  51.9 0.7 collective-permute-start.13
  52.6 3.5 %collective-permute-done.14.refs_3_ = bf16[1424,256]{1,0:T(8,128)(2,1)S(1)} collective-permute-done((bf16[1424,256]{1,0:T(8,128)(2,1)S(1)}, bf16[1424,256]{1,0:T(8,128)(2,1)S(1)}, u32[]{:S(2)}, u32[]{:S(2)}) %collective-permute-start.14) | collective-permute-done | bytes 729120 | tf_op jit(solution)/shard_map/ppermute | solution.py:59
  56.1 2.8 %collective-permute-start.3 = (bf16[1424,256]{1,0:T(8,128)(2,1)S(1)}, bf16[1424,256]{1,0:T(8,128)(2,1)S(1)}, u32[]{:S(2)}, u32[]{:S(2)}) collective-permute-start(bf16[1424,256]{1,0:T(8,128)(2,1)S(1)} %collective-permute-done.2.refs_2_), channel_id=1, source_target_pairs={{0,192},{16,80},{64,0},{80,144},{128,64},{144,208},{192,128},{208,... | collective-permute-start | bytes 2187272 | tf_op jit(solution)/shard_map/ppermute | solution.py:59
  58.9 4.6 %forward_early.2 = (bf16[16,256,384]{2,1,0:T(8,128)(2,1)S(1)}, bf16[16,1424,256]{2,1,0:T(8,128)(2,1)S(1)}, f32[13,256,256]{2,1,0:T(8,128)S(1)}) custom-call(s32[16]{0:T(128)S(1)} %get-tuple-element.117.pick, s32[16,22]{1,0:T(8,128)S(1)} %fusion.names, ...), custom_call_target="tpu_custom_call", output_to_operand_aliasing={{0}: (7, {}), {1}: (8, {})} | custom-call | flops 1107296256 | bytes 6291456 | tf_op jit(solution)/shard_map/forward_early/pallas_call | solution.py:179
  63.6 1.0 collective-permute-done.13.refs_1_
  64.6 0.5 collective-permute-start.19
  65.2 3.0 %collective-permute-start.21 = (bf16[256,384]{1,0:T(8,128)(2,1)S(1)}, bf16[256,384]{1,0:T(8,128)(2,1)S(1)}, u32[]{:S(2)}, u32[]{:S(2)}) collective-permute-start(bf16[256,384]{1,0:T(8,128)(2,1)S(1)} %slice_bitcast_fusion.1), channel_id=1, source_target_pairs={{0,1},{1,2},{2,3},{3,4},{4,5},{5,6},{6,7},{7,0},{8,9},{9,10},{10,1... | collective-permute-start | bytes 589832 | tf_op jit(solution)/shard_map/ppermute | solution.py:51
  68.3 1.4 collective-permute-start.22
  69.7 0.1 fusion.1.names
  69.8 7.4 %forward_early.3 = (bf16[16,256,384]{2,1,0:T(8,128)(2,1)S(1)}, bf16[16,1424,256]{2,1,0:T(8,128)(2,1)S(1)}, f32[13,256,256]{2,1,0:T(8,128)S(1)}) custom-call(s32[16]{0:T(128)S(1)} %get-tuple-element.117.pick, s32[16,22]{1,0:T(8,128)S(1)} %fusion.1.names, ...), custom_call_target="tpu_custom_call", output_to_operand_aliasing={{0}: (9, {}), {1}: (10, {}), {2}: (11, {})} | custom-call | tf_op jit(solution)/shard_map/forward_early/pallas_call | solution.py:179
  77.4 2.2 %collective-permute-done.23.refs_3_ = bf16[1424,256]{1,0:T(8,128)(2,1)S(1)} collective-permute-done((bf16[1424,256]{1,0:T(8,128)(2,1)S(1)}, bf16[1424,256]{1,0:T(8,128)(2,1)S(1)}, u32[]{:S(2)}, u32[]{:S(2)}) %collective-permute-start.23) | collective-permute-done | bytes 729120 | tf_op jit(solution)/shard_map/ppermute | solution.py:51
  79.6 0.1 select_convert_fusion.names
  79.7 5.8 %forward_late.1 = (bf16[256,1536]{1,0:T(8,128)(2,1)}, bf16[12,256,256]{2,1,0:T(8,128)(2,1)S(1)}, bf16[16,256,384]{2,1,0:T(8,128)(2,1)S(1)}, bf16[16,1424,256]{2,1,0:T(8,128)(2,1)S(1)}, f32[13,256,256]{2,1,0:T(8,128)S(1)}) custom-call(s32[16]{0:T(128)S(1)} %get-tuple-element.117.pick, ...), custom_call_target="tpu_custom_call", output_to_operand_aliasing={{2}: (7, {}), {3}: (8, {}), {4}: (9, {})} | custom-call | flops 738197504 | bytes 3932160 | tf_op jit(solution)/shard_map/forward_late/pallas_call | solution.py:201
  85.5 2.2 %backward.6 = (bf16[1,256,384]{2,1,0:T(8,128)(2,1)S(1)}, bf16[2,256,384]{2,1,0:T(8,128)(2,1)S(1)}) custom-call(s32[16]{0:T(128)S(1)} %get-tuple-element.116.places, s32[16,22]{1,0:T(8,128)S(1)} %select_convert_fusion.names, bf16[12,256,256]{2,1,0:T(8,128)(2,1)S(1)} %get-tuple-element.100.grads_ref, bf16[16,1424,256]{2,1,0:T(8,128)(2,1)S(1)} %get-tuple-element.101.w_ref), custom_call_target="tpu_custom_call" | custom-call | flops 553648128 | bytes 2187264 | tf_op jit(solution)/shard_map/backward/pallas_call | solution.py:255
  87.7 2.8 %collective-permute-start.24 = (bf16[1,256,384]{2,1,0:T(8,128)(2,1)S(1)}, bf16[1,256,384]{2,1,0:T(8,128)(2,1)S(1)}, u32[]{:S(2)}, u32[]{:S(2)}) collective-permute-start(bf16[1,256,384]{2,1,0:T(8,128)(2,1)S(1)} %get-tuple-element.102), channel_id=1, source_target_pairs={{0,8},{8,0},{1,9},{9,1},{2,10},{10,2},{3,11},{11,3},{4,12},{12,4},... | collective-permute-start | bytes 589832 | tf_op jit(solution)/shard_map/ppermute | solution.py:51
  90.5 0.8 collective-permute-start.26
  91.3 5.7 %collective-permute-done.24.refs_0_ = bf16[1,256,384]{2,1,0:T(8,128)(2,1)S(1)} collective-permute-done((bf16[1,256,384]{2,1,0:T(8,128)(2,1)S(1)}, bf16[1,256,384]{2,1,0:T(8,128)(2,1)S(1)}, u32[]{:S(2)}, u32[]{:S(2)}) %collective-permute-start.24) | collective-permute-done | bytes 196640 | tf_op jit(solution)/shard_map/ppermute | solution.py:51
  97.0 2.1 %backward.7 = (bf16[1,256,384]{2,1,0:T(8,128)(2,1)S(1)}, bf16[2,256,384]{2,1,0:T(8,128)(2,1)S(1)}) custom-call(s32[16]{0:T(128)S(1)} %get-tuple-element.116.places, s32[16,22]{1,0:T(8,128)S(1)} %select_convert_fusion.names, bf16[12,256,256]{2,1,0:T(8,128)(2,1)S(1)} %get-tuple-element.100.grads_ref, bf16[16,1424,256]{2,1,0:T(8,128)(2,1)S(1)} %get-tuple-element.101.w_ref, ...), custom_call_target="tpu_custom_call" | custom-call | flops 553648128 | bytes 2187264 | tf_op jit(solution)/shard_map/backward/pallas_call | solution.py:255
  99.2 1.6 %collective-permute-start.27 = (bf16[1,256,384]{2,1,0:T(8,128)(2,1)S(1)}, bf16[1,256,384]{2,1,0:T(8,128)(2,1)S(1)}, u32[]{:S(2)}, u32[]{:S(2)}) collective-permute-start(bf16[1,256,384]{2,1,0:T(8,128)(2,1)S(1)} %get-tuple-element.105), channel_id=1, source_target_pairs={{0,1},{1,2},{2,3},{3,4},{4,5},{5,6},{6,7},{7,0},{8,9},{9,10},{10,1... | collective-permute-start | bytes 589832 | tf_op jit(solution)/shard_map/ppermute | solution.py:51
  100.7 2.7 %collective-permute-start.25 = (bf16[2,256,384]{2,1,0:T(8,128)(2,1)S(1)}, bf16[2,256,384]{2,1,0:T(8,128)(2,1)S(1)}, u32[]{:S(2)}, u32[]{:S(2)}) collective-permute-start(bf16[2,256,384]{2,1,0:T(8,128)(2,1)S(1)} %get-tuple-element.103), channel_id=1, source_target_pairs={{0,8},{8,0},{1,9},{9,1},{2,10},{10,2},{3,11},{11,3},{4,12},{12,4},... | collective-permute-start | bytes 1179656 | tf_op jit(solution)/shard_map/ppermute | solution.py:51
  103.4 1.7 %collective-permute-done.27.refs_1_ = bf16[1,256,384]{2,1,0:T(8,128)(2,1)S(1)} collective-permute-done((bf16[1,256,384]{2,1,0:T(8,128)(2,1)S(1)}, bf16[1,256,384]{2,1,0:T(8,128)(2,1)S(1)}, u32[]{:S(2)}, u32[]{:S(2)}) %collective-permute-start.27) | collective-permute-done | bytes 196640 | tf_op jit(solution)/shard_map/ppermute | solution.py:51
  105.1 0.3 collective-permute-done.26.refs_0_
  105.4 2.6 %backward.8 = (bf16[1,256,384]{2,1,0:T(8,128)(2,1)S(1)}, bf16[1,256,384]{2,1,0:T(8,128)(2,1)S(1)}, bf16[2,256,384]{2,1,0:T(8,128)(2,1)S(1)}) custom-call(s32[16]{0:T(128)S(1)} %get-tuple-element.116.places, s32[16,22]{1,0:T(8,128)S(1)} %select_convert_fusion.names, bf16[12,256,256]{2,1,0:T(8,128)(2,1)S(1)} %get-tuple-element.100.grads_ref, ...), custom_call_target="tpu_custom_call" | custom-call | flops 738197504 | bytes 2916352 | tf_op jit(solution)/shard_map/backward/pallas_call | solution.py:255
  108.0 1.3 collective-permute-start.28
  109.4 1.1 collective-permute-start.29
  110.5 2.9 %collective-permute-start.31 = (bf16[2,256,384]{2,1,0:T(8,128)(2,1)S(1)}, bf16[2,256,384]{2,1,0:T(8,128)(2,1)S(1)}, u32[]{:S(2)}, u32[]{:S(2)}) collective-permute-start(bf16[2,256,384]{2,1,0:T(8,128)(2,1)S(1)} %get-tuple-element.109), channel_id=1, source_target_pairs={{0,8},{8,0},{1,9},{9,1},{2,10},{10,2},{3,11},{11,3},{4,12},{12,4},... | collective-permute-start | bytes 1179656 | tf_op jit(solution)/shard_map/ppermute | solution.py:51
  113.3 0.7 collective-permute-done.28.refs_1_
  114.0 1.0 collective-permute-done.29.refs_2_
  115.1 2.2 %backward.9 = (bf16[1,256,384]{2,1,0:T(8,128)(2,1)S(1)}, bf16[1,256,384]{2,1,0:T(8,128)(2,1)S(1)}, bf16[1,256,384]{2,1,0:T(8,128)(2,1)S(1)}) custom-call(s32[16]{0:T(128)S(1)} %get-tuple-element.116.places, s32[16,22]{1,0:T(8,128)S(1)} %select_convert_fusion.names, bf16[12,256,256]{2,1,0:T(8,128)(2,1)S(1)} %get-tuple-element.100.grads_ref, ...), custom_call_target="tpu_custom_call" | custom-call | flops 553648128 | bytes 2187264 | tf_op jit(solution)/shard_map/backward/pallas_call | solution.py:255
  117.3 3.1 %collective-permute-start.32 = (bf16[1,256,384]{2,1,0:T(8,128)(2,1)S(1)}, bf16[1,256,384]{2,1,0:T(8,128)(2,1)S(1)}, u32[]{:S(2)}, u32[]{:S(2)}) collective-permute-start(bf16[1,256,384]{2,1,0:T(8,128)(2,1)S(1)} %get-tuple-element.110), channel_id=1, source_target_pairs={{0,1},{1,2},{2,3},{3,4},{4,5},{5,6},{6,7},{7,0},{8,9},{9,10},{10,1... | collective-permute-start | bytes 589832 | tf_op jit(solution)/shard_map/ppermute | solution.py:51
  120.3 2.8 %collective-permute-start.30 = (bf16[1,256,384]{2,1,0:T(8,128)(2,1)S(1)}, bf16[1,256,384]{2,1,0:T(8,128)(2,1)S(1)}, u32[]{:S(2)}, u32[]{:S(2)}) collective-permute-start(bf16[1,256,384]{2,1,0:T(8,128)(2,1)S(1)} %get-tuple-element.108), channel_id=1, source_target_pairs={{0,8},{8,0},{1,9},{9,1},{2,10},{10,2},{3,11},{11,3},{4,12},{12,4},... | collective-permute-start | bytes 589832 | tf_op jit(solution)/shard_map/ppermute | solution.py:51
  123.1 0.4 collective-permute-done.32.refs_1_
  123.5 3.7 %collective-permute-done.33.refs_2_ = bf16[1,256,384]{2,1,0:T(8,128)(2,1)S(1)} collective-permute-done((bf16[1,256,384]{2,1,0:T(8,128)(2,1)S(1)}, bf16[1,256,384]{2,1,0:T(8,128)(2,1)S(1)}, u32[]{:S(2)}, u32[]{:S(2)}) %collective-permute-start.33) | collective-permute-done | bytes 196640 | tf_op jit(solution)/shard_map/ppermute | solution.py:51
  127.2 1.7 %backward.10 = (bf16[1,256,384]{2,1,0:T(8,128)(2,1)S(1)}, bf16[1,256,384]{2,1,0:T(8,128)(2,1)S(1)}) custom-call(s32[16]{0:T(128)S(1)} %get-tuple-element.116.places, s32[16,22]{1,0:T(8,128)S(1)} %select_convert_fusion.names, bf16[12,256,256]{2,1,0:T(8,128)(2,1)S(1)} %get-tuple-element.100.grads_ref, bf16[16,1424,256]{2,1,0:T(8,128)(2,1)S(1)} %get-tuple-element.101.w_ref, ...), custom_call_target="tpu_custom_call" | custom-call | flops 369098752 | bytes 1458176 | tf_op jit(solution)/shard_map/backward/pallas_call | solution.py:255
  129.0 2.1 %collective-permute-start.34 = (bf16[1,256,384]{2,1,0:T(8,128)(2,1)S(1)}, bf16[1,256,384]{2,1,0:T(8,128)(2,1)S(1)}, u32[]{:S(2)}, u32[]{:S(2)}) collective-permute-start(bf16[1,256,384]{2,1,0:T(8,128)(2,1)S(1)} %get-tuple-element.112), channel_id=1, source_target_pairs={{0,1},{1,2},{2,3},{3,4},{4,5},{5,6},{6,7},{7,0},{8,9},{9,10},{10,1... | collective-permute-start | bytes 589832 | tf_op jit(solution)/shard_map/ppermute | solution.py:51
  131.1 3.6 %collective-permute-done.34.refs_1_ = bf16[1,256,384]{2,1,0:T(8,128)(2,1)S(1)} collective-permute-done((bf16[1,256,384]{2,1,0:T(8,128)(2,1)S(1)}, bf16[1,256,384]{2,1,0:T(8,128)(2,1)S(1)}, u32[]{:S(2)}, u32[]{:S(2)}) %collective-permute-start.34) | collective-permute-done | bytes 196640 | tf_op jit(solution)/shard_map/ppermute | solution.py:51
  134.7 2.0 %collective-permute-done.35.refs_2_ = bf16[1,256,384]{2,1,0:T(8,128)(2,1)S(1)} collective-permute-done((bf16[1,256,384]{2,1,0:T(8,128)(2,1)S(1)}, bf16[1,256,384]{2,1,0:T(8,128)(2,1)S(1)}, u32[]{:S(2)}, u32[]{:S(2)}) %collective-permute-start.35) | collective-permute-done | bytes 196640 | tf_op jit(solution)/shard_map/ppermute | solution.py:51
  136.7 2.0 %backward.11 = bf16[1,256,384]{2,1,0:T(8,128)(2,1)} custom-call(s32[16]{0:T(128)S(1)} %get-tuple-element.116.places, s32[16,22]{1,0:T(8,128)S(1)} %select_convert_fusion.names, bf16[12,256,256]{2,1,0:T(8,128)(2,1)S(1)} %get-tuple-element.100.grads_ref, bf16[16,1424,256]{2,1,0:T(8,128)(2,1)S(1)} %get-tuple-element.101.w_ref, ...), custom_call_target="tpu_custom_call" | custom-call | flops 184549376 | bytes 729088 | tf_op jit(solution)/shard_map/backward/pallas_call | solution.py:255
  (56 shorter events, 0.8 us)
Async XLA Ops:
  3.4 10.7 %collective-permute-start = (bf16[1424,256]{1,0:T(8,128)(2,1)S(1)}, bf16[1424,256]{1,0:T(8,128)(2,1)S(1)}, u32[]{:S(2)}, u32[]{:S(2)}) collective-permute-start(bf16[1424,256]{1,0:T(8,128)(2,1)S(1)} %pad_maximum_fusion.refs_3_), channel_id=1, source_target_pairs={{0,16},{16,0},{1,17},{17,1},{2,18},{18,2},{3,19},{19,3},{4,20},{20... | collective-permute-start | bytes 2187272 | tf_op jit(solution)/shard_map/ppermute | solution.py:51
  3.5 12.7 %collective-permute-start.4 = (bf16[1424,256]{1,0:T(8,128)(2,1)S(1)}, bf16[1424,256]{1,0:T(8,128)(2,1)S(1)}, u32[]{:S(2)}, u32[]{:S(2)}) collective-permute-start(bf16[1424,256]{1,0:T(8,128)(2,1)S(1)} %pad_maximum_fusion.refs_3_), channel_id=1, source_target_pairs={{0,64},{16,208},{64,128},{80,16},{128,192},{144,80},{192,0},{208,1... | collective-permute-start | bytes 2187272 | tf_op jit(solution)/shard_map/ppermute | solution.py:59
  5.1 8.9 %collective-permute-start.5 = (bf16[256,384]{1,0:T(8,128)(2,1)}, bf16[256,384]{1,0:T(8,128)(2,1)S(1)}, u32[]{:S(2)}, u32[]{:S(2)}) collective-permute-start(bf16[256,384]{1,0:T(8,128)(2,1)} %param.7), channel_id=1, source_target_pairs={{0,8},{8,0},{1,9},{9,1},{2,10},{10,2},{3,11},{11,3},{4,12},{12,4},... | collective-permute-start | bytes 589832 | tf_op jit(solution)/shard_map/ppermute | solution.py:51
  16.1 19.3 %collective-permute-start.1 = (bf16[1424,256]{1,0:T(8,128)(2,1)S(1)}, bf16[1424,256]{1,0:T(8,128)(2,1)S(1)}, u32[]{:S(2)}, u32[]{:S(2)}) collective-permute-start(bf16[1424,256]{1,0:T(8,128)(2,1)S(1)} %pad_maximum_fusion.refs_3_), channel_id=1, source_target_pairs={{0,32},{32,0},{1,33},{33,1},{2,34},{34,2},{3,35},{35,3},{4,36},{36... | collective-permute-start | bytes 2187272 | tf_op jit(solution)/shard_map/ppermute | solution.py:51
  18.6 9.7 %collective-permute-start.7 = (bf16[2,256,384]{2,1,0:T(8,128)(2,1)S(1)}, bf16[2,256,384]{2,1,0:T(8,128)(2,1)S(1)}, u32[]{:S(2)}, u32[]{:S(2)}) collective-permute-start(bf16[2,256,384]{2,1,0:T(8,128)(2,1)S(1)} %pad_maximum_fusion.2.refs_0_), channel_id=1, source_target_pairs={{0,1},{1,2},{2,3},{3,4},{4,5},{5,6},{6,7},{7,0},{8,9},{9,10},{10,1... | collective-permute-start | bytes 1179656 | tf_op jit(solution)/shard_map/ppermute | solution.py:51
  20.6 18.6 %collective-permute-start.6 = (bf16[1424,256]{1,0:T(8,128)(2,1)S(1)}, bf16[1424,256]{1,0:T(8,128)(2,1)S(1)}, u32[]{:S(2)}, u32[]{:S(2)}) collective-permute-start(bf16[1424,256]{1,0:T(8,128)(2,1)S(1)} %collective-permute-done.4.refs_5_), channel_id=1, source_target_pairs={{0,64},{16,208},{64,128},{80,16},{128,192},{144,80},{192,0},{208,1... | collective-permute-start | bytes 2187272 | tf_op jit(solution)/shard_map/ppermute | solution.py:59
  21.0 18.3 %collective-permute-start.9 = (bf16[1424,256]{1,0:T(8,128)(2,1)S(1)}, bf16[1424,256]{1,0:T(8,128)(2,1)S(1)}, u32[]{:S(2)}, u32[]{:S(2)}) collective-permute-start(bf16[1424,256]{1,0:T(8,128)(2,1)S(1)} %collective-permute-done.4.refs_5_), channel_id=1, source_target_pairs={{0,16},{16,0},{1,17},{17,1},{2,18},{18,2},{3,19},{19,3},{4,20},{20... | collective-permute-start | bytes 2187272 | tf_op jit(solution)/shard_map/ppermute | solution.py:51
  22.1 26.8 %collective-permute-start.15 = (bf16[1424,256]{1,0:T(8,128)(2,1)S(1)}, bf16[1424,256]{1,0:T(8,128)(2,1)S(1)}, u32[]{:S(2)}, u32[]{:S(2)}) collective-permute-start(bf16[1424,256]{1,0:T(8,128)(2,1)S(1)} %collective-permute-done.4.refs_5_), channel_id=1, source_target_pairs={{0,32},{32,0},{1,33},{33,1},{2,34},{34,2},{3,35},{35,3},{4,36},{36... | collective-permute-start | bytes 2187272 | tf_op jit(solution)/shard_map/ppermute | solution.py:51
  28.3 10.9 %collective-permute-start.8 = (bf16[2,256,384]{2,1,0:T(8,128)(2,1)S(1)}, bf16[2,256,384]{2,1,0:T(8,128)(2,1)S(1)}, u32[]{:S(2)}, u32[]{:S(2)}) collective-permute-start(bf16[2,256,384]{2,1,0:T(8,128)(2,1)S(1)} %pad_maximum_fusion.2.refs_0_), channel_id=1, source_target_pairs={{0,7},{1,0},{2,1},{3,2},{4,3},{5,4},{6,5},{7,6},{8,15},{9,8},{10,9... | collective-permute-start | bytes 1179656 | tf_op jit(solution)/shard_map/ppermute | solution.py:51
  35.4 16.6 %collective-permute-start.2 = (bf16[1424,256]{1,0:T(8,128)(2,1)S(1)}, bf16[1424,256]{1,0:T(8,128)(2,1)S(1)}, u32[]{:S(2)}, u32[]{:S(2)}) collective-permute-start(bf16[1424,256]{1,0:T(8,128)(2,1)S(1)} %collective-permute-done.1.refs_7_), channel_id=1, source_target_pairs={{0,192},{16,80},{64,0},{80,144},{128,64},{144,208},{192,128},{208,... | collective-permute-start | bytes 2187272 | tf_op jit(solution)/shard_map/ppermute | solution.py:59
  39.2 9.6 %collective-permute-start.10 = (bf16[2,256,384]{2,1,0:T(8,128)(2,1)S(1)}, bf16[2,256,384]{2,1,0:T(8,128)(2,1)S(1)}, u32[]{:S(2)}, u32[]{:S(2)}) collective-permute-start(bf16[2,256,384]{2,1,0:T(8,128)(2,1)S(1)} %collective-permute-done.7.refs_1_), channel_id=1, source_target_pairs={{0,1},{1,2},{2,3},{3,4},{4,5},{5,6},{6,7},{7,0},{8,9},{9,10},{10,1... | collective-permute-start | bytes 1179656 | tf_op jit(solution)/shard_map/ppermute | solution.py:51
  39.8 9.7 %collective-permute-start.11 = (bf16[2,256,384]{2,1,0:T(8,128)(2,1)S(1)}, bf16[2,256,384]{2,1,0:T(8,128)(2,1)S(1)}, u32[]{:S(2)}, u32[]{:S(2)}) collective-permute-start(bf16[2,256,384]{2,1,0:T(8,128)(2,1)S(1)} %collective-permute-done.8.refs_2_), channel_id=1, source_target_pairs={{0,7},{1,0},{2,1},{3,2},{4,3},{5,4},{6,5},{7,6},{8,15},{9,8},{10,9... | collective-permute-start | bytes 1179656 | tf_op jit(solution)/shard_map/ppermute | solution.py:51
  41.8 14.3 %collective-permute-start.14 = (bf16[1424,256]{1,0:T(8,128)(2,1)S(1)}, bf16[1424,256]{1,0:T(8,128)(2,1)S(1)}, u32[]{:S(2)}, u32[]{:S(2)}) collective-permute-start(bf16[1424,256]{1,0:T(8,128)(2,1)S(1)} %collective-permute-done.6.refs_8_), channel_id=1, source_target_pairs={{0,64},{16,208},{64,128},{80,16},{128,192},{144,80},{192,0},{208,1... | collective-permute-start | bytes 2187272 | tf_op jit(solution)/shard_map/ppermute | solution.py:59
  49.5 14.1 %collective-permute-start.12 = (bf16[2,256,384]{2,1,0:T(8,128)(2,1)S(1)}, bf16[2,256,384]{2,1,0:T(8,128)(2,1)S(1)}, u32[]{:S(2)}, u32[]{:S(2)}) collective-permute-start(bf16[2,256,384]{2,1,0:T(8,128)(2,1)S(1)} %collective-permute-done.10.refs_0_), channel_id=1, source_target_pairs={{0,1},{1,2},{2,3},{3,4},{4,5},{5,6},{6,7},{7,0},{8,9},{9,10},{10,1... | collective-permute-start | bytes 1179656 | tf_op jit(solution)/shard_map/ppermute | solution.py:51
  51.4 13.1 %collective-permute-start.16 = (bf16[1424,256]{1,0:T(8,128)(2,1)S(1)}, bf16[1424,256]{1,0:T(8,128)(2,1)S(1)}, u32[]{:S(2)}, u32[]{:S(2)}) collective-permute-start(bf16[1424,256]{1,0:T(8,128)(2,1)S(1)} %collective-permute-done.1.refs_7_), channel_id=1, source_target_pairs={{0,16},{16,0},{1,17},{17,1},{2,18},{18,2},{3,19},{19,3},{4,20},{20... | collective-permute-start | bytes 2187272 | tf_op jit(solution)/shard_map/ppermute | solution.py:51
  51.4 13.1 %collective-permute-start.17 = (bf16[1424,256]{1,0:T(8,128)(2,1)S(1)}, bf16[1424,256]{1,0:T(8,128)(2,1)S(1)}, u32[]{:S(2)}, u32[]{:S(2)}) collective-permute-start(bf16[1424,256]{1,0:T(8,128)(2,1)S(1)} %collective-permute-done.6.refs_8_), channel_id=1, source_target_pairs={{0,16},{16,0},{1,17},{17,1},{2,18},{18,2},{3,19},{19,3},{4,20},{20... | collective-permute-start | bytes 2187272 | tf_op jit(solution)/shard_map/ppermute | solution.py:51
  51.9 12.6 %collective-permute-start.13 = (bf16[2,256,384]{2,1,0:T(8,128)(2,1)S(1)}, bf16[2,256,384]{2,1,0:T(8,128)(2,1)S(1)}, u32[]{:S(2)}, u32[]{:S(2)}) collective-permute-start(bf16[2,256,384]{2,1,0:T(8,128)(2,1)S(1)} %collective-permute-done.11.refs_1_), channel_id=1, source_target_pairs={{0,7},{1,0},{2,1},{3,2},{4,3},{5,4},{6,5},{7,6},{8,15},{9,8},{10,9... | collective-permute-start | bytes 1179656 | tf_op jit(solution)/shard_map/ppermute | solution.py:51
  56.1 21.2 %collective-permute-start.3 = (bf16[1424,256]{1,0:T(8,128)(2,1)S(1)}, bf16[1424,256]{1,0:T(8,128)(2,1)S(1)}, u32[]{:S(2)}, u32[]{:S(2)}) collective-permute-start(bf16[1424,256]{1,0:T(8,128)(2,1)S(1)} %collective-permute-done.2.refs_2_), channel_id=1, source_target_pairs={{0,192},{16,80},{64,0},{80,144},{128,64},{144,208},{192,128},{208,... | collective-permute-start | bytes 2187272 | tf_op jit(solution)/shard_map/ppermute | solution.py:59
  64.5 3.7 %collective-permute-start.20 = (bf16[1424,256]{1,0:T(8,128)(2,1)S(1)}, bf16[1424,256]{1,0:T(8,128)(2,1)S(1)}, u32[]{:S(2)}, u32[]{:S(2)}) collective-permute-start(bf16[1424,256]{1,0:T(8,128)(2,1)S(1)} %collective-permute-done.2.refs_2_), channel_id=1, source_target_pairs={{0,16},{16,0},{1,17},{17,1},{2,18},{18,2},{3,19},{19,3},{4,20},{20... | collective-permute-start | bytes 2187272 | tf_op jit(solution)/shard_map/ppermute | solution.py:51
  64.6 5.1 %collective-permute-start.19 = (bf16[1424,256]{1,0:T(8,128)(2,1)S(1)}, bf16[1424,256]{1,0:T(8,128)(2,1)S(1)}, u32[]{:S(2)}, u32[]{:S(2)}) collective-permute-start(bf16[1424,256]{1,0:T(8,128)(2,1)S(1)} %collective-permute-done.14.refs_3_), channel_id=1, source_target_pairs={{0,16},{16,0},{1,17},{17,1},{2,18},{18,2},{3,19},{19,3},{4,20},{20... | collective-permute-start | bytes 2187272 | tf_op jit(solution)/shard_map/ppermute | solution.py:51
  65.1 4.6 %collective-permute-start.18 = (bf16[1424,256]{1,0:T(8,128)(2,1)S(1)}, bf16[1424,256]{1,0:T(8,128)(2,1)S(1)}, u32[]{:S(2)}, u32[]{:S(2)}) collective-permute-start(bf16[1424,256]{1,0:T(8,128)(2,1)S(1)} %collective-permute-done.15.refs_4_), channel_id=1, source_target_pairs={{0,16},{16,0},{1,17},{17,1},{2,18},{18,2},{3,19},{19,3},{4,20},{20... | collective-permute-start | bytes 2187272 | tf_op jit(solution)/shard_map/ppermute | solution.py:51
  65.2 12.0 %collective-permute-start.21 = (bf16[256,384]{1,0:T(8,128)(2,1)S(1)}, bf16[256,384]{1,0:T(8,128)(2,1)S(1)}, u32[]{:S(2)}, u32[]{:S(2)}) collective-permute-start(bf16[256,384]{1,0:T(8,128)(2,1)S(1)} %slice_bitcast_fusion.1), channel_id=1, source_target_pairs={{0,1},{1,2},{2,3},{3,4},{4,5},{5,6},{6,7},{7,0},{8,9},{9,10},{10,1... | collective-permute-start | bytes 589832 | tf_op jit(solution)/shard_map/ppermute | solution.py:51
  68.3 9.0 %collective-permute-start.22 = (bf16[256,384]{1,0:T(8,128)(2,1)S(1)}, bf16[256,384]{1,0:T(8,128)(2,1)S(1)}, u32[]{:S(2)}, u32[]{:S(2)}) collective-permute-start(bf16[256,384]{1,0:T(8,128)(2,1)S(1)} %slice_bitcast_fusion), channel_id=1, source_target_pairs={{0,7},{1,0},{2,1},{3,2},{4,3},{5,4},{6,5},{7,6},{8,15},{9,8},{10,9... | collective-permute-start | bytes 589832 | tf_op jit(solution)/shard_map/ppermute | solution.py:51
  69.8 9.9 %copy-start = (bf16[256,1536]{1,0:T(8,128)(2,1)S(1)}, bf16[256,1536]{1,0:T(8,128)(2,1)}, u32[]{:S(2)}) copy-start(bf16[256,1536]{1,0:T(8,128)(2,1)} %up_ref.1) | copy-start | bytes 2359300
  77.3 2.3 %collective-permute-start.23 = (bf16[1424,256]{1,0:T(8,128)(2,1)S(1)}, bf16[1424,256]{1,0:T(8,128)(2,1)S(1)}, u32[]{:S(2)}, u32[]{:S(2)}) collective-permute-start(bf16[1424,256]{1,0:T(8,128)(2,1)S(1)} %collective-permute-done.3.refs_2_), channel_id=1, source_target_pairs={{0,16},{16,0},{1,17},{17,1},{2,18},{18,2},{3,19},{19,3},{4,20},{20... | collective-permute-start | bytes 2187272 | tf_op jit(solution)/shard_map/ppermute | solution.py:51
  87.7 9.3 %collective-permute-start.24 = (bf16[1,256,384]{2,1,0:T(8,128)(2,1)S(1)}, bf16[1,256,384]{2,1,0:T(8,128)(2,1)S(1)}, u32[]{:S(2)}, u32[]{:S(2)}) collective-permute-start(bf16[1,256,384]{2,1,0:T(8,128)(2,1)S(1)} %get-tuple-element.102), channel_id=1, source_target_pairs={{0,8},{8,0},{1,9},{9,1},{2,10},{10,2},{3,11},{11,3},{4,12},{12,4},... | collective-permute-start | bytes 589832 | tf_op jit(solution)/shard_map/ppermute | solution.py:51
  90.5 15.0 %collective-permute-start.26 = (bf16[2,256,384]{2,1,0:T(8,128)(2,1)S(1)}, bf16[2,256,384]{2,1,0:T(8,128)(2,1)S(1)}, u32[]{:S(2)}, u32[]{:S(2)}) collective-permute-start(bf16[2,256,384]{2,1,0:T(8,128)(2,1)S(1)} %get-tuple-element.104), channel_id=1, source_target_pairs={{0,8},{8,0},{1,9},{9,1},{2,10},{10,2},{3,11},{11,3},{4,12},{12,4},... | collective-permute-start | bytes 1179656 | tf_op jit(solution)/shard_map/ppermute | solution.py:51
  99.2 6.0 %collective-permute-start.27 = (bf16[1,256,384]{2,1,0:T(8,128)(2,1)S(1)}, bf16[1,256,384]{2,1,0:T(8,128)(2,1)S(1)}, u32[]{:S(2)}, u32[]{:S(2)}) collective-permute-start(bf16[1,256,384]{2,1,0:T(8,128)(2,1)S(1)} %get-tuple-element.105), channel_id=1, source_target_pairs={{0,1},{1,2},{2,3},{3,4},{4,5},{5,6},{6,7},{7,0},{8,9},{9,10},{10,1... | collective-permute-start | bytes 589832 | tf_op jit(solution)/shard_map/ppermute | solution.py:51
  100.7 14.3 %collective-permute-start.25 = (bf16[2,256,384]{2,1,0:T(8,128)(2,1)S(1)}, bf16[2,256,384]{2,1,0:T(8,128)(2,1)S(1)}, u32[]{:S(2)}, u32[]{:S(2)}) collective-permute-start(bf16[2,256,384]{2,1,0:T(8,128)(2,1)S(1)} %get-tuple-element.103), channel_id=1, source_target_pairs={{0,8},{8,0},{1,9},{9,1},{2,10},{10,2},{3,11},{11,3},{4,12},{12,4},... | collective-permute-start | bytes 1179656 | tf_op jit(solution)/shard_map/ppermute | solution.py:51
  108.0 6.0 %collective-permute-start.28 = (bf16[1,256,384]{2,1,0:T(8,128)(2,1)S(1)}, bf16[1,256,384]{2,1,0:T(8,128)(2,1)S(1)}, u32[]{:S(2)}, u32[]{:S(2)}) collective-permute-start(bf16[1,256,384]{2,1,0:T(8,128)(2,1)S(1)} %get-tuple-element.106), channel_id=1, source_target_pairs={{0,1},{1,2},{2,3},{3,4},{4,5},{5,6},{6,7},{7,0},{8,9},{9,10},{10,1... | collective-permute-start | bytes 589832 | tf_op jit(solution)/shard_map/ppermute | solution.py:51
  109.4 5.7 %collective-permute-start.29 = (bf16[1,256,384]{2,1,0:T(8,128)(2,1)S(1)}, bf16[1,256,384]{2,1,0:T(8,128)(2,1)S(1)}, u32[]{:S(2)}, u32[]{:S(2)}) collective-permute-start(bf16[1,256,384]{2,1,0:T(8,128)(2,1)S(1)} %get-tuple-element.107), channel_id=1, source_target_pairs={{0,7},{1,0},{2,1},{3,2},{4,3},{5,4},{6,5},{7,6},{8,15},{9,8},{10,9... | collective-permute-start | bytes 589832 | tf_op jit(solution)/shard_map/ppermute | solution.py:51
  110.5 16.7 %collective-permute-start.31 = (bf16[2,256,384]{2,1,0:T(8,128)(2,1)S(1)}, bf16[2,256,384]{2,1,0:T(8,128)(2,1)S(1)}, u32[]{:S(2)}, u32[]{:S(2)}) collective-permute-start(bf16[2,256,384]{2,1,0:T(8,128)(2,1)S(1)} %get-tuple-element.109), channel_id=1, source_target_pairs={{0,8},{8,0},{1,9},{9,1},{2,10},{10,2},{3,11},{11,3},{4,12},{12,4},... | collective-permute-start | bytes 1179656 | tf_op jit(solution)/shard_map/ppermute | solution.py:51
  117.3 6.3 %collective-permute-start.32 = (bf16[1,256,384]{2,1,0:T(8,128)(2,1)S(1)}, bf16[1,256,384]{2,1,0:T(8,128)(2,1)S(1)}, u32[]{:S(2)}, u32[]{:S(2)}) collective-permute-start(bf16[1,256,384]{2,1,0:T(8,128)(2,1)S(1)} %get-tuple-element.110), channel_id=1, source_target_pairs={{0,1},{1,2},{2,3},{3,4},{4,5},{5,6},{6,7},{7,0},{8,9},{9,10},{10,1... | collective-permute-start | bytes 589832 | tf_op jit(solution)/shard_map/ppermute | solution.py:51
  120.3 6.9 %collective-permute-start.33 = (bf16[1,256,384]{2,1,0:T(8,128)(2,1)S(1)}, bf16[1,256,384]{2,1,0:T(8,128)(2,1)S(1)}, u32[]{:S(2)}, u32[]{:S(2)}) collective-permute-start(bf16[1,256,384]{2,1,0:T(8,128)(2,1)S(1)} %get-tuple-element.111), channel_id=1, source_target_pairs={{0,7},{1,0},{2,1},{3,2},{4,3},{5,4},{6,5},{7,6},{8,15},{9,8},{10,9... | collective-permute-start | bytes 589832 | tf_op jit(solution)/shard_map/ppermute | solution.py:51
  120.3 10.7 %collective-permute-start.30 = (bf16[1,256,384]{2,1,0:T(8,128)(2,1)S(1)}, bf16[1,256,384]{2,1,0:T(8,128)(2,1)S(1)}, u32[]{:S(2)}, u32[]{:S(2)}) collective-permute-start(bf16[1,256,384]{2,1,0:T(8,128)(2,1)S(1)} %get-tuple-element.108), channel_id=1, source_target_pairs={{0,8},{8,0},{1,9},{9,1},{2,10},{10,2},{3,11},{11,3},{4,12},{12,4},... | collective-permute-start | bytes 589832 | tf_op jit(solution)/shard_map/ppermute | solution.py:51
  129.0 5.7 %collective-permute-start.34 = (bf16[1,256,384]{2,1,0:T(8,128)(2,1)S(1)}, bf16[1,256,384]{2,1,0:T(8,128)(2,1)S(1)}, u32[]{:S(2)}, u32[]{:S(2)}) collective-permute-start(bf16[1,256,384]{2,1,0:T(8,128)(2,1)S(1)} %get-tuple-element.112), channel_id=1, source_target_pairs={{0,1},{1,2},{2,3},{3,4},{4,5},{5,6},{6,7},{7,0},{8,9},{9,10},{10,1... | collective-permute-start | bytes 589832 | tf_op jit(solution)/shard_map/ppermute | solution.py:51
  131.1 5.7 %collective-permute-start.35 = (bf16[1,256,384]{2,1,0:T(8,128)(2,1)S(1)}, bf16[1,256,384]{2,1,0:T(8,128)(2,1)S(1)}, u32[]{:S(2)}, u32[]{:S(2)}) collective-permute-start(bf16[1,256,384]{2,1,0:T(8,128)(2,1)S(1)} %get-tuple-element.113), channel_id=1, source_target_pairs={{0,7},{1,0},{2,1},{3,2},{4,3},{5,4},{6,5},{7,6},{8,15},{9,8},{10,9... | collective-permute-start | bytes 589832 | tf_op jit(solution)/shard_map/ppermute | solution.py:51

commit v5 on v4

--- a/solution.py
+++ b/solution.py
@@ -248,7 +248,7 @@
         filled[k] += 1
 
 
-def backward(jobs, added, places, names, grads, w):
+def backward(jobs, added, places, names, grads, w, dtype):
     tokens = grads.shape[1]
     n_out = max(k for k, _, _ in jobs) + 1
     sizes = [sum(k == out for k, _, _ in jobs) for out in range(n_out)]
@@ -256,7 +256,7 @@
         functools.partial(backward_kernel, jobs),
         in_specs=[SCALARS] * 2 + [ON_CHIP] * (2 + len(added)),
         out_specs=[ON_CHIP] * n_out,
-        out_shape=[jax.ShapeDtypeStruct((size, tokens, 3 * SIDE), jnp.bfloat16) for size in sizes],
+        out_shape=[jax.ShapeDtypeStruct((size, tokens, 3 * SIDE), dtype) for size in sizes],
         scratch_shapes=[pltpu.VMEM((4, tokens, SIDE), jnp.float32)],
         compiler_params=pltpu.CompilerParams(vmem_limit_bytes=VMEM_LIMIT),
         cost_estimate=cost(len(jobs), names.shape[1] // 2, tokens, 2 * len(jobs) * w.size // w.shape[0], 0),
@@ -332,8 +332,8 @@
     names = names_of(known + w_late)
     hidden, grads, w = forward_late(pick, names, upstream, x_late, w_late, x, w, acc)
 
-    def share(jobs, added):
-        return backward(jobs, added, places, names, grads, w)
+    def share(jobs, added, dtype=bf16):
+        return backward(jobs, added, places, names, grads, w, dtype)
 
     x4, x3 = share([(0, 0, ()), (1, 1, ()), (1, 2, ())], [])
     x4, x3 = shift(x4, "x_hi", 1), shift(x3, "x_hi", 1)
@@ -348,7 +348,8 @@
     plus, minus = share(
         [(0, 13, ((0, 0), (1, 0))), (1, 14, ((0, 1), (2, 0)))], [x1, plus, minus])
     plus, minus = shift(plus, "z", 1), shift(minus, "z", -1)
-    grad_tokens, = share([(0, 15, ((0, 0), (1, 0), (2, 0)))], [x0, plus, minus])
+    own, = share([(0, 15, ((0, 0),))], [x0], jnp.float32)
+    grad_tokens = (own + plus.astype(jnp.float32) + minus.astype(jnp.float32)).astype(bf16)
     return hidden, grad_tokens[0]
 
 

time: 139 us -> 138 us (level)
  transfers between devices with their start and end apart: 36 -> 36, of which waited for: 19 -> 19; matrix products, arithmetic and copies ran while one was open for 1% -> 1% of each run, Pallas kernels for 17% -> 18%
where the time goes in v5:
time: 138 us; the launch traced here: 137 us
  starting transfers between devices  52.4 us (38%)
  waiting for transfers between devices  46.7 us (34%)
  Pallas kernels  32.4 us (23%)
  other arithmetic  4.11 us (3%)
    ppermute x31, starting transfers between devices, shift(): lax.ppermute(value, axis, [(i, (i + step) % size) for i in range(size)])  44.5 us
    ppermute x31, waiting for transfers between devices, shift(): lax.ppermute(value, axis, [(i, (i + step) % size) for i in range(size)])  41.2 us
    pallas_call x6, Pallas kernels, backward(): pl.pallas_call(functools.partial(backward_kernel, jobs), in_specs=[SCALAR...  12.1 us
    pallas_call x2, Pallas kernels, forward_early(): pl.pallas_call(functools.partial(early_kernel, stage, len(x_parts), len(w...  12.1 us
    ppermute x5, starting transfers between devices, turn(): return lax.ppermute(value, ('y', 'core'), pairs)  7.97 us
    pallas_call x1, Pallas kernels, forward_late(): pl.pallas_call(functools.partial(late_kernel, len(x_parts), len(w_parts))...  5.81 us
    ppermute x5, waiting for transfers between devices, turn(): return lax.ppermute(value, ('y', 'core'), pairs)  5.53 us
  transfers between devices with their start and end apart: 36, of which 19 were waited for; matrix products, arithmetic and copies ran while one was open for 1% of the time, Pallas kernels for 18%

profile of v5, /device:TPU:32, one launch (start us, length us, event | category | flops | bytes accessed | tf_op | source)
XLA Modules:
  0.0 137.5 jit_solution(3197789343887443300)
XLA Ops:
  0.6 0.7 dynamic-slice_bitcast_fusion
  1.3 1.2 pad_maximum_fusion.1
  2.5 0.7 fusion.10
  3.5 1.7 %collective-permute-start.4 = (bf16[1424,256]{1,0:T(8,128)(2,1)S(1)}, bf16[1424,256]{1,0:T(8,128)(2,1)S(1)}, u32[]{:S(2)}, u32[]{:S(2)}) collective-permute-start(bf16[1424,256]{1,0:T(8,128)(2,1)S(1)} %pad_maximum_fusion.refs_3_), channel_id=1, source_target_pairs={{0,64},{16,208},{64,128},{80,16},{128,192},{144,80},{192,0},{208,1... | collective-permute-start | bytes 2187272 | tf_op jit(solution)/shard_map/ppermute | solution.py:59
  5.1 3.0 %collective-permute-start.5 = (bf16[256,384]{1,0:T(8,128)(2,1)}, bf16[256,384]{1,0:T(8,128)(2,1)S(1)}, u32[]{:S(2)}, u32[]{:S(2)}) collective-permute-start(bf16[256,384]{1,0:T(8,128)(2,1)} %param.7), channel_id=1, source_target_pairs={{0,8},{8,0},{1,9},{9,1},{2,10},{10,2},{3,11},{11,3},{4,12},{12,4},... | collective-permute-start | bytes 589832 | tf_op jit(solution)/shard_map/ppermute | solution.py:51
  8.2 5.9 %collective-permute-done.5 = bf16[256,384]{1,0:T(8,128)(2,1)S(1)} collective-permute-done((bf16[256,384]{1,0:T(8,128)(2,1)}, bf16[256,384]{1,0:T(8,128)(2,1)S(1)}, u32[]{:S(2)}, u32[]{:S(2)}) %collective-permute-start.5) | collective-permute-done | bytes 196640 | tf_op jit(solution)/shard_map/ppermute | solution.py:51
  14.1 2.1 %collective-permute-done.4.refs_5_ = bf16[1424,256]{1,0:T(8,128)(2,1)S(1)} collective-permute-done((bf16[1424,256]{1,0:T(8,128)(2,1)S(1)}, bf16[1424,256]{1,0:T(8,128)(2,1)S(1)}, u32[]{:S(2)}, u32[]{:S(2)}) %collective-permute-start.4) | collective-permute-done | bytes 729120 | tf_op jit(solution)/shard_map/ppermute | solution.py:59
  16.1 1.5 %collective-permute-start.1 = (bf16[1424,256]{1,0:T(8,128)(2,1)S(1)}, bf16[1424,256]{1,0:T(8,128)(2,1)S(1)}, u32[]{:S(2)}, u32[]{:S(2)}) collective-permute-start(bf16[1424,256]{1,0:T(8,128)(2,1)S(1)} %pad_maximum_fusion.refs_3_), channel_id=1, source_target_pairs={{0,32},{32,0},{1,33},{33,1},{2,34},{34,2},{3,35},{35,3},{4,36},{36... | collective-permute-start | bytes 2187272 | tf_op jit(solution)/shard_map/ppermute | solution.py:51
  17.6 1.0 pad_maximum_fusion.2.refs_0_
  18.6 2.0 %collective-permute-start.7 = (bf16[2,256,384]{2,1,0:T(8,128)(2,1)S(1)}, bf16[2,256,384]{2,1,0:T(8,128)(2,1)S(1)}, u32[]{:S(2)}, u32[]{:S(2)}) collective-permute-start(bf16[2,256,384]{2,1,0:T(8,128)(2,1)S(1)} %pad_maximum_fusion.2.refs_0_), channel_id=1, source_target_pairs={{0,1},{1,2},{2,3},{3,4},{4,5},{5,6},{6,7},{7,0},{8,9},{9,10},{10,1... | collective-permute-start | bytes 1179656 | tf_op jit(solution)/shard_map/ppermute | solution.py:51
  20.6 0.4 collective-permute-start.6
  21.0 1.1 collective-permute-start.9
  22.1 0.6 collective-permute-start.15
  22.7 5.6 %collective-permute-done.7.refs_1_ = bf16[2,256,384]{2,1,0:T(8,128)(2,1)S(1)} collective-permute-done((bf16[2,256,384]{2,1,0:T(8,128)(2,1)S(1)}, bf16[2,256,384]{2,1,0:T(8,128)(2,1)S(1)}, u32[]{:S(2)}, u32[]{:S(2)}) %collective-permute-start.7) | collective-permute-done | bytes 393248 | tf_op jit(solution)/shard_map/ppermute | solution.py:51
  28.3 4.2 %collective-permute-start.8 = (bf16[2,256,384]{2,1,0:T(8,128)(2,1)S(1)}, bf16[2,256,384]{2,1,0:T(8,128)(2,1)S(1)}, u32[]{:S(2)}, u32[]{:S(2)}) collective-permute-start(bf16[2,256,384]{2,1,0:T(8,128)(2,1)S(1)} %pad_maximum_fusion.2.refs_0_), channel_id=1, source_target_pairs={{0,7},{1,0},{2,1},{3,2},{4,3},{5,4},{6,5},{7,6},{8,15},{9,8},{10,9... | collective-permute-start | bytes 1179656 | tf_op jit(solution)/shard_map/ppermute | solution.py:51
  32.6 2.8 %collective-permute-done.1.refs_7_ = bf16[1424,256]{1,0:T(8,128)(2,1)S(1)} collective-permute-done((bf16[1424,256]{1,0:T(8,128)(2,1)S(1)}, bf16[1424,256]{1,0:T(8,128)(2,1)S(1)}, u32[]{:S(2)}, u32[]{:S(2)}) %collective-permute-start.1) | collective-permute-done | bytes 729120 | tf_op jit(solution)/shard_map/ppermute | solution.py:51
  35.4 1.7 %collective-permute-start.2 = (bf16[1424,256]{1,0:T(8,128)(2,1)S(1)}, bf16[1424,256]{1,0:T(8,128)(2,1)S(1)}, u32[]{:S(2)}, u32[]{:S(2)}) collective-permute-start(bf16[1424,256]{1,0:T(8,128)(2,1)S(1)} %collective-permute-done.1.refs_7_), channel_id=1, source_target_pairs={{0,192},{16,80},{64,0},{80,144},{128,64},{144,208},{192,128},{208,... | collective-permute-start | bytes 2187272 | tf_op jit(solution)/shard_map/ppermute | solution.py:59
  37.0 2.2 %collective-permute-done.8.refs_2_ = bf16[2,256,384]{2,1,0:T(8,128)(2,1)S(1)} collective-permute-done((bf16[2,256,384]{2,1,0:T(8,128)(2,1)S(1)}, bf16[2,256,384]{2,1,0:T(8,128)(2,1)S(1)}, u32[]{:S(2)}, u32[]{:S(2)}) %collective-permute-start.8) | collective-permute-done | bytes 393248 | tf_op jit(solution)/shard_map/ppermute | solution.py:51
  39.2 0.5 collective-permute-start.10
  39.8 2.1 %collective-permute-start.11 = (bf16[2,256,384]{2,1,0:T(8,128)(2,1)S(1)}, bf16[2,256,384]{2,1,0:T(8,128)(2,1)S(1)}, u32[]{:S(2)}, u32[]{:S(2)}) collective-permute-start(bf16[2,256,384]{2,1,0:T(8,128)(2,1)S(1)} %collective-permute-done.8.refs_2_), channel_id=1, source_target_pairs={{0,7},{1,0},{2,1},{3,2},{4,3},{5,4},{6,5},{7,6},{8,15},{9,8},{10,9... | collective-permute-start | bytes 1179656 | tf_op jit(solution)/shard_map/ppermute | solution.py:51
  41.8 1.5 %collective-permute-start.14 = (bf16[1424,256]{1,0:T(8,128)(2,1)S(1)}, bf16[1424,256]{1,0:T(8,128)(2,1)S(1)}, u32[]{:S(2)}, u32[]{:S(2)}) collective-permute-start(bf16[1424,256]{1,0:T(8,128)(2,1)S(1)} %collective-permute-done.6.refs_8_), channel_id=1, source_target_pairs={{0,64},{16,208},{64,128},{80,16},{128,192},{144,80},{192,0},{208,1... | collective-permute-start | bytes 2187272 | tf_op jit(solution)/shard_map/ppermute | solution.py:59
  43.3 2.4 %store.1 = (bf16[16,256,384]{2,1,0:T(8,128)(2,1)S(1)}, bf16[16,1424,256]{2,1,0:T(8,128)(2,1)S(1)}) custom-call(bf16[2,256,384]{2,1,0:T(8,128)(2,1)S(1)} %pad_maximum_fusion.2.refs_0_, bf16[2,256,384]{2,1,0:T(8,128)(2,1)S(1)} %collective-permute-done.7.refs_1_, bf16[2,256,384]{2,1,0:T(8,128)(2,1)S(1)} %collective-permute-done.8.refs_2_, ...), custom_call_target="tpu_custom_call" | custom-call | bytes 13123584 | tf_op jit(solution)/shard_map/store/pallas_call | solution.py:89
  45.8 3.1 %collective-permute-done.15.refs_4_ = bf16[1424,256]{1,0:T(8,128)(2,1)S(1)} collective-permute-done((bf16[1424,256]{1,0:T(8,128)(2,1)S(1)}, bf16[1424,256]{1,0:T(8,128)(2,1)S(1)}, u32[]{:S(2)}, u32[]{:S(2)}) %collective-permute-start.15) | collective-permute-done | bytes 729120 | tf_op jit(solution)/shard_map/ppermute | solution.py:51
  48.9 0.6 collective-permute-done.11.refs_1_
  49.5 1.9 %collective-permute-start.12 = (bf16[2,256,384]{2,1,0:T(8,128)(2,1)S(1)}, bf16[2,256,384]{2,1,0:T(8,128)(2,1)S(1)}, u32[]{:S(2)}, u32[]{:S(2)}) collective-permute-start(bf16[2,256,384]{2,1,0:T(8,128)(2,1)S(1)} %collective-permute-done.10.refs_0_), channel_id=1, source_target_pairs={{0,1},{1,2},{2,3},{3,4},{4,5},{5,6},{6,7},{7,0},{8,9},{9,10},{10,1... | collective-permute-start | bytes 1179656 | tf_op jit(solution)/shard_map/ppermute | solution.py:51
  51.4 0.5 collective-permute-start.17
  51.9 0.7 collective-permute-start.13
  52.6 3.5 %collective-permute-done.14.refs_3_ = bf16[1424,256]{1,0:T(8,128)(2,1)S(1)} collective-permute-done((bf16[1424,256]{1,0:T(8,128)(2,1)S(1)}, bf16[1424,256]{1,0:T(8,128)(2,1)S(1)}, u32[]{:S(2)}, u32[]{:S(2)}) %collective-permute-start.14) | collective-permute-done | bytes 729120 | tf_op jit(solution)/shard_map/ppermute | solution.py:59
  56.1 2.8 %collective-permute-start.3 = (bf16[1424,256]{1,0:T(8,128)(2,1)S(1)}, bf16[1424,256]{1,0:T(8,128)(2,1)S(1)}, u32[]{:S(2)}, u32[]{:S(2)}) collective-permute-start(bf16[1424,256]{1,0:T(8,128)(2,1)S(1)} %collective-permute-done.2.refs_2_), channel_id=1, source_target_pairs={{0,192},{16,80},{64,0},{80,144},{128,64},{144,208},{192,128},{208,... | collective-permute-start | bytes 2187272 | tf_op jit(solution)/shard_map/ppermute | solution.py:59
  58.9 4.6 %forward_early.2 = (bf16[16,256,384]{2,1,0:T(8,128)(2,1)S(1)}, bf16[16,1424,256]{2,1,0:T(8,128)(2,1)S(1)}, f32[13,256,256]{2,1,0:T(8,128)S(1)}) custom-call(s32[16]{0:T(128)S(1)} %get-tuple-element.117.pick, s32[16,22]{1,0:T(8,128)S(1)} %fusion.1.names, ...), custom_call_target="tpu_custom_call", output_to_operand_aliasing={{0}: (7, {}), {1}: (8, {})} | custom-call | flops 1107296256 | bytes 6291456 | tf_op jit(solution)/shard_map/forward_early/pallas_call | solution.py:179
  63.6 0.9 collective-permute-done.13.refs_1_
  64.6 0.5 collective-permute-start.19
  65.2 3.0 %collective-permute-start.21 = (bf16[256,384]{1,0:T(8,128)(2,1)S(1)}, bf16[256,384]{1,0:T(8,128)(2,1)S(1)}, u32[]{:S(2)}, u32[]{:S(2)}) collective-permute-start(bf16[256,384]{1,0:T(8,128)(2,1)S(1)} %slice_bitcast_fusion.1), channel_id=1, source_target_pairs={{0,1},{1,2},{2,3},{3,4},{4,5},{5,6},{6,7},{7,0},{8,9},{9,10},{10,1... | collective-permute-start | bytes 589832 | tf_op jit(solution)/shard_map/ppermute | solution.py:51
  68.3 1.4 %collective-permute-start.22 = (bf16[256,384]{1,0:T(8,128)(2,1)S(1)}, bf16[256,384]{1,0:T(8,128)(2,1)S(1)}, u32[]{:S(2)}, u32[]{:S(2)}) collective-permute-start(bf16[256,384]{1,0:T(8,128)(2,1)S(1)} %slice_bitcast_fusion), channel_id=1, source_target_pairs={{0,7},{1,0},{2,1},{3,2},{4,3},{5,4},{6,5},{7,6},{8,15},{9,8},{10,9... | collective-permute-start | bytes 589832 | tf_op jit(solution)/shard_map/ppermute | solution.py:51
  69.7 0.1 fusion.2.names
  69.8 7.4 %forward_early.3 = (bf16[16,256,384]{2,1,0:T(8,128)(2,1)S(1)}, bf16[16,1424,256]{2,1,0:T(8,128)(2,1)S(1)}, f32[13,256,256]{2,1,0:T(8,128)S(1)}) custom-call(s32[16]{0:T(128)S(1)} %get-tuple-element.117.pick, s32[16,22]{1,0:T(8,128)S(1)} %fusion.2.names, ...), custom_call_target="tpu_custom_call", output_to_operand_aliasing={{0}: (9, {}), {1}: (10, {}), {2}: (11, {})} | custom-call | tf_op jit(solution)/shard_map/forward_early/pallas_call | solution.py:179
  77.4 2.2 %collective-permute-done.23.refs_3_ = bf16[1424,256]{1,0:T(8,128)(2,1)S(1)} collective-permute-done((bf16[1424,256]{1,0:T(8,128)(2,1)S(1)}, bf16[1424,256]{1,0:T(8,128)(2,1)S(1)}, u32[]{:S(2)}, u32[]{:S(2)}) %collective-permute-start.23) | collective-permute-done | bytes 729120 | tf_op jit(solution)/shard_map/ppermute | solution.py:51
  79.7 5.8 %forward_late.1 = (bf16[256,1536]{1,0:T(8,128)(2,1)}, bf16[12,256,256]{2,1,0:T(8,128)(2,1)S(1)}, bf16[16,256,384]{2,1,0:T(8,128)(2,1)S(1)}, bf16[16,1424,256]{2,1,0:T(8,128)(2,1)S(1)}, f32[13,256,256]{2,1,0:T(8,128)S(1)}) custom-call(s32[16]{0:T(128)S(1)} %get-tuple-element.117.pick, ...), custom_call_target="tpu_custom_call", output_to_operand_aliasing={{2}: (7, {}), {3}: (8, {}), {4}: (9, {})} | custom-call | flops 738197504 | bytes 3932160 | tf_op jit(solution)/shard_map/forward_late/pallas_call | solution.py:201
  85.5 2.2 %backward.6 = (bf16[1,256,384]{2,1,0:T(8,128)(2,1)S(1)}, bf16[2,256,384]{2,1,0:T(8,128)(2,1)S(1)}) custom-call(s32[16]{0:T(128)S(1)} %get-tuple-element.116.places, s32[16,22]{1,0:T(8,128)S(1)} %select_convert_fusion.names, bf16[12,256,256]{2,1,0:T(8,128)(2,1)S(1)} %get-tuple-element.100.grads_ref, bf16[16,1424,256]{2,1,0:T(8,128)(2,1)S(1)} %get-tuple-element.101.w_ref), custom_call_target="tpu_custom_call" | custom-call | flops 553648128 | bytes 2187264 | tf_op jit(solution)/shard_map/backward/pallas_call | solution.py:255
  87.7 2.8 %collective-permute-start.24 = (bf16[1,256,384]{2,1,0:T(8,128)(2,1)S(1)}, bf16[1,256,384]{2,1,0:T(8,128)(2,1)S(1)}, u32[]{:S(2)}, u32[]{:S(2)}) collective-permute-start(bf16[1,256,384]{2,1,0:T(8,128)(2,1)S(1)} %get-tuple-element.102), channel_id=1, source_target_pairs={{0,8},{8,0},{1,9},{9,1},{2,10},{10,2},{3,11},{11,3},{4,12},{12,4},... | collective-permute-start | bytes 589832 | tf_op jit(solution)/shard_map/ppermute | solution.py:51
  90.5 0.8 collective-permute-start.26
  91.3 5.7 %collective-permute-done.24.refs_0_ = bf16[1,256,384]{2,1,0:T(8,128)(2,1)S(1)} collective-permute-done((bf16[1,256,384]{2,1,0:T(8,128)(2,1)S(1)}, bf16[1,256,384]{2,1,0:T(8,128)(2,1)S(1)}, u32[]{:S(2)}, u32[]{:S(2)}) %collective-permute-start.24) | collective-permute-done | bytes 196640 | tf_op jit(solution)/shard_map/ppermute | solution.py:51
  97.0 2.1 %backward.7 = (bf16[1,256,384]{2,1,0:T(8,128)(2,1)S(1)}, bf16[2,256,384]{2,1,0:T(8,128)(2,1)S(1)}) custom-call(s32[16]{0:T(128)S(1)} %get-tuple-element.116.places, s32[16,22]{1,0:T(8,128)S(1)} %select_convert_fusion.names, bf16[12,256,256]{2,1,0:T(8,128)(2,1)S(1)} %get-tuple-element.100.grads_ref, bf16[16,1424,256]{2,1,0:T(8,128)(2,1)S(1)} %get-tuple-element.101.w_ref, ...), custom_call_target="tpu_custom_call" | custom-call | flops 553648128 | bytes 2187264 | tf_op jit(solution)/shard_map/backward/pallas_call | solution.py:255
  99.2 1.6 %collective-permute-start.27 = (bf16[1,256,384]{2,1,0:T(8,128)(2,1)S(1)}, bf16[1,256,384]{2,1,0:T(8,128)(2,1)S(1)}, u32[]{:S(2)}, u32[]{:S(2)}) collective-permute-start(bf16[1,256,384]{2,1,0:T(8,128)(2,1)S(1)} %get-tuple-element.105), channel_id=1, source_target_pairs={{0,1},{1,2},{2,3},{3,4},{4,5},{5,6},{6,7},{7,0},{8,9},{9,10},{10,1... | collective-permute-start | bytes 589832 | tf_op jit(solution)/shard_map/ppermute | solution.py:51
  100.7 2.7 %collective-permute-start.25 = (bf16[2,256,384]{2,1,0:T(8,128)(2,1)S(1)}, bf16[2,256,384]{2,1,0:T(8,128)(2,1)S(1)}, u32[]{:S(2)}, u32[]{:S(2)}) collective-permute-start(bf16[2,256,384]{2,1,0:T(8,128)(2,1)S(1)} %get-tuple-element.103), channel_id=1, source_target_pairs={{0,8},{8,0},{1,9},{9,1},{2,10},{10,2},{3,11},{11,3},{4,12},{12,4},... | collective-permute-start | bytes 1179656 | tf_op jit(solution)/shard_map/ppermute | solution.py:51
  103.4 1.7 %collective-permute-done.27.refs_1_ = bf16[1,256,384]{2,1,0:T(8,128)(2,1)S(1)} collective-permute-done((bf16[1,256,384]{2,1,0:T(8,128)(2,1)S(1)}, bf16[1,256,384]{2,1,0:T(8,128)(2,1)S(1)}, u32[]{:S(2)}, u32[]{:S(2)}) %collective-permute-start.27) | collective-permute-done | bytes 196640 | tf_op jit(solution)/shard_map/ppermute | solution.py:51
  105.1 0.3 collective-permute-done.26.refs_0_
  105.5 2.6 %backward.8 = (bf16[1,256,384]{2,1,0:T(8,128)(2,1)S(1)}, bf16[1,256,384]{2,1,0:T(8,128)(2,1)S(1)}, bf16[2,256,384]{2,1,0:T(8,128)(2,1)S(1)}) custom-call(s32[16]{0:T(128)S(1)} %get-tuple-element.116.places, s32[16,22]{1,0:T(8,128)S(1)} %select_convert_fusion.names, bf16[12,256,256]{2,1,0:T(8,128)(2,1)S(1)} %get-tuple-element.100.grads_ref, ...), custom_call_target="tpu_custom_call" | custom-call | flops 738197504 | bytes 2916352 | tf_op jit(solution)/shard_map/backward/pallas_call | solution.py:255
  108.1 1.3 collective-permute-start.28
  109.4 1.1 collective-permute-start.29
  110.5 2.8 %collective-permute-start.31 = (bf16[2,256,384]{2,1,0:T(8,128)(2,1)S(1)}, bf16[2,256,384]{2,1,0:T(8,128)(2,1)S(1)}, u32[]{:S(2)}, u32[]{:S(2)}) collective-permute-start(bf16[2,256,384]{2,1,0:T(8,128)(2,1)S(1)} %get-tuple-element.109), channel_id=1, source_target_pairs={{0,8},{8,0},{1,9},{9,1},{2,10},{10,2},{3,11},{11,3},{4,12},{12,4},... | collective-permute-start | bytes 1179656 | tf_op jit(solution)/shard_map/ppermute | solution.py:51
  113.3 0.7 collective-permute-done.28.refs_1_
  114.0 1.0 collective-permute-done.29.refs_2_
  115.0 2.2 %backward.9 = (bf16[1,256,384]{2,1,0:T(8,128)(2,1)S(1)}, bf16[1,256,384]{2,1,0:T(8,128)(2,1)S(1)}, bf16[1,256,384]{2,1,0:T(8,128)(2,1)S(1)}) custom-call(s32[16]{0:T(128)S(1)} %get-tuple-element.116.places, s32[16,22]{1,0:T(8,128)S(1)} %select_convert_fusion.names, bf16[12,256,256]{2,1,0:T(8,128)(2,1)S(1)} %get-tuple-element.100.grads_ref, ...), custom_call_target="tpu_custom_call" | custom-call | flops 553648128 | bytes 2187264 | tf_op jit(solution)/shard_map/backward/pallas_call | solution.py:255
  117.2 3.1 %collective-permute-start.32 = (bf16[1,256,384]{2,1,0:T(8,128)(2,1)S(1)}, bf16[1,256,384]{2,1,0:T(8,128)(2,1)S(1)}, u32[]{:S(2)}, u32[]{:S(2)}) collective-permute-start(bf16[1,256,384]{2,1,0:T(8,128)(2,1)S(1)} %get-tuple-element.110), channel_id=1, source_target_pairs={{0,1},{1,2},{2,3},{3,4},{4,5},{5,6},{6,7},{7,0},{8,9},{9,10},{10,1... | collective-permute-start | bytes 589832 | tf_op jit(solution)/shard_map/ppermute | solution.py:51
  120.3 2.8 %collective-permute-start.30 = (bf16[1,256,384]{2,1,0:T(8,128)(2,1)S(1)}, bf16[1,256,384]{2,1,0:T(8,128)(2,1)S(1)}, u32[]{:S(2)}, u32[]{:S(2)}) collective-permute-start(bf16[1,256,384]{2,1,0:T(8,128)(2,1)S(1)} %get-tuple-element.108), channel_id=1, source_target_pairs={{0,8},{8,0},{1,9},{9,1},{2,10},{10,2},{3,11},{11,3},{4,12},{12,4},... | collective-permute-start | bytes 589832 | tf_op jit(solution)/shard_map/ppermute | solution.py:51
  123.1 0.4 collective-permute-done.32.refs_1_
  123.5 3.7 %collective-permute-done.33.refs_2_ = bf16[1,256,384]{2,1,0:T(8,128)(2,1)S(1)} collective-permute-done((bf16[1,256,384]{2,1,0:T(8,128)(2,1)S(1)}, bf16[1,256,384]{2,1,0:T(8,128)(2,1)S(1)}, u32[]{:S(2)}, u32[]{:S(2)}) %collective-permute-start.33) | collective-permute-done | bytes 196640 | tf_op jit(solution)/shard_map/ppermute | solution.py:51
  127.2 1.7 %backward.11 = (bf16[1,256,384]{2,1,0:T(8,128)(2,1)S(1)}, bf16[1,256,384]{2,1,0:T(8,128)(2,1)S(1)}) custom-call(s32[16]{0:T(128)S(1)} %get-tuple-element.116.places, s32[16,22]{1,0:T(8,128)S(1)} %select_convert_fusion.names, bf16[12,256,256]{2,1,0:T(8,128)(2,1)S(1)} %get-tuple-element.100.grads_ref, bf16[16,1424,256]{2,1,0:T(8,128)(2,1)S(1)} %get-tuple-element.101.w_ref, ...), custom_call_target="tpu_custom_call" | custom-call | flops 369098752 | bytes 1458176 | tf_op jit(solution)/shard_map/backward/pallas_call | solution.py:255
  129.0 2.1 %collective-permute-start.34 = (bf16[1,256,384]{2,1,0:T(8,128)(2,1)S(1)}, bf16[1,256,384]{2,1,0:T(8,128)(2,1)S(1)}, u32[]{:S(2)}, u32[]{:S(2)}) collective-permute-start(bf16[1,256,384]{2,1,0:T(8,128)(2,1)S(1)} %get-tuple-element.112), channel_id=1, source_target_pairs={{0,1},{1,2},{2,3},{3,4},{4,5},{5,6},{6,7},{7,0},{8,9},{9,10},{10,1... | collective-permute-start | bytes 589832 | tf_op jit(solution)/shard_map/ppermute | solution.py:51
  131.1 1.3 backward.10
  132.3 2.4 %collective-permute-done.34 = bf16[1,256,384]{2,1,0:T(8,128)(2,1)S(1)} collective-permute-done((bf16[1,256,384]{2,1,0:T(8,128)(2,1)S(1)}, bf16[1,256,384]{2,1,0:T(8,128)(2,1)S(1)}, u32[]{:S(2)}, u32[]{:S(2)}) %collective-permute-start.34) | collective-permute-done | bytes 196640 | tf_op jit(solution)/shard_map/ppermute | solution.py:51
  134.7 2.0 %collective-permute-done.35 = bf16[1,256,384]{2,1,0:T(8,128)(2,1)S(1)} collective-permute-done((bf16[1,256,384]{2,1,0:T(8,128)(2,1)S(1)}, bf16[1,256,384]{2,1,0:T(8,128)(2,1)S(1)}, u32[]{:S(2)}, u32[]{:S(2)}) %collective-permute-start.35) | collective-permute-done | bytes 196640 | tf_op jit(solution)/shard_map/ppermute | solution.py:51
  136.7 0.8 fusion
  (57 shorter events, 0.9 us)
Async XLA Ops:
  3.4 10.7 %collective-permute-start = (bf16[1424,256]{1,0:T(8,128)(2,1)S(1)}, bf16[1424,256]{1,0:T(8,128)(2,1)S(1)}, u32[]{:S(2)}, u32[]{:S(2)}) collective-permute-start(bf16[1424,256]{1,0:T(8,128)(2,1)S(1)} %pad_maximum_fusion.refs_3_), channel_id=1, source_target_pairs={{0,16},{16,0},{1,17},{17,1},{2,18},{18,2},{3,19},{19,3},{4,20},{20... | collective-permute-start | bytes 2187272 | tf_op jit(solution)/shard_map/ppermute | solution.py:51
  3.5 12.7 %collective-permute-start.4 = (bf16[1424,256]{1,0:T(8,128)(2,1)S(1)}, bf16[1424,256]{1,0:T(8,128)(2,1)S(1)}, u32[]{:S(2)}, u32[]{:S(2)}) collective-permute-start(bf16[1424,256]{1,0:T(8,128)(2,1)S(1)} %pad_maximum_fusion.refs_3_), channel_id=1, source_target_pairs={{0,64},{16,208},{64,128},{80,16},{128,192},{144,80},{192,0},{208,1... | collective-permute-start | bytes 2187272 | tf_op jit(solution)/shard_map/ppermute | solution.py:59
  5.1 8.9 %collective-permute-start.5 = (bf16[256,384]{1,0:T(8,128)(2,1)}, bf16[256,384]{1,0:T(8,128)(2,1)S(1)}, u32[]{:S(2)}, u32[]{:S(2)}) collective-permute-start(bf16[256,384]{1,0:T(8,128)(2,1)} %param.7), channel_id=1, source_target_pairs={{0,8},{8,0},{1,9},{9,1},{2,10},{10,2},{3,11},{11,3},{4,12},{12,4},... | collective-permute-start | bytes 589832 | tf_op jit(solution)/shard_map/ppermute | solution.py:51
  16.1 19.3 %collective-permute-start.1 = (bf16[1424,256]{1,0:T(8,128)(2,1)S(1)}, bf16[1424,256]{1,0:T(8,128)(2,1)S(1)}, u32[]{:S(2)}, u32[]{:S(2)}) collective-permute-start(bf16[1424,256]{1,0:T(8,128)(2,1)S(1)} %pad_maximum_fusion.refs_3_), channel_id=1, source_target_pairs={{0,32},{32,0},{1,33},{33,1},{2,34},{34,2},{3,35},{35,3},{4,36},{36... | collective-permute-start | bytes 2187272 | tf_op jit(solution)/shard_map/ppermute | solution.py:51
  18.6 9.7 %collective-permute-start.7 = (bf16[2,256,384]{2,1,0:T(8,128)(2,1)S(1)}, bf16[2,256,384]{2,1,0:T(8,128)(2,1)S(1)}, u32[]{:S(2)}, u32[]{:S(2)}) collective-permute-start(bf16[2,256,384]{2,1,0:T(8,128)(2,1)S(1)} %pad_maximum_fusion.2.refs_0_), channel_id=1, source_target_pairs={{0,1},{1,2},{2,3},{3,4},{4,5},{5,6},{6,7},{7,0},{8,9},{9,10},{10,1... | collective-permute-start | bytes 1179656 | tf_op jit(solution)/shard_map/ppermute | solution.py:51
  20.6 18.6 %collective-permute-start.6 = (bf16[1424,256]{1,0:T(8,128)(2,1)S(1)}, bf16[1424,256]{1,0:T(8,128)(2,1)S(1)}, u32[]{:S(2)}, u32[]{:S(2)}) collective-permute-start(bf16[1424,256]{1,0:T(8,128)(2,1)S(1)} %collective-permute-done.4.refs_5_), channel_id=1, source_target_pairs={{0,64},{16,208},{64,128},{80,16},{128,192},{144,80},{192,0},{208,1... | collective-permute-start | bytes 2187272 | tf_op jit(solution)/shard_map/ppermute | solution.py:59
  21.0 18.3 %collective-permute-start.9 = (bf16[1424,256]{1,0:T(8,128)(2,1)S(1)}, bf16[1424,256]{1,0:T(8,128)(2,1)S(1)}, u32[]{:S(2)}, u32[]{:S(2)}) collective-permute-start(bf16[1424,256]{1,0:T(8,128)(2,1)S(1)} %collective-permute-done.4.refs_5_), channel_id=1, source_target_pairs={{0,16},{16,0},{1,17},{17,1},{2,18},{18,2},{3,19},{19,3},{4,20},{20... | collective-permute-start | bytes 2187272 | tf_op jit(solution)/shard_map/ppermute | solution.py:51
  22.1 26.8 %collective-permute-start.15 = (bf16[1424,256]{1,0:T(8,128)(2,1)S(1)}, bf16[1424,256]{1,0:T(8,128)(2,1)S(1)}, u32[]{:S(2)}, u32[]{:S(2)}) collective-permute-start(bf16[1424,256]{1,0:T(8,128)(2,1)S(1)} %collective-permute-done.4.refs_5_), channel_id=1, source_target_pairs={{0,32},{32,0},{1,33},{33,1},{2,34},{34,2},{3,35},{35,3},{4,36},{36... | collective-permute-start | bytes 2187272 | tf_op jit(solution)/shard_map/ppermute | solution.py:51
  28.3 10.9 %collective-permute-start.8 = (bf16[2,256,384]{2,1,0:T(8,128)(2,1)S(1)}, bf16[2,256,384]{2,1,0:T(8,128)(2,1)S(1)}, u32[]{:S(2)}, u32[]{:S(2)}) collective-permute-start(bf16[2,256,384]{2,1,0:T(8,128)(2,1)S(1)} %pad_maximum_fusion.2.refs_0_), channel_id=1, source_target_pairs={{0,7},{1,0},{2,1},{3,2},{4,3},{5,4},{6,5},{7,6},{8,15},{9,8},{10,9... | collective-permute-start | bytes 1179656 | tf_op jit(solution)/shard_map/ppermute | solution.py:51
  35.4 16.6 %collective-permute-start.2 = (bf16[1424,256]{1,0:T(8,128)(2,1)S(1)}, bf16[1424,256]{1,0:T(8,128)(2,1)S(1)}, u32[]{:S(2)}, u32[]{:S(2)}) collective-permute-start(bf16[1424,256]{1,0:T(8,128)(2,1)S(1)} %collective-permute-done.1.refs_7_), channel_id=1, source_target_pairs={{0,192},{16,80},{64,0},{80,144},{128,64},{144,208},{192,128},{208,... | collective-permute-start | bytes 2187272 | tf_op jit(solution)/shard_map/ppermute | solution.py:59
  39.2 9.6 %collective-permute-start.10 = (bf16[2,256,384]{2,1,0:T(8,128)(2,1)S(1)}, bf16[2,256,384]{2,1,0:T(8,128)(2,1)S(1)}, u32[]{:S(2)}, u32[]{:S(2)}) collective-permute-start(bf16[2,256,384]{2,1,0:T(8,128)(2,1)S(1)} %collective-permute-done.7.refs_1_), channel_id=1, source_target_pairs={{0,1},{1,2},{2,3},{3,4},{4,5},{5,6},{6,7},{7,0},{8,9},{9,10},{10,1... | collective-permute-start | bytes 1179656 | tf_op jit(solution)/shard_map/ppermute | solution.py:51
  39.8 9.7 %collective-permute-start.11 = (bf16[2,256,384]{2,1,0:T(8,128)(2,1)S(1)}, bf16[2,256,384]{2,1,0:T(8,128)(2,1)S(1)}, u32[]{:S(2)}, u32[]{:S(2)}) collective-permute-start(bf16[2,256,384]{2,1,0:T(8,128)(2,1)S(1)} %collective-permute-done.8.refs_2_), channel_id=1, source_target_pairs={{0,7},{1,0},{2,1},{3,2},{4,3},{5,4},{6,5},{7,6},{8,15},{9,8},{10,9... | collective-permute-start | bytes 1179656 | tf_op jit(solution)/shard_map/ppermute | solution.py:51
  41.8 14.3 %collective-permute-start.14 = (bf16[1424,256]{1,0:T(8,128)(2,1)S(1)}, bf16[1424,256]{1,0:T(8,128)(2,1)S(1)}, u32[]{:S(2)}, u32[]{:S(2)}) collective-permute-start(bf16[1424,256]{1,0:T(8,128)(2,1)S(1)} %collective-permute-done.6.refs_8_), channel_id=1, source_target_pairs={{0,64},{16,208},{64,128},{80,16},{128,192},{144,80},{192,0},{208,1... | collective-permute-start | bytes 2187272 | tf_op jit(solution)/shard_map/ppermute | solution.py:59
  49.5 14.1 %collective-permute-start.12 = (bf16[2,256,384]{2,1,0:T(8,128)(2,1)S(1)}, bf16[2,256,384]{2,1,0:T(8,128)(2,1)S(1)}, u32[]{:S(2)}, u32[]{:S(2)}) collective-permute-start(bf16[2,256,384]{2,1,0:T(8,128)(2,1)S(1)} %collective-permute-done.10.refs_0_), channel_id=1, source_target_pairs={{0,1},{1,2},{2,3},{3,4},{4,5},{5,6},{6,7},{7,0},{8,9},{9,10},{10,1... | collective-permute-start | bytes 1179656 | tf_op jit(solution)/shard_map/ppermute | solution.py:51
  51.4 13.1 %collective-permute-start.16 = (bf16[1424,256]{1,0:T(8,128)(2,1)S(1)}, bf16[1424,256]{1,0:T(8,128)(2,1)S(1)}, u32[]{:S(2)}, u32[]{:S(2)}) collective-permute-start(bf16[1424,256]{1,0:T(8,128)(2,1)S(1)} %collective-permute-done.1.refs_7_), channel_id=1, source_target_pairs={{0,16},{16,0},{1,17},{17,1},{2,18},{18,2},{3,19},{19,3},{4,20},{20... | collective-permute-start | bytes 2187272 | tf_op jit(solution)/shard_map/ppermute | solution.py:51
  51.4 13.1 %collective-permute-start.17 = (bf16[1424,256]{1,0:T(8,128)(2,1)S(1)}, bf16[1424,256]{1,0:T(8,128)(2,1)S(1)}, u32[]{:S(2)}, u32[]{:S(2)}) collective-permute-start(bf16[1424,256]{1,0:T(8,128)(2,1)S(1)} %collective-permute-done.6.refs_8_), channel_id=1, source_target_pairs={{0,16},{16,0},{1,17},{17,1},{2,18},{18,2},{3,19},{19,3},{4,20},{20... | collective-permute-start | bytes 2187272 | tf_op jit(solution)/shard_map/ppermute | solution.py:51
  51.9 12.6 %collective-permute-start.13 = (bf16[2,256,384]{2,1,0:T(8,128)(2,1)S(1)}, bf16[2,256,384]{2,1,0:T(8,128)(2,1)S(1)}, u32[]{:S(2)}, u32[]{:S(2)}) collective-permute-start(bf16[2,256,384]{2,1,0:T(8,128)(2,1)S(1)} %collective-permute-done.11.refs_1_), channel_id=1, source_target_pairs={{0,7},{1,0},{2,1},{3,2},{4,3},{5,4},{6,5},{7,6},{8,15},{9,8},{10,9... | collective-permute-start | bytes 1179656 | tf_op jit(solution)/shard_map/ppermute | solution.py:51
  56.1 21.2 %collective-permute-start.3 = (bf16[1424,256]{1,0:T(8,128)(2,1)S(1)}, bf16[1424,256]{1,0:T(8,128)(2,1)S(1)}, u32[]{:S(2)}, u32[]{:S(2)}) collective-permute-start(bf16[1424,256]{1,0:T(8,128)(2,1)S(1)} %collective-permute-done.2.refs_2_), channel_id=1, source_target_pairs={{0,192},{16,80},{64,0},{80,144},{128,64},{144,208},{192,128},{208,... | collective-permute-start | bytes 2187272 | tf_op jit(solution)/shard_map/ppermute | solution.py:59
  64.5 3.7 %collective-permute-start.20 = (bf16[1424,256]{1,0:T(8,128)(2,1)S(1)}, bf16[1424,256]{1,0:T(8,128)(2,1)S(1)}, u32[]{:S(2)}, u32[]{:S(2)}) collective-permute-start(bf16[1424,256]{1,0:T(8,128)(2,1)S(1)} %collective-permute-done.2.refs_2_), channel_id=1, source_target_pairs={{0,16},{16,0},{1,17},{17,1},{2,18},{18,2},{3,19},{19,3},{4,20},{20... | collective-permute-start | bytes 2187272 | tf_op jit(solution)/shard_map/ppermute | solution.py:51
  64.6 5.1 %collective-permute-start.19 = (bf16[1424,256]{1,0:T(8,128)(2,1)S(1)}, bf16[1424,256]{1,0:T(8,128)(2,1)S(1)}, u32[]{:S(2)}, u32[]{:S(2)}) collective-permute-start(bf16[1424,256]{1,0:T(8,128)(2,1)S(1)} %collective-permute-done.14.refs_3_), channel_id=1, source_target_pairs={{0,16},{16,0},{1,17},{17,1},{2,18},{18,2},{3,19},{19,3},{4,20},{20... | collective-permute-start | bytes 2187272 | tf_op jit(solution)/shard_map/ppermute | solution.py:51
  65.1 4.6 %collective-permute-start.18 = (bf16[1424,256]{1,0:T(8,128)(2,1)S(1)}, bf16[1424,256]{1,0:T(8,128)(2,1)S(1)}, u32[]{:S(2)}, u32[]{:S(2)}) collective-permute-start(bf16[1424,256]{1,0:T(8,128)(2,1)S(1)} %collective-permute-done.15.refs_4_), channel_id=1, source_target_pairs={{0,16},{16,0},{1,17},{17,1},{2,18},{18,2},{3,19},{19,3},{4,20},{20... | collective-permute-start | bytes 2187272 | tf_op jit(solution)/shard_map/ppermute | solution.py:51
  65.2 12.0 %collective-permute-start.21 = (bf16[256,384]{1,0:T(8,128)(2,1)S(1)}, bf16[256,384]{1,0:T(8,128)(2,1)S(1)}, u32[]{:S(2)}, u32[]{:S(2)}) collective-permute-start(bf16[256,384]{1,0:T(8,128)(2,1)S(1)} %slice_bitcast_fusion.1), channel_id=1, source_target_pairs={{0,1},{1,2},{2,3},{3,4},{4,5},{5,6},{6,7},{7,0},{8,9},{9,10},{10,1... | collective-permute-start | bytes 589832 | tf_op jit(solution)/shard_map/ppermute | solution.py:51
  68.3 9.0 %collective-permute-start.22 = (bf16[256,384]{1,0:T(8,128)(2,1)S(1)}, bf16[256,384]{1,0:T(8,128)(2,1)S(1)}, u32[]{:S(2)}, u32[]{:S(2)}) collective-permute-start(bf16[256,384]{1,0:T(8,128)(2,1)S(1)} %slice_bitcast_fusion), channel_id=1, source_target_pairs={{0,7},{1,0},{2,1},{3,2},{4,3},{5,4},{6,5},{7,6},{8,15},{9,8},{10,9... | collective-permute-start | bytes 589832 | tf_op jit(solution)/shard_map/ppermute | solution.py:51
  69.8 9.9 %copy-start = (bf16[256,1536]{1,0:T(8,128)(2,1)S(1)}, bf16[256,1536]{1,0:T(8,128)(2,1)}, u32[]{:S(2)}) copy-start(bf16[256,1536]{1,0:T(8,128)(2,1)} %up_ref.1) | copy-start | bytes 2359300
  77.3 2.3 %collective-permute-start.23 = (bf16[1424,256]{1,0:T(8,128)(2,1)S(1)}, bf16[1424,256]{1,0:T(8,128)(2,1)S(1)}, u32[]{:S(2)}, u32[]{:S(2)}) collective-permute-start(bf16[1424,256]{1,0:T(8,128)(2,1)S(1)} %collective-permute-done.3.refs_2_), channel_id=1, source_target_pairs={{0,16},{16,0},{1,17},{17,1},{2,18},{18,2},{3,19},{19,3},{4,20},{20... | collective-permute-start | bytes 2187272 | tf_op jit(solution)/shard_map/ppermute | solution.py:51
  87.7 9.3 %collective-permute-start.24 = (bf16[1,256,384]{2,1,0:T(8,128)(2,1)S(1)}, bf16[1,256,384]{2,1,0:T(8,128)(2,1)S(1)}, u32[]{:S(2)}, u32[]{:S(2)}) collective-permute-start(bf16[1,256,384]{2,1,0:T(8,128)(2,1)S(1)} %get-tuple-element.102), channel_id=1, source_target_pairs={{0,8},{8,0},{1,9},{9,1},{2,10},{10,2},{3,11},{11,3},{4,12},{12,4},... | collective-permute-start | bytes 589832 | tf_op jit(solution)/shard_map/ppermute | solution.py:51
  90.5 15.0 %collective-permute-start.26 = (bf16[2,256,384]{2,1,0:T(8,128)(2,1)S(1)}, bf16[2,256,384]{2,1,0:T(8,128)(2,1)S(1)}, u32[]{:S(2)}, u32[]{:S(2)}) collective-permute-start(bf16[2,256,384]{2,1,0:T(8,128)(2,1)S(1)} %get-tuple-element.104), channel_id=1, source_target_pairs={{0,8},{8,0},{1,9},{9,1},{2,10},{10,2},{3,11},{11,3},{4,12},{12,4},... | collective-permute-start | bytes 1179656 | tf_op jit(solution)/shard_map/ppermute | solution.py:51
  99.2 6.0 %collective-permute-start.27 = (bf16[1,256,384]{2,1,0:T(8,128)(2,1)S(1)}, bf16[1,256,384]{2,1,0:T(8,128)(2,1)S(1)}, u32[]{:S(2)}, u32[]{:S(2)}) collective-permute-start(bf16[1,256,384]{2,1,0:T(8,128)(2,1)S(1)} %get-tuple-element.105), channel_id=1, source_target_pairs={{0,1},{1,2},{2,3},{3,4},{4,5},{5,6},{6,7},{7,0},{8,9},{9,10},{10,1... | collective-permute-start | bytes 589832 | tf_op jit(solution)/shard_map/ppermute | solution.py:51
  100.7 14.3 %collective-permute-start.25 = (bf16[2,256,384]{2,1,0:T(8,128)(2,1)S(1)}, bf16[2,256,384]{2,1,0:T(8,128)(2,1)S(1)}, u32[]{:S(2)}, u32[]{:S(2)}) collective-permute-start(bf16[2,256,384]{2,1,0:T(8,128)(2,1)S(1)} %get-tuple-element.103), channel_id=1, source_target_pairs={{0,8},{8,0},{1,9},{9,1},{2,10},{10,2},{3,11},{11,3},{4,12},{12,4},... | collective-permute-start | bytes 1179656 | tf_op jit(solution)/shard_map/ppermute | solution.py:51
  108.1 6.0 %collective-permute-start.28 = (bf16[1,256,384]{2,1,0:T(8,128)(2,1)S(1)}, bf16[1,256,384]{2,1,0:T(8,128)(2,1)S(1)}, u32[]{:S(2)}, u32[]{:S(2)}) collective-permute-start(bf16[1,256,384]{2,1,0:T(8,128)(2,1)S(1)} %get-tuple-element.106), channel_id=1, source_target_pairs={{0,1},{1,2},{2,3},{3,4},{4,5},{5,6},{6,7},{7,0},{8,9},{9,10},{10,1... | collective-permute-start | bytes 589832 | tf_op jit(solution)/shard_map/ppermute | solution.py:51
  109.4 5.7 %collective-permute-start.29 = (bf16[1,256,384]{2,1,0:T(8,128)(2,1)S(1)}, bf16[1,256,384]{2,1,0:T(8,128)(2,1)S(1)}, u32[]{:S(2)}, u32[]{:S(2)}) collective-permute-start(bf16[1,256,384]{2,1,0:T(8,128)(2,1)S(1)} %get-tuple-element.107), channel_id=1, source_target_pairs={{0,7},{1,0},{2,1},{3,2},{4,3},{5,4},{6,5},{7,6},{8,15},{9,8},{10,9... | collective-permute-start | bytes 589832 | tf_op jit(solution)/shard_map/ppermute | solution.py:51
  110.5 16.7 %collective-permute-start.31 = (bf16[2,256,384]{2,1,0:T(8,128)(2,1)S(1)}, bf16[2,256,384]{2,1,0:T(8,128)(2,1)S(1)}, u32[]{:S(2)}, u32[]{:S(2)}) collective-permute-start(bf16[2,256,384]{2,1,0:T(8,128)(2,1)S(1)} %get-tuple-element.109), channel_id=1, source_target_pairs={{0,8},{8,0},{1,9},{9,1},{2,10},{10,2},{3,11},{11,3},{4,12},{12,4},... | collective-permute-start | bytes 1179656 | tf_op jit(solution)/shard_map/ppermute | solution.py:51
  117.2 6.3 %collective-permute-start.32 = (bf16[1,256,384]{2,1,0:T(8,128)(2,1)S(1)}, bf16[1,256,384]{2,1,0:T(8,128)(2,1)S(1)}, u32[]{:S(2)}, u32[]{:S(2)}) collective-permute-start(bf16[1,256,384]{2,1,0:T(8,128)(2,1)S(1)} %get-tuple-element.110), channel_id=1, source_target_pairs={{0,1},{1,2},{2,3},{3,4},{4,5},{5,6},{6,7},{7,0},{8,9},{9,10},{10,1... | collective-permute-start | bytes 589832 | tf_op jit(solution)/shard_map/ppermute | solution.py:51
  120.3 6.9 %collective-permute-start.33 = (bf16[1,256,384]{2,1,0:T(8,128)(2,1)S(1)}, bf16[1,256,384]{2,1,0:T(8,128)(2,1)S(1)}, u32[]{:S(2)}, u32[]{:S(2)}) collective-permute-start(bf16[1,256,384]{2,1,0:T(8,128)(2,1)S(1)} %get-tuple-element.111), channel_id=1, source_target_pairs={{0,7},{1,0},{2,1},{3,2},{4,3},{5,4},{6,5},{7,6},{8,15},{9,8},{10,9... | collective-permute-start | bytes 589832 | tf_op jit(solution)/shard_map/ppermute | solution.py:51
  120.3 10.7 %collective-permute-start.30 = (bf16[1,256,384]{2,1,0:T(8,128)(2,1)S(1)}, bf16[1,256,384]{2,1,0:T(8,128)(2,1)S(1)}, u32[]{:S(2)}, u32[]{:S(2)}) collective-permute-start(bf16[1,256,384]{2,1,0:T(8,128)(2,1)S(1)} %get-tuple-element.108), channel_id=1, source_target_pairs={{0,8},{8,0},{1,9},{9,1},{2,10},{10,2},{3,11},{11,3},{4,12},{12,4},... | collective-permute-start | bytes 589832 | tf_op jit(solution)/shard_map/ppermute | solution.py:51
  129.0 5.7 %collective-permute-start.34 = (bf16[1,256,384]{2,1,0:T(8,128)(2,1)S(1)}, bf16[1,256,384]{2,1,0:T(8,128)(2,1)S(1)}, u32[]{:S(2)}, u32[]{:S(2)}) collective-permute-start(bf16[1,256,384]{2,1,0:T(8,128)(2,1)S(1)} %get-tuple-element.112), channel_id=1, source_target_pairs={{0,1},{1,2},{2,3},{3,4},{4,5},{5,6},{6,7},{7,0},{8,9},{9,10},{10,1... | collective-permute-start | bytes 589832 | tf_op jit(solution)/shard_map/ppermute | solution.py:51
  131.0 5.7 %collective-permute-start.35 = (bf16[1,256,384]{2,1,0:T(8,128)(2,1)S(1)}, bf16[1,256,384]{2,1,0:T(8,128)(2,1)S(1)}, u32[]{:S(2)}, u32[]{:S(2)}) collective-permute-start(bf16[1,256,384]{2,1,0:T(8,128)(2,1)S(1)} %get-tuple-element.113), channel_id=1, source_target_pairs={{0,7},{1,0},{2,1},{3,2},{4,3},{5,4},{6,5},{7,6},{8,15},{9,8},{10,9... | collective-permute-start | bytes 589832 | tf_op jit(solution)/shard_map/ppermute | solution.py:51
